TPU v7x, 128 devices: a whole 4x4x4 slice. The times are simulated.
128 devices in a mesh: gx: 16 (over x, z), gy: 8 (over y, core).
Axes of the slice: x: 4, y: 4, z: 4, core: 2. Of those that a mesh axis runs over, the one named last changes fastest.
Arguments:
- basis: float32 [4, 40, 256, 1024], P(None, None, 'gx', 'gy'), may hold values from -6 to 6
- soil: int32 [40, 256, 1024], P(None, 'gx', 'gy'), may hold values from 0 to 7
- frozen: int32 [40, 256, 1024], P(None, 'gx', 'gy'), may hold values 0 or 1
- soil_table: float32 [4, 8], replicated, may hold values from 0.25 to 4
- coarse_basis: bfloat16 [16, 8, 32, 307200], P('gx', 'gy'), may hold values from -0.01171875 to 0.01171875
- coarse_inverse: float32 [4096, 4096], P(('gx', 'gy')), as said below
- active_count: int32 [16, 8], P('gx', 'gy'), may hold values from 8 to 32, as said below
Outputs:
- precond: float32 [40, 256, 1024], P(None, 'gx', 'gy')
- next_vector: float32 [40, 256, 1024], P(None, 'gx', 'gy')
- hessenberg: float32 [5], replicated
Inputs may be any that keep to these rules, and one draw needn't show every extreme that they name: coarse_inverse is symmetric: entry (i, j) equals entry (j, i). A subdomain uses its first active_count coarse vectors; both 32 and 8 occur in every draw.
All inputs are finite; a program needn't handle non-finite values. No bound on the sum of `frozen` on one device may be relied on, other than what follows from the above.
Results may differ from a plain program's by a relative error of at most 0.005.
Values may be sent and summed in bfloat16 or wider, within the bound.
No kernel may reach another device: no remote copies, remote signals or barrier semaphores. Data moves between devices by JAX's collectives and lax.ppermute only.
A program may use at most 128 MiB of HBM per device.

v0:
```python
import functools

import jax
import jax.numpy as jnp
from jax import lax
from jax.experimental import pallas as pl
from jax.experimental.pallas import tpu as pltpu
from jax.sharding import PartitionSpec as P

F32 = jnp.float32
BF16 = jnp.bfloat16

LAYERS, ROWS, COLS, OV, K = 40, 16, 128, 16, 32
CELLS = LAYERS * ROWS
RUNS = CELLS // 4
FLAT = 5 * RUNS
WINDOW = 7680
PART = 2560
WEIGHT_V, WEIGHT_H, EPS = 4.0, 1.0, 1e-06

VM = pl.BlockSpec(memory_space=pltpu.VMEM)
SM = pl.BlockSpec(memory_space=pltpu.SMEM)


def shape(*dims, dtype=F32):
    return jax.ShapeDtypeStruct(dims, dtype)


def call(kernel, outs, specs, args, scratch=(), out_specs=None, flops=0, moved=0, name=None):
    return pl.pallas_call(
        kernel,
        out_shape=outs,
        in_specs=specs,
        out_specs=out_specs if out_specs is not None else jax.tree.map(lambda _: VM, outs),
        scratch_shapes=list(scratch),
        compiler_params=pltpu.CompilerParams(vmem_limit_bytes=16 * 2**20),
        cost_estimate=pl.CostEstimate(flops=flops, bytes_accessed=moved, transcendentals=0),
        name=name,
    )(*args)


def lanes(rows):
    return lax.broadcasted_iota(jnp.int32, (rows, COLS), 1)


def harmonic(first, second):
    return 2.0 * first * second / (first + second)


def turn(values, amount):
    return pltpu.roll(values, amount % COLS, 1)


def pack_kernel(basis, soil, frozen, up, dn, flat, code):
    code[...] = (soil[...] + 8 * frozen[...]).astype(F32)
    at = lanes(RUNS)
    to_up = jnp.zeros((RUNS, COLS), F32)
    to_dn = to_up
    flats = [jnp.zeros((RUNS, COLS), F32) for _ in range(5)]
    for q in range(4):
        cut = 32 * q + 16
        turned = turn(basis[0, pl.ds(q, RUNS, stride=4), :], cut)
        kind = code[pl.ds(q, RUNS, stride=4), :]
        low = (at >= cut - 16) & (at < cut)
        high = (at >= cut) & (at < cut + 16)
        to_up = jnp.where(low, turned, jnp.where(at == cut, turn(kind, cut + 1), to_up))
        to_dn = jnp.where(high, turned, jnp.where(at == cut - 1, turn(kind, cut - 1), to_dn))
        flats[q] = jnp.where(at >= cut, turned, flats[q])
        flats[q + 1] = jnp.where(at < cut, turned, flats[q + 1])
    up[...] = to_up.astype(BF16)
    dn[...] = to_dn.astype(BF16)
    for j in range(5):
        flat[j * RUNS : (j + 1) * RUNS, :] = flats[j].astype(BF16)
    rows = [code[pl.ds(0, LAYERS, stride=ROWS), :], code[pl.ds(ROWS - 1, LAYERS, stride=ROWS), :]]
    flat[FLAT:, :] = jnp.concatenate(rows, axis=0).astype(BF16)


def flat_kernel(own, left, right, out):
    place = lax.axis_index("gy")
    last = lax.axis_size("gy") - 1
    at = lanes(RUNS)
    from_left = jnp.where(place > 0, left[...].astype(F32), 0.0)
    from_right = jnp.where(place < last, right[...].astype(F32), 0.0)
    for j in range(5):
        part = own[j * RUNS : (j + 1) * RUNS, :].astype(F32)
        if j < 4:
            part = jnp.where((at >= 32 * j) & (at < 32 * j + 16), from_left, part)
        if j > 0:
            part = jnp.where((at >= 32 * j - 16) & (at < 32 * j), from_right, part)
        out[j * RUNS : (j + 1) * RUNS, :] = part.astype(BF16)
    out[FLAT:, :] = own[FLAT:, :]


def project_part(coarse, vector, part, totals):
    def body(layer, totals):
        totals = list(totals)
        base = pl.multiple_of(layer * WINDOW + part * PART, 128)
        wide = jnp.concatenate(
            [
                jnp.broadcast_to(vector[pl.ds(j * RUNS + layer * 4 + m, 1), :], (8, COLS))
                for m in range(4)
                for j in range(5)
            ],
            axis=1,
        )
        for r in range(4):
            product = coarse[8 * r : 8 * r + 8, pl.ds(base, PART)].astype(F32) * wide
            for t in range(20):
                slot = 2 * r + t % 2
                totals[slot] = totals[slot] + product[:, t * COLS : (t + 1) * COLS]
        return tuple(totals)

    return lax.fori_loop(0, LAYERS, body, totals, unroll=4)


def own_rhs_kernel(coarse, own, out, vector):
    vector[...] = own[:FLAT, :].astype(F32)
    zero = jnp.zeros((8, COLS), F32)
    totals = project_part(coarse, vector, 1, (zero,) * 8)
    for r in range(4):
        out[8 * r : 8 * r + 8, :] = totals[2 * r] + totals[2 * r + 1]


def rhs_kernel(coarse, begun, before, after, count, out, vector):
    place = lax.axis_index("gx")
    last = lax.axis_size("gx") - 1
    zero = jnp.zeros((8, COLS), F32)
    totals = tuple(begun[4 * s : 4 * s + 8, :] if s % 2 == 0 else zero for s in range(8))
    vector[...] = jnp.where(place > 0, before[:FLAT, :].astype(F32), 0.0)
    totals = project_part(coarse, vector, 0, totals)
    vector[...] = jnp.where(place < last, after[:FLAT, :].astype(F32), 0.0)
    totals = project_part(coarse, vector, 2, totals)
    full = jnp.concatenate([totals[2 * r] + totals[2 * r + 1] for r in range(4)], axis=0)
    sums = jnp.sum(full, axis=1, keepdims=True)
    index = lax.broadcasted_iota(jnp.int32, (K, COLS), 0)
    keep = (lanes(K) % K == index) & (index < count[0, 0])
    row = jnp.sum(jnp.where(keep, sums, 0.0), axis=0, keepdims=True)
    out[...] = jnp.broadcast_to(row, out.shape)


def reduce_eight(parts, where):
    four, two, one = where

    def merge(a, b, mask, step):
        kept = jnp.where(mask, a, b)
        moved = jnp.where(mask, b, a)
        if step == 4:
            return kept + pltpu.roll(moved, 4, 0)
        return kept + jnp.where(mask, pltpu.roll(moved, 8 - step, 0), pltpu.roll(moved, step, 0))

    parts = [merge(parts[t], parts[t + 4], four, 4) for t in range(4)]
    parts = [merge(parts[t], parts[t + 2], two, 2) for t in range(2)]
    return merge(parts[0], parts[1], one, 1)


def spread_part(coarse, weights, part, out):
    row = lax.broadcasted_iota(jnp.int32, (8, COLS), 0)
    where = (row < 4, row % 4 < 2, row % 2 < 1)

    def body(pair, carry):
        halves = []
        for half in range(2):
            base = pl.multiple_of((2 * pair + half) * WINDOW + part * PART, 128)
            terms = [
                coarse[8 * r : 8 * r + 8, pl.ds(base, PART)].astype(F32) * weights[r]
                for r in range(4)
            ]
            halves.append((terms[0] + terms[1]) + (terms[2] + terms[3]))
        for j in range(5):
            tiles = [
                halves[half][:, (5 * m + j) * COLS : (5 * m + j + 1) * COLS]
                for half in range(2)
                for m in range(4)
            ]
            start = pl.multiple_of(j * RUNS + 8 * pair, 8)
            out[pl.ds(start, 8), :] = reduce_eight(tiles, where)
        return carry

    lax.fori_loop(0, LAYERS // 2, body, 0, unroll=2)


def spread_kernel(
    coarse, inverse, gathered, count, local, own, up, dn, up2, dn2, edge, rhs, low, high
):
    at = lanes(K)
    rows = jnp.zeros((K, COLS), F32)
    for e in range(4):
        rows = jnp.where(at // K == e, gathered[pl.ds(e, K, stride=4), :], rows)
    rhs[...] = rows
    total = jnp.zeros((K, COLS), F32)
    for i in range(K):
        total = total + inverse[:, i * COLS : (i + 1) * COLS] * rhs[i : i + 1, :]
    solved = jnp.sum(total, axis=1, keepdims=True)
    index = lax.broadcasted_iota(jnp.int32, (K, COLS), 0)
    solved = jnp.where(index < count[0, 0], solved, 0.0).astype(BF16).astype(F32)
    weights = [
        jnp.concatenate([solved[8 * r : 8 * r + 8, :]] * (PART // COLS), axis=1) for r in range(4)
    ]
    spread_part(coarse, weights, 0, low)
    spread_part(coarse, weights, 2, high)
    spread_part(coarse, weights, 1, own)
    at = lanes(LAYERS)

    def strip(ref, j, m):
        return ref[pl.ds(j * RUNS + m, LAYERS, stride=4), :]

    def both(first, second):
        return jnp.concatenate([first, second], axis=0)

    def put(ref, whole, ring):
        ref[:FLAT, :] = whole[...].astype(BF16)
        top = ring.astype(BF16)
        ref[FLAT : FLAT + 80, :] = top
        ref[FLAT + 80 :, :] = (ring - top.astype(F32)).astype(BF16)

    last = strip(local, 3, 3)
    put(
        up,
        high,
        both(
            strip(own, 3, 3) + jnp.where(at >= 112, last, 0.0),
            strip(own, 4, 3) + jnp.where(at < 112, last, 0.0),
        ),
    )
    first = strip(local, 0, 0)
    put(
        dn,
        low,
        both(
            strip(own, 0, 0) + jnp.where(at >= 16, first, 0.0),
            strip(own, 1, 0) + jnp.where(at < 16, first, 0.0),
        ),
    )
    up2[...] = both(strip(high, 3, 3), strip(high, 4, 3)).astype(BF16)
    dn2[...] = both(strip(low, 0, 0), strip(low, 1, 0)).astype(BF16)
    edge[:80, :] = both(strip(low, 3, 3), strip(low, 4, 3))
    edge[80:, :] = both(strip(high, 0, 0), strip(high, 1, 0))


def fold_rows_kernel(own, edge, local, before, after, before2, after2, field, rim, up, dn):
    place = lax.axis_index("gx")
    last = lax.axis_size("gx") - 1
    at = lanes(RUNS)
    whole = []
    for j in range(5):
        cut = slice(j * RUNS, (j + 1) * RUNS)
        part = (
            own[cut, :]
            + jnp.where(place > 0, before[cut, :].astype(F32), 0.0)
            + jnp.where(place < last, after[cut, :].astype(F32), 0.0)
        )
        if j < 4:
            part = part + jnp.where(at >= 32 * j + 16, local[cut, :], 0.0)
        if j > 0:
            behind = local[(j - 1) * RUNS : j * RUNS, :]
            part = part + jnp.where(at < 32 * j - 16, behind, 0.0)
        whole.append(part)
    to_up = jnp.zeros((RUNS, COLS), F32)
    to_dn = to_up
    for q in range(4):
        field[q * RUNS : (q + 1) * RUNS, :] = jnp.where(
            at >= 32 * q + 16, whole[q], whole[q + 1]
        )
        band = (at >= 32 * q) & (at < 32 * q + 32)
        to_up = jnp.where(band, whole[q + 1], to_up)
        to_dn = jnp.where(band, whole[q], to_dn)
    up[:RUNS, :] = to_up
    dn[:RUNS, :] = to_dn

    def ring(ours, near, far, valid):
        return (
            ours
            + near[FLAT : FLAT + 80, :].astype(F32)
            + near[FLAT + 80 :, :].astype(F32)
            + jnp.where(valid, far[...].astype(F32), 0.0)
        )

    top = ring(edge[:80, :], before, before2, place > 1)
    bottom = ring(edge[80:, :], after, after2, place < last - 1)
    at = lanes(LAYERS)
    half = LAYERS
    rim[:half, :] = jnp.where(at >= 112, top[:half], top[half:])
    rim[half:, :] = jnp.where(at >= 16, bottom[:half], bottom[half:])
    up[RUNS:, :] = jnp.where(at >= 96, top[half:], bottom[half:])
    dn[RUNS:, :] = jnp.where(at >= 96, top[:half], bottom[:half])


def look_up(kind, table, rows):
    value = jnp.zeros(kind.shape, F32)
    for index in range(8):
        value = jnp.where(kind == index, table[rows[0], index], value)
        value = jnp.where(kind == index + 8, table[rows[1], index], value)
    return value


def columns_kernel(basis, soil, frozen, table, conduct, diagonal, above, local, gram, ratio, value):
    kind = soil[...] + 8 * frozen[...]
    conduct[...] = look_up(kind, table, (0, 1))
    diagonal[...] = look_up(kind, table, (2, 3))
    zero = jnp.zeros((ROWS, COLS), F32)
    grams = [jnp.zeros((8, COLS), F32) for _ in range(10)]
    below = zero
    last_ratio = zero
    last_value = zero
    for level in range(LAYERS):
        cut = slice(level * ROWS, (level + 1) * ROWS)
        own = conduct[cut, :]
        over = zero
        if level < LAYERS - 1:
            over = WEIGHT_V * harmonic(own, conduct[(level + 1) * ROWS : (level + 2) * ROWS, :])
        above[cut, :] = over
        sides = diagonal[cut, :] + below + over
        diagonal[cut, :] = sides
        denom = sides + 4.0 * WEIGHT_H * own + below * last_ratio
        inverse = 1.0 / denom
        last_ratio = -over * inverse
        last_value = (basis[3, cut, :] + below * last_value) * inverse
        ratio[cut, :] = last_ratio
        value[cut, :] = last_value
        below = over
        vectors = [basis[j, cut, :] for j in range(4)]
        slot = 0
        for i in range(4):
            for j in range(i, 4):
                square = vectors[i] * vectors[j]
                grams[slot] = grams[slot] + (square[:8] + square[8:])
                slot += 1
    for level in range(LAYERS - 2, -1, -1):
        cut = slice(level * ROWS, (level + 1) * ROWS)
        last_value = value[cut, :] - ratio[cut, :] * last_value
        value[cut, :] = last_value
    for q in range(4):
        local[q * RUNS : (q + 1) * RUNS, :] = turn(value[pl.ds(q, RUNS, stride=4), :], 32 * q + 16)
    for slot in range(10):
        gram[8 * slot : 8 * slot + 8, :] = grams[slot]


def faces_kernel(conduct, diagonal, table, left, right, before, after, faces, total, side):
    gx, gy = lax.axis_index("gx"), lax.axis_index("gy")
    last_x, last_y = lax.axis_size("gx") - 1, lax.axis_size("gy") - 1
    at = lanes(RUNS)
    from_left, from_right = left[...].astype(F32), right[...].astype(F32)
    kinds = jnp.zeros((RUNS, COLS), F32)
    for q in range(4):
        kinds = jnp.where(at == 32 * q + 16, from_left, kinds)
        kinds = jnp.where(at == 32 * q + 15, from_right, kinds)
    known = look_up(kinds.astype(jnp.int32), table, (0, 1))
    for q in range(4):
        side[pl.ds(q, RUNS, stride=4), :] = turn(known, -(32 * q + 16))
    row_before = look_up(before[FLAT:, :].astype(F32).astype(jnp.int32), table, (0, 1))
    row_after = look_up(after[FLAT:, :].astype(F32).astype(jnp.int32), table, (0, 1))
    at = lanes(ROWS)
    row = lax.broadcasted_iota(jnp.int32, (ROWS, COLS), 0)
    for level in range(LAYERS):
        cut = slice(level * ROWS, (level + 1) * ROWS)
        own = conduct[cut, :]
        aside = side[cut, :]
        over = row_before[LAYERS + level : LAYERS + level + 1, :]
        under = row_after[level : level + 1, :]
        weights = [
            jnp.where((at > 0) | (gy > 0), harmonic(own, jnp.where(at == 0, aside, turn(own, 1))), 0.0),
            jnp.where(
                (at < COLS - 1) | (gy < last_y),
                harmonic(own, jnp.where(at == COLS - 1, aside, turn(own, -1))),
                0.0,
            ),
            jnp.where(
                (row > 0) | (gx > 0),
                harmonic(own, jnp.where(row == 0, over, pltpu.roll(own, 1, 0))),
                0.0,
            ),
            jnp.where(
                (row < ROWS - 1) | (gx < last_x),
                harmonic(own, jnp.where(row == ROWS - 1, under, pltpu.roll(own, ROWS - 1, 0))),
                0.0,
            ),
        ]
        for index in range(4):
            faces[index, cut, :] = WEIGHT_H * weights[index]
        total[cut, :] = diagonal[cut, :] + WEIGHT_H * (
            (weights[0] + weights[1]) + (weights[2] + weights[3])
        )


def image_kernel(
    field, rim, up, dn, left, right, basis, faces, total, above, gram, precond, image, sums, side
):
    gy = lax.axis_index("gy")
    last_y = lax.axis_size("gy") - 1
    at = lanes(RUNS)
    from_left = jnp.where(gy > 0, left[...], 0.0)
    from_right = jnp.where(gy < last_y, right[...], 0.0)
    to_left = dn[...] + from_left
    to_right = up[...] + from_right
    for q in range(4):
        cut = 32 * q + 16
        turned = field[q * RUNS : (q + 1) * RUNS, :]
        turned = turned + jnp.where((at >= cut) & (at < cut + 16), from_left[:RUNS], 0.0)
        turned = turned + jnp.where((at >= cut - 16) & (at < cut), from_right[:RUNS], 0.0)
        precond[pl.ds(q, RUNS, stride=4), :] = turn(turned, -cut)
        edges = jnp.where(at == cut - 1, to_left[:RUNS], to_right[:RUNS])
        side[pl.ds(q, RUNS, stride=4), :] = turn(edges, -cut)
    at = lanes(LAYERS)
    rim_left, rim_right = from_left[RUNS:], from_right[RUNS:]
    over = rim[:LAYERS, :]
    over = over + jnp.where(at >= 112, rim_left, 0.0)
    over = turn(over + jnp.where((at >= 96) & (at < 112), rim_right, 0.0), -112)
    under = rim[LAYERS:, :]
    under = under + jnp.where((at >= 16) & (at < 32), rim_left, 0.0)
    under = turn(under + jnp.where(at < 16, rim_right, 0.0), -16)
    at = lanes(ROWS)
    row = lax.broadcasted_iota(jnp.int32, (ROWS, COLS), 0)
    totals = [jnp.zeros((8, COLS), F32) for _ in range(5)]
    for level in range(LAYERS):
        cut = slice(level * ROWS, (level + 1) * ROWS)
        own = precond[cut, :]
        aside = side[cut, :]
        result = total[cut, :] * own
        result = result - faces[0, cut, :] * jnp.where(at == 0, turn(aside, 1), turn(own, 1))
        result = result - faces[1, cut, :] * jnp.where(
            at == COLS - 1, turn(aside, -1), turn(own, -1)
        )
        result = result - faces[2, cut, :] * jnp.where(
            row == 0, over[level : level + 1, :], pltpu.roll(own, 1, 0)
        )
        result = result - faces[3, cut, :] * jnp.where(
            row == ROWS - 1, under[level : level + 1, :], pltpu.roll(own, ROWS - 1, 0)
        )
        if level > 0:
            back = slice((level - 1) * ROWS, level * ROWS)
            result = result - above[back, :] * precond[back, :]
        if level < LAYERS - 1:
            ahead = slice((level + 1) * ROWS, (level + 2) * ROWS)
            result = result - above[cut, :] * precond[ahead, :]
        image[cut, :] = result
        for j in range(5):
            product = (basis[j, cut, :] if j < 4 else result) * result
            totals[j] = totals[j] + (product[:8] + product[8:])
    totals += [gram[8 * slot : 8 * slot + 8, :] for slot in range(10)]
    totals.append(jnp.zeros((8, COLS), F32))
    rows = jnp.concatenate([jnp.sum(part, axis=0, keepdims=True) for part in totals], axis=0)
    column = jnp.sum(rows, axis=1, keepdims=True)
    keep = lanes(ROWS) == lax.broadcasted_iota(jnp.int32, (ROWS, COLS), 0)
    line = jnp.sum(jnp.where(keep, column, 0.0), axis=0, keepdims=True)
    sums[...] = jnp.broadcast_to(line, sums.shape)


def next_kernel(gathered, image, basis, out, hessenberg):
    cells = float(CELLS * COLS * lax.axis_size("gx") * lax.axis_size("gy"))
    line = jnp.sum(gathered[...], axis=0, keepdims=True) / cells
    entry = [line[:, i : i + 1] for i in range(15)]
    project = entry[:4]
    square = entry[4]
    for j in range(4):
        square = square - 2.0 * project[j] * project[j]
    slot = 5
    for i in range(4):
        for j in range(i, 4):
            square = square + (1.0 if i == j else 2.0) * project[i] * project[j] * entry[slot]
            slot += 1
    length = jnp.sqrt(jnp.maximum(square, 0.0) + EPS)
    at = lanes(1)
    found = jnp.where(at == 4, length, jnp.where(at < 4, line, 0.0))
    for i in range(5):
        hessenberg[i] = found[0, i]
    inverse = 1.0 / length
    scaled = [project[j] * inverse for j in range(4)]
    for level in range(LAYERS):
        cut = slice(level * ROWS, (level + 1) * ROWS)
        value = image[cut, :] * inverse
        for j in range(4):
            value = value - scaled[j] * basis[j, cut, :]
        out[cut, :] = value


def shift(values, axis, step):
    count = lax.axis_size(axis)
    return lax.ppermute(values, axis, [(i, (i + step) % count) for i in range(count)])


def exchange(lines):
    size = lines.shape[0]
    out = lax.all_to_all(lines.reshape(size, 1, COLS), ("gx", "gy"), 0, 0)
    return out.reshape(size, COLS)


def on_device(basis, soil, frozen, soil_table, coarse_basis, coarse_inverse, active_count):
    basis = basis.reshape(4, CELLS, COLS)
    soil, frozen = soil.reshape(CELLS, COLS), frozen.reshape(CELLS, COLS)
    coarse = pltpu.with_memory_space_constraint(coarse_basis.reshape(K, -1), pltpu.VMEM)
    devices = lax.axis_size("gx") * lax.axis_size("gy")

    def pack(basis_ref, *refs):
        pack_kernel(basis_ref, *refs)

    one = pl.BlockSpec((1, CELLS, COLS), lambda i: (3, 0, 0))
    whole = pl.BlockSpec((CELLS, COLS), lambda i: (0, 0))
    up, dn, flat = pl.pallas_call(
        pack,
        grid=(1,),
        in_specs=[one, whole, whole],
        out_specs=[
            pl.BlockSpec((RUNS, COLS), lambda i: (0, 0)),
            pl.BlockSpec((RUNS, COLS), lambda i: (0, 0)),
            pl.BlockSpec((FLAT + 80, COLS), lambda i: (0, 0)),
        ],
        out_shape=[
            shape(RUNS, COLS, dtype=BF16),
            shape(RUNS, COLS, dtype=BF16),
            shape(FLAT + 80, COLS, dtype=BF16),
        ],
        scratch_shapes=[pltpu.VMEM((CELLS, COLS), F32)],
        compiler_params=pltpu.CompilerParams(vmem_limit_bytes=16 * 2**20),
        name="pack",
    )(basis, soil, frozen)
    left, right = shift(up, "gy", 1), shift(dn, "gy", -1)
    conduct, diagonal, above, local, gram = call(
        columns_kernel,
        [shape(CELLS, COLS)] * 4 + [shape(80, COLS)],
        [VM, VM, VM, SM],
        (basis, soil, frozen, soil_table),
        [pltpu.VMEM((CELLS, COLS), F32)] * 2,
        flops=10_000_000,
        moved=4_000_000,
        name="columns",
    )
    flat = call(
        flat_kernel, shape(FLAT + 80, COLS, dtype=BF16), [VM] * 3, (flat, left, right), name="flat"
    )
    before, after = shift(flat, "gx", 1), shift(flat, "gx", -1)
    begun = call(
        own_rhs_kernel,
        shape(K, COLS),
        [VM] * 2,
        (coarse, flat),
        [pltpu.VMEM((FLAT, COLS), F32)],
        flops=6_000_000,
        moved=6_000_000,
        name="own_rhs",
    )
    lines = call(
        rhs_kernel,
        shape(devices, COLS),
        [VM] * 4 + [SM],
        (coarse, begun, before, after, active_count),
        [pltpu.VMEM((FLAT, COLS), F32)],
        flops=12_000_000,
        moved=12_000_000,
        name="rhs",
    )
    gathered = exchange(lines)
    message = shape(FLAT + 160, COLS, dtype=BF16)
    small = shape(80, COLS, dtype=BF16)
    own, up, dn, up2, dn2, edge = call(
        spread_kernel,
        [shape(FLAT, COLS), message, message, small, small, shape(160, COLS)],
        [VM, VM, VM, SM, VM],
        (coarse, coarse_inverse, gathered, active_count, local),
        [pltpu.VMEM((K, COLS), F32)] + [pltpu.VMEM((FLAT, COLS), F32)] * 2,
        flops=40_000_000,
        moved=20_000_000,
        name="spread",
    )
    near = shift(up, "gx", 1), shift(dn, "gx", -1)
    far = shift(up2, "gx", 2), shift(dn2, "gx", -2)
    faces, total = call(
        faces_kernel,
        [shape(4, CELLS, COLS), shape(CELLS, COLS)],
        [VM, VM, SM, VM, VM, VM, VM],
        (conduct, diagonal, soil_table, left, right, before, after),
        [pltpu.VMEM((CELLS, COLS), F32)],
        flops=4_000_000,
        moved=2_000_000,
        name="faces",
    )
    field, rim, up, dn = call(
        fold_rows_kernel,
        [shape(CELLS, COLS), shape(80, COLS), shape(RUNS + LAYERS, COLS), shape(RUNS + LAYERS, COLS)],
        [VM] * 7,
        (own, edge, local, *near, *far),
        name="fold_rows",
    )
    left, right = shift(up, "gy", 1), shift(dn, "gy", -1)
    precond, image, sums = call(
        image_kernel,
        [shape(CELLS, COLS), shape(CELLS, COLS), shape(devices, COLS)],
        [VM] * 11,
        (field, rim, up, dn, left, right, basis, faces, total, above, gram),
        [pltpu.VMEM((CELLS, COLS), F32)],
        name="image",
    )
    gathered = exchange(sums)
    following, hessenberg = call(
        next_kernel,
        [shape(CELLS, COLS), shape(5)],
        [VM] * 3,
        (gathered, image, basis),
        out_specs=[VM, SM],
        name="next",
    )
    tile = (LAYERS, ROWS, COLS)
    return precond.reshape(tile), following.reshape(tile), hessenberg


def solution(mesh):
    placed = (
        P(None, None, "gx", "gy"),
        P(None, "gx", "gy"),
        P(None, "gx", "gy"),
        P(),
        P("gx", "gy", None, None),
        P(("gx", "gy"), None),
        P("gx", "gy"),
    )
    return jax.shard_map(
        on_device,
        mesh=mesh,
        in_specs=placed,
        out_specs=(P(None, "gx", "gy"), P(None, "gx", "gy"), P()),
        check_vma=False,
    )
```

profile of v0, /device:TPU:1, one launch (start us, length us, event | category | flops | bytes accessed | tf_op | source)
XLA Modules:
  0.0 103.5 jit_solution(1590767890025415227)
XLA Ops:
  0.6 0.0 copy-start.3
  0.6 1.3 %copy-done.3 = f32[4,40,16,128]{3,2,1,0:T(8,128)S(1)} copy-done((f32[4,40,16,128]{3,2,1,0:T(8,128)S(1)}, f32[4,40,16,128]{3,2,1,0:T(8,128)}, u32[]{:S(2)}) %copy-start.3) | copy-done | bytes 1310744
  2.0 1.0 copy-done.5
  2.9 1.0 copy-done.7
  3.9 0.3 pack.1
  4.2 2.7 %collective-permute-start = (bf16[160,128]{1,0:T(8,128)(2,1)S(1)}, bf16[160,128]{1,0:T(8,128)(2,1)S(1)}, u32[]{:S(2)}, u32[]{:S(2)}) collective-permute-start(bf16[160,128]{1,0:T(8,128)(2,1)S(1)} %get-tuple-element.29), channel_id=1, source_target_pairs={{0,1},{1,2},{2,3},{3,4},{4,5},{5,6},{6,7},{7,0},{8,9},{9,10},{10,1... | collective-permute-start | bytes 122888 | tf_op jit(solution)/shard_map/ppermute | solution.py:478
  6.9 0.0 collective-permute-start.1
  6.9 1.1 %collective-permute-done.left = bf16[160,128]{1,0:T(8,128)(2,1)S(1)} collective-permute-done((bf16[160,128]{1,0:T(8,128)(2,1)S(1)}, bf16[160,128]{1,0:T(8,128)(2,1)S(1)}, u32[]{:S(2)}, u32[]{:S(2)}) %collective-permute-start) | collective-permute-done | bytes 40992 | tf_op jit(solution)/shard_map/ppermute | solution.py:478
  8.0 2.3 %collective-permute-done.1.right = bf16[160,128]{1,0:T(8,128)(2,1)S(1)} collective-permute-done((bf16[160,128]{1,0:T(8,128)(2,1)S(1)}, bf16[160,128]{1,0:T(8,128)(2,1)S(1)}, u32[]{:S(2)}, u32[]{:S(2)}) %collective-permute-start.1) | collective-permute-done | bytes 40992 | tf_op jit(solution)/shard_map/ppermute | solution.py:478
  10.3 0.1 flat.1.own
  10.3 6.0 %collective-permute-start.3 = (bf16[880,128]{1,0:T(8,128)(2,1)S(1)}, bf16[880,128]{1,0:T(8,128)(2,1)S(1)}, u32[]{:S(2)}, u32[]{:S(2)}) collective-permute-start(bf16[880,128]{1,0:T(8,128)(2,1)S(1)} %flat.1.own), channel_id=1, source_target_pairs={{0,120},{8,0},{16,8},{24,16},{32,24},{40,32},{48,40},{56,48},{64,5... | collective-permute-start | bytes 675848 | tf_op jit(solution)/shard_map/ppermute | solution.py:478
  17.0 0.0 copy-start
  17.0 6.6 %copy-done = bf16[1,1,32,307200]{3,2,1,0:T(8,128)(2,1)S(1)} copy-done((bf16[1,1,32,307200]{3,2,1,0:T(8,128)(2,1)S(1)}, bf16[1,1,32,307200]{3,2,1,0:T(8,128)(2,1)}, u32[]{:S(2)}) %copy-start) | copy-done | bytes 19660824
  23.6 1.4 %own_rhs.1.begun = f32[32,128]{1,0:T(8,128)S(1)} custom-call(bf16[32,307200]{1,0:T(8,128)(2,1)S(1)} %bitcast.14, bf16[880,128]{1,0:T(8,128)(2,1)S(1)} %flat.1.own), custom_call_target="tpu_custom_call" | custom-call | flops 6000000 | bytes 6000000 | tf_op jit(solution)/shard_map/own_rhs/pallas_call | solution.py:30
  25.0 0.0 copy-start.4
  25.0 0.0 copy-start.6
  25.0 0.0 copy-start.8
  25.1 0.0 copy-start.16
  25.1 1.4 %collective-permute-done.2.before = bf16[880,128]{1,0:T(8,128)(2,1)S(1)} collective-permute-done((bf16[880,128]{1,0:T(8,128)(2,1)S(1)}, bf16[880,128]{1,0:T(8,128)(2,1)S(1)}, u32[]{:S(2)}, u32[]{:S(2)}) %collective-permute-start.2) | collective-permute-done | bytes 225312 | tf_op jit(solution)/shard_map/ppermute | solution.py:478
  26.5 3.7 %copy-done.1 = bf16[1,1,32,307200]{3,2,1,0:T(8,128)(2,1)S(1)} copy-done((bf16[1,1,32,307200]{3,2,1,0:T(8,128)(2,1)S(1)}, bf16[1,1,32,307200]{3,2,1,0:T(8,128)(2,1)}, u32[]{:S(2)}) %copy-start.1) | copy-done | bytes 19660824
  30.2 3.5 %rhs.1 = f32[128,128]{1,0:T(8,128)} custom-call(bf16[32,307200]{1,0:T(8,128)(2,1)S(1)} %bitcast.15, f32[32,128]{1,0:T(8,128)S(1)} %own_rhs.1.begun, bf16[880,128]{1,0:T(8,128)(2,1)S(1)} %collective-permute-done.2.before, bf16[880,128]{1,0:T(8,128)(2,1)S(1)} %collective-permute-done.3.after, s32[1,1]{1,0:T(1,128)S(6)} %copy.12.count), custom_call_target="tpu_custom_call" | custom-call | flops 12000000 | bytes 12000000 | tf_op jit(solution)/shard_map/rhs/pallas_call | solution.py:30
  33.7 8.4 %all-to-all-start = ((f32[128,1,128]{2,1,0:T(1,128)}), f32[128,1,128]{2,1,0:T(1,128)S(1)}, u32[]{:S(2)}, u32[]{:S(2)}) async-start(f32[128,1,128]{2,1,0:T(1,128)} %bitcast.5), calls=%async_computation | async-start | bytes 131072 | tf_op jit(solution)/shard_map/all_to_all | solution.py:483
  42.1 2.1 %columns.1 = (f32[640,128]{1,0:T(8,128)S(1)}, f32[640,128]{1,0:T(8,128)S(1)}, f32[640,128]{1,0:T(8,128)S(1)}, f32[640,128]{1,0:T(8,128)S(1)}, f32[80,128]{1,0:T(8,128)S(1)}) custom-call(f32[4,640,128]{2,1,0:T(8,128)S(1)} %bitcast.18, s32[640,128]{1,0:T(8,128)S(1)} %bitcast.22, s32[640,128]{1,0:T(8,128)S(1)} %bitcast.24, f32[4,8]{1,0:T(4,128)S(1)} %copy-done.16), custom_call_target="tpu_custom_call" | custom-call | flops 10000000 | bytes 4000000 | tf_op jit(solution)/shard_map/columns/pallas_call | solution.py:30
  44.2 0.0 copy-start.10
  44.3 0.7 copy-done.10
  45.0 0.7 copy-done.12
  45.7 0.7 copy-done.14
  46.4 5.2 %all-to-all-done = f32[128,1,128]{2,1,0:T(1,128)S(1)} async-done(((f32[128,1,128]{2,1,0:T(1,128)}), f32[128,1,128]{2,1,0:T(1,128)S(1)}, u32[]{:S(2)}, u32[]{:S(2)}) %all-to-all-start) | async-done | bytes 65568 | tf_op jit(solution)/shard_map/all_to_all | solution.py:483
  51.6 6.6 %copy-done.2 = bf16[1,1,32,307200]{3,2,1,0:T(8,128)(2,1)S(1)} copy-done((bf16[1,1,32,307200]{3,2,1,0:T(8,128)(2,1)S(1)}, bf16[1,1,32,307200]{3,2,1,0:T(8,128)(2,1)}, u32[]{:S(2)}) %copy-start.2) | copy-done | bytes 19660824
  58.2 5.3 %spread.1 = (f32[800,128]{1,0:T(8,128)S(1)}, bf16[960,128]{1,0:T(8,128)(2,1)S(1)}, bf16[960,128]{1,0:T(8,128)(2,1)S(1)}, bf16[80,128]{1,0:T(8,128)(2,1)S(1)}, bf...) custom-call(bf16[32,307200]{1,0:T(8,128)(2,1)S(1)} %bitcast.16, f32[32,4096]{1,0:T(8,128)S(1)} %copy-done.9, ...), custom_call_target="tpu_custom_call" | custom-call | flops 40000000 | bytes 20000000 | tf_op jit(solution)/shard_map/spread/pallas_call | solution.py:30
  63.5 0.0 copy-start.11
  63.5 0.0 copy-start.13
  63.5 0.4 collective-permute-start.4
  64.0 4.4 %collective-permute-start.5 = (bf16[960,128]{1,0:T(8,128)(2,1)S(1)}, bf16[960,128]{1,0:T(8,128)(2,1)S(1)}, u32[]{:S(2)}, u32[]{:S(2)}) collective-permute-start(bf16[960,128]{1,0:T(8,128)(2,1)S(1)} %get-tuple-element.35), channel_id=1, source_target_pairs={{0,120},{8,0},{16,8},{24,16},{32,24},{40,32},{48,40},{56,48},{64,5... | collective-permute-start | bytes 737288 | tf_op jit(solution)/shard_map/ppermute | solution.py:478
  68.4 0.0 collective-permute-start.6
  68.4 5.1 %collective-permute-start.7 = (bf16[80,128]{1,0:T(8,128)(2,1)S(1)}, bf16[80,128]{1,0:T(8,128)(2,1)S(1)}, u32[]{:S(2)}, u32[]{:S(2)}) collective-permute-start(bf16[80,128]{1,0:T(8,128)(2,1)S(1)} %get-tuple-element.37), channel_id=1, source_target_pairs={{0,112},{8,120},{16,0},{24,8},{32,16},{40,24},{48,32},{56,40},{64,... | collective-permute-start | bytes 61448 | tf_op jit(solution)/shard_map/ppermute | solution.py:478
  73.5 1.6 %collective-permute-done.6.before2 = bf16[80,128]{1,0:T(8,128)(2,1)S(1)} collective-permute-done((bf16[80,128]{1,0:T(8,128)(2,1)S(1)}, bf16[80,128]{1,0:T(8,128)(2,1)S(1)}, u32[]{:S(2)}, u32[]{:S(2)}) %collective-permute-start.6) | collective-permute-done | bytes 20512 | tf_op jit(solution)/shard_map/ppermute | solution.py:478
  75.1 0.0 collective-permute-done.4.before
  75.1 0.0 collective-permute-done.5.after
  75.1 0.2 fold_rows.1
  75.3 2.3 %collective-permute-start.8 = (f32[200,128]{1,0:T(8,128)S(1)}, f32[200,128]{1,0:T(8,128)S(1)}, u32[]{:S(2)}, u32[]{:S(2)}) collective-permute-start(f32[200,128]{1,0:T(8,128)S(1)} %get-tuple-element.40.up), channel_id=1, source_target_pairs={{0,1},{1,2},{2,3},{3,4},{4,5},{5,6},{6,7},{7,0},{8,9},{9,10},{10,1... | collective-permute-start | bytes 307208 | tf_op jit(solution)/shard_map/ppermute | solution.py:478
  77.6 0.0 collective-permute-start.9
  77.6 1.2 %faces.1 = (f32[4,640,128]{2,1,0:T(8,128)S(1)}, f32[640,128]{1,0:T(8,128)S(1)}) custom-call(f32[640,128]{1,0:T(8,128)S(1)} %copy-done.11, f32[640,128]{1,0:T(8,128)S(1)} %copy-done.13, f32[4,8]{1,0:T(4,128)S(1)} %copy-done.16, bf16[160,128]{1,0:T(8,128)(2,1)S(1)} %collective-permute-done.left, bf16[160,128]{1,0:T(8,128)(2,1)S(1)} %collective-permute-done.1.right, ...), custom_call_target="tpu_custom_call" | custom-call | flops 4000000 | bytes 2000000 | tf_op jit(solution)/shard_map/faces/pallas_call | solution.py:30
  78.8 0.5 collective-permute-done.8.left
  79.3 2.7 %collective-permute-done.9.right = f32[200,128]{1,0:T(8,128)S(1)} collective-permute-done((f32[200,128]{1,0:T(8,128)S(1)}, f32[200,128]{1,0:T(8,128)S(1)}, u32[]{:S(2)}, u32[]{:S(2)}) %collective-permute-start.9) | collective-permute-done | bytes 102432 | tf_op jit(solution)/shard_map/ppermute | solution.py:478
  82.0 1.4 %image.1 = (f32[640,128]{1,0:T(8,128)}, f32[640,128]{1,0:T(8,128)S(1)}, f32[128,128]{1,0:T(8,128)S(1)}) custom-call(f32[640,128]{1,0:T(8,128)S(1)} %get-tuple-element.38.field, f32[80,128]{1,0:T(8,128)S(1)} %get-tuple-element.39.rim, f32[200,128]{1,0:T(8,128)S(1)} %get-tuple-element.40.up, f32[200,128]{1,0:T(8,128)S(1)} %get-tuple-element.41.dn, ...), custom_call_target="tpu_custom_call" | custom-call | tf_op jit(solution)/shard_map/image/pallas_call | solution.py:30
  83.4 18.9 %all_to_all.10 = f32[128,1,128]{2,1,0:T(1,128)S(1)} all-to-all(f32[128,1,128]{2,1,0:T(1,128)S(1)} %bitcast.27), channel_id=1, replica_groups=mesh['gx'=16,'gy'=8] {'gx','gy'}, dimensions={0} | all-to-all | bytes 131072 | tf_op jit(solution)/shard_map/all_to_all | solution.py:483
  102.3 1.2 %next.1 = (f32[640,128]{1,0:T(8,128)}, f32[5]{0:T(128)}) custom-call(f32[128,128]{1,0:T(8,128)S(1)} %bitcast.26, f32[640,128]{1,0:T(8,128)S(1)} %get-tuple-element.50.image, f32[4,640,128]{2,1,0:T(8,128)S(1)} %bitcast.20), custom_call_target="tpu_custom_call" | custom-call | tf_op jit(solution)/shard_map/next/pallas_call | solution.py:30
  (19 shorter events, 0.0 us)
Async XLA Ops:
  0.6 1.3 %copy-start.3 = (f32[4,40,16,128]{3,2,1,0:T(8,128)S(1)}, f32[4,40,16,128]{3,2,1,0:T(8,128)}, u32[]{:S(2)}) copy-start(f32[4,40,16,128]{3,2,1,0:T(8,128)} %param.7) | copy-start | bytes 3932164
  1.9 1.0 copy-start.5
  2.9 1.0 copy-start.7
  4.2 3.8 %collective-permute-start = (bf16[160,128]{1,0:T(8,128)(2,1)S(1)}, bf16[160,128]{1,0:T(8,128)(2,1)S(1)}, u32[]{:S(2)}, u32[]{:S(2)}) collective-permute-start(bf16[160,128]{1,0:T(8,128)(2,1)S(1)} %get-tuple-element.29), channel_id=1, source_target_pairs={{0,1},{1,2},{2,3},{3,4},{4,5},{5,6},{6,7},{7,0},{8,9},{9,10},{10,1... | collective-permute-start | bytes 122888 | tf_op jit(solution)/shard_map/ppermute | solution.py:478
  6.9 3.4 %collective-permute-start.1 = (bf16[160,128]{1,0:T(8,128)(2,1)S(1)}, bf16[160,128]{1,0:T(8,128)(2,1)S(1)}, u32[]{:S(2)}, u32[]{:S(2)}) collective-permute-start(bf16[160,128]{1,0:T(8,128)(2,1)S(1)} %get-tuple-element.30), channel_id=1, source_target_pairs={{0,7},{1,0},{2,1},{3,2},{4,3},{5,4},{6,5},{7,6},{8,15},{9,8},{10,9... | collective-permute-start | bytes 122888 | tf_op jit(solution)/shard_map/ppermute | solution.py:478
  10.3 14.7 %collective-permute-start.3 = (bf16[880,128]{1,0:T(8,128)(2,1)S(1)}, bf16[880,128]{1,0:T(8,128)(2,1)S(1)}, u32[]{:S(2)}, u32[]{:S(2)}) collective-permute-start(bf16[880,128]{1,0:T(8,128)(2,1)S(1)} %flat.1.own), channel_id=1, source_target_pairs={{0,120},{8,0},{16,8},{24,16},{32,24},{40,32},{48,40},{56,48},{64,5... | collective-permute-start | bytes 675848 | tf_op jit(solution)/shard_map/ppermute | solution.py:478
  16.4 10.1 %collective-permute-start.2 = (bf16[880,128]{1,0:T(8,128)(2,1)S(1)}, bf16[880,128]{1,0:T(8,128)(2,1)S(1)}, u32[]{:S(2)}, u32[]{:S(2)}) collective-permute-start(bf16[880,128]{1,0:T(8,128)(2,1)S(1)} %flat.1.own), channel_id=1, source_target_pairs={{0,8},{8,16},{16,24},{24,32},{32,40},{40,48},{48,56},{56,64},{64,7... | collective-permute-start | bytes 675848 | tf_op jit(solution)/shard_map/ppermute | solution.py:478
  17.0 6.6 %copy-start = (bf16[1,1,32,307200]{3,2,1,0:T(8,128)(2,1)S(1)}, bf16[1,1,32,307200]{3,2,1,0:T(8,128)(2,1)}, u32[]{:S(2)}) copy-start(bf16[1,1,32,307200]{3,2,1,0:T(8,128)(2,1)} %param.11) | copy-start | bytes 58982404
  23.6 6.6 %copy-start.1 = (bf16[1,1,32,307200]{3,2,1,0:T(8,128)(2,1)S(1)}, bf16[1,1,32,307200]{3,2,1,0:T(8,128)(2,1)}, u32[]{:S(2)}) copy-start(bf16[1,1,32,307200]{3,2,1,0:T(8,128)(2,1)} %param.11) | copy-start | bytes 58982404
  25.0 17.1 %copy-start.4 = (f32[4,40,16,128]{3,2,1,0:T(8,128)S(1)}, f32[4,40,16,128]{3,2,1,0:T(8,128)}, u32[]{:S(2)}) copy-start(f32[4,40,16,128]{3,2,1,0:T(8,128)} %param.7) | copy-start | bytes 3932164
  25.0 17.1 %copy-start.6 = (s32[40,16,128]{2,1,0:T(8,128)S(1)}, s32[40,16,128]{2,1,0:T(8,128)}, u32[]{:S(2)}) copy-start(s32[40,16,128]{2,1,0:T(8,128)} %param.8) | copy-start | bytes 983044
  25.0 17.0 %copy-start.8 = (s32[40,16,128]{2,1,0:T(8,128)S(1)}, s32[40,16,128]{2,1,0:T(8,128)}, u32[]{:S(2)}) copy-start(s32[40,16,128]{2,1,0:T(8,128)} %param.9) | copy-start | bytes 983044
  25.1 17.0 %copy-start.16 = (f32[4,8]{1,0:T(4,128)S(1)}, f32[4,8]{1,0:T(4,128)}, u32[]{:S(2)}) copy-start(f32[4,8]{1,0:T(4,128)} %table.3) | copy-start | bytes 388
  33.7 17.9 %copy-start.9 = (f32[32,4096]{1,0:T(8,128)S(1)}, f32[32,4096]{1,0:T(8,128)}, u32[]{:S(2)}) copy-start(f32[32,4096]{1,0:T(8,128)} %inverse.1) | copy-start | bytes 1572868
  33.7 17.9 %all-to-all-start = ((f32[128,1,128]{2,1,0:T(1,128)}), f32[128,1,128]{2,1,0:T(1,128)S(1)}, u32[]{:S(2)}, u32[]{:S(2)}) async-start(f32[128,1,128]{2,1,0:T(1,128)} %bitcast.5), calls=%async_computation | async-start | bytes 131072 | tf_op jit(solution)/shard_map/all_to_all | solution.py:483
  44.2 0.7 copy-start.10
  45.0 0.7 copy-start.12
  45.7 0.7 copy-start.14
  51.6 6.6 %copy-start.2 = (bf16[1,1,32,307200]{3,2,1,0:T(8,128)(2,1)S(1)}, bf16[1,1,32,307200]{3,2,1,0:T(8,128)(2,1)}, u32[]{:S(2)}) copy-start(bf16[1,1,32,307200]{3,2,1,0:T(8,128)(2,1)} %param.11) | copy-start | bytes 58982404
  63.5 14.1 %copy-start.11 = (f32[640,128]{1,0:T(8,128)S(1)}, f32[640,128]{1,0:T(8,128)}, u32[]{:S(2)}) copy-start(f32[640,128]{1,0:T(8,128)} %copy-done.10) | copy-start | bytes 983044
  63.5 14.1 %copy-start.13 = (f32[640,128]{1,0:T(8,128)S(1)}, f32[640,128]{1,0:T(8,128)}, u32[]{:S(2)}) copy-start(f32[640,128]{1,0:T(8,128)} %copy-done.12) | copy-start | bytes 983044
  63.5 18.5 %copy-start.15 = (f32[640,128]{1,0:T(8,128)S(1)}, f32[640,128]{1,0:T(8,128)}, u32[]{:S(2)}) copy-start(f32[640,128]{1,0:T(8,128)} %copy-done.14) | copy-start | bytes 983044
  63.5 11.5 %collective-permute-start.4 = (bf16[960,128]{1,0:T(8,128)(2,1)S(1)}, bf16[960,128]{1,0:T(8,128)(2,1)S(1)}, u32[]{:S(2)}, u32[]{:S(2)}) collective-permute-start(bf16[960,128]{1,0:T(8,128)(2,1)S(1)} %get-tuple-element.34), channel_id=1, source_target_pairs={{0,8},{8,16},{16,24},{24,32},{32,40},{40,48},{48,56},{56,64},{64,7... | collective-permute-start | bytes 737288 | tf_op jit(solution)/shard_map/ppermute | solution.py:478
  64.0 11.1 %collective-permute-start.5 = (bf16[960,128]{1,0:T(8,128)(2,1)S(1)}, bf16[960,128]{1,0:T(8,128)(2,1)S(1)}, u32[]{:S(2)}, u32[]{:S(2)}) collective-permute-start(bf16[960,128]{1,0:T(8,128)(2,1)S(1)} %get-tuple-element.35), channel_id=1, source_target_pairs={{0,120},{8,0},{16,8},{24,16},{32,24},{40,32},{48,40},{56,48},{64,5... | collective-permute-start | bytes 737288 | tf_op jit(solution)/shard_map/ppermute | solution.py:478
  68.4 6.7 %collective-permute-start.6 = (bf16[80,128]{1,0:T(8,128)(2,1)S(1)}, bf16[80,128]{1,0:T(8,128)(2,1)S(1)}, u32[]{:S(2)}, u32[]{:S(2)}) collective-permute-start(bf16[80,128]{1,0:T(8,128)(2,1)S(1)} %get-tuple-element.36), channel_id=1, source_target_pairs={{0,16},{8,24},{16,32},{24,40},{32,48},{40,56},{48,64},{56,72},{64,... | collective-permute-start | bytes 61448 | tf_op jit(solution)/shard_map/ppermute | solution.py:478
  68.4 6.7 %collective-permute-start.7 = (bf16[80,128]{1,0:T(8,128)(2,1)S(1)}, bf16[80,128]{1,0:T(8,128)(2,1)S(1)}, u32[]{:S(2)}, u32[]{:S(2)}) collective-permute-start(bf16[80,128]{1,0:T(8,128)(2,1)S(1)} %get-tuple-element.37), channel_id=1, source_target_pairs={{0,112},{8,120},{16,0},{24,8},{32,16},{40,24},{48,32},{56,40},{64,... | collective-permute-start | bytes 61448 | tf_op jit(solution)/shard_map/ppermute | solution.py:478
  75.3 4.0 %collective-permute-start.8 = (f32[200,128]{1,0:T(8,128)S(1)}, f32[200,128]{1,0:T(8,128)S(1)}, u32[]{:S(2)}, u32[]{:S(2)}) collective-permute-start(f32[200,128]{1,0:T(8,128)S(1)} %get-tuple-element.40.up), channel_id=1, source_target_pairs={{0,1},{1,2},{2,3},{3,4},{4,5},{5,6},{6,7},{7,0},{8,9},{9,10},{10,1... | collective-permute-start | bytes 307208 | tf_op jit(solution)/shard_map/ppermute | solution.py:478
  77.6 4.4 %collective-permute-start.9 = (f32[200,128]{1,0:T(8,128)S(1)}, f32[200,128]{1,0:T(8,128)S(1)}, u32[]{:S(2)}, u32[]{:S(2)}) collective-permute-start(f32[200,128]{1,0:T(8,128)S(1)} %get-tuple-element.41.dn), channel_id=1, source_target_pairs={{0,7},{1,0},{2,1},{3,2},{4,3},{5,4},{6,5},{7,6},{8,15},{9,8},{10,9... | collective-permute-start | bytes 307208 | tf_op jit(solution)/shard_map/ppermute | solution.py:478
where the time goes:
time: 104 us; the launch traced here: 103 us
  starting transfers between devices  29.4 us (28%)
  local copies, waits for them, and re-layouts  22.4 us (22%)
  blocking collectives  18.9 us (18%)
  Pallas kernels  16.6 us (16%)
  waiting for transfers between devices  14.8 us (14%)
  between operations  1.48 us (1%)
    unnamed x34, local copies, waits for them, and re-layouts  22.4 us
    ppermute x10, starting transfers between devices, shift(): lax.ppermute(values, axis, [(i, (i + step) % count) for i in range(count)])  21 us
    all_to_all x1, blocking collectives, exchange(): out = lax.all_to_all(lines.reshape(size, 1, COLS), ('gx', 'gy'), 0, 0)  18.9 us
    pallas_call x9, Pallas kernels, call(): pl.pallas_call(kernel, out_shape=outs, in_specs=specs, out_specs=out_spec...  16.3 us
    ppermute x10, waiting for transfers between devices, shift(): lax.ppermute(values, axis, [(i, (i + step) % count) for i in range(count)])  9.64 us
    all_to_all x1, starting transfers between devices, exchange(): out = lax.all_to_all(lines.reshape(size, 1, COLS), ('gx', 'gy'), 0, 0)  8.38 us
    all_to_all x1, waiting for transfers between devices, exchange(): out = lax.all_to_all(lines.reshape(size, 1, COLS), ('gx', 'gy'), 0, 0)  5.15 us
  transfers between devices with their start and end apart: 11, of which 7 were waited for; matrix products, arithmetic and copies ran while one was open for 0% of the time, Pallas kernels for 5%

commit v1 on v0

--- a/solution.py
+++ b/solution.py
@@ -15,11 +15,14 @@
 RUNS = CELLS // 4
 FLAT = 5 * RUNS
 WINDOW = 7680
+EARLY = 10
+CHUNK = 10
 PART = 2560
 WEIGHT_V, WEIGHT_H, EPS = 4.0, 1.0, 1e-06
 
 VM = pl.BlockSpec(memory_space=pltpu.VMEM)
 SM = pl.BlockSpec(memory_space=pltpu.SMEM)
+HB = pl.BlockSpec(memory_space=pltpu.HBM)
 
 
 def shape(*dims, dtype=F32):
@@ -51,7 +54,16 @@
     return pltpu.roll(values, amount % COLS, 1)
 
 
-def pack_kernel(basis, soil, frozen, up, dn, flat, code):
+def pack_kernel(basis_in, soil_in, frozen_in, up, dn, flat, basis, soil, frozen, code, arrived):
+    copies = [
+        pltpu.make_async_copy(basis_in.at[3], basis, arrived.at[0]),
+        pltpu.make_async_copy(soil_in, soil, arrived.at[1]),
+        pltpu.make_async_copy(frozen_in, frozen, arrived.at[2]),
+    ]
+    for copy in copies:
+        copy.start()
+    for copy in copies:
+        copy.wait()
     code[...] = (soil[...] + 8 * frozen[...]).astype(F32)
     at = lanes(RUNS)
     to_up = jnp.zeros((RUNS, COLS), F32)
@@ -59,7 +71,7 @@
     flats = [jnp.zeros((RUNS, COLS), F32) for _ in range(5)]
     for q in range(4):
         cut = 32 * q + 16
-        turned = turn(basis[0, pl.ds(q, RUNS, stride=4), :], cut)
+        turned = turn(basis[pl.ds(q, RUNS, stride=4), :], cut)
         kind = code[pl.ds(q, RUNS, stride=4), :]
         low = (at >= cut - 16) & (at < cut)
         high = (at >= cut) & (at < cut + 16)
@@ -91,13 +103,14 @@
     out[FLAT:, :] = own[FLAT:, :]
 
 
-def project_part(coarse, vector, part, totals):
+def project_part(coarse, vector, part, totals, first, begin, count):
     def body(layer, totals):
         totals = list(totals)
-        base = pl.multiple_of(layer * WINDOW + part * PART, 128)
+        base = pl.multiple_of((begin + layer) * WINDOW + part * PART, 128)
+        row = (first + begin + layer) * 4
         wide = jnp.concatenate(
             [
-                jnp.broadcast_to(vector[pl.ds(j * RUNS + layer * 4 + m, 1), :], (8, COLS))
+                jnp.broadcast_to(vector[pl.ds(j * RUNS + row + m, 1), :], (8, COLS))
                 for m in range(4)
                 for j in range(5)
             ],
@@ -110,26 +123,71 @@
                 totals[slot] = totals[slot] + product[:, t * COLS : (t + 1) * COLS]
         return tuple(totals)
 
-    return lax.fori_loop(0, LAYERS, body, totals, unroll=4)
-
-
-def own_rhs_kernel(coarse, own, out, vector):
+    return lax.fori_loop(0, count, body, totals, unroll=5)
+
+
+def early_kernel(source, out, arrived):
+    copy = pltpu.make_async_copy(source.at[:, : EARLY * WINDOW], out, arrived)
+    copy.start()
+    copy.wait()
+
+
+def load_kernel(
+    source,
+    early,
+    own,
+    basis,
+    soil,
+    frozen,
+    table,
+    late,
+    begun,
+    conduct,
+    diagonal,
+    above,
+    local,
+    gram,
+    vector,
+    ratio,
+    value,
+    arrived,
+):
+    copies = []
+    for index in range((LAYERS - EARLY) // CHUNK):
+        begin, size = index * CHUNK * WINDOW, CHUNK * WINDOW
+        copies.append(
+            pltpu.make_async_copy(
+                source.at[:, EARLY * WINDOW + begin : EARLY * WINDOW + begin + size],
+                late.at[:, begin : begin + size],
+                arrived.at[index],
+            )
+        )
+    for copy in copies:
+        copy.start()
+    columns_kernel(
+        basis, soil, frozen, table, conduct, diagonal, above, local, gram, ratio, value
+    )
     vector[...] = own[:FLAT, :].astype(F32)
-    zero = jnp.zeros((8, COLS), F32)
-    totals = project_part(coarse, vector, 1, (zero,) * 8)
+    totals = (jnp.zeros((8, COLS), F32),) * 8
+    totals = project_part(early, vector, 1, totals, 0, 0, EARLY)
+    for index, copy in enumerate(copies):
+        copy.wait()
+        totals = project_part(late, vector, 1, totals, EARLY, index * CHUNK, CHUNK)
     for r in range(4):
-        out[8 * r : 8 * r + 8, :] = totals[2 * r] + totals[2 * r + 1]
-
-
-def rhs_kernel(coarse, begun, before, after, count, out, vector):
+        begun[8 * r : 8 * r + 8, :] = totals[2 * r] + totals[2 * r + 1]
+
+
+def rhs_kernel(early, late, begun, before, after, count, out, vector):
     place = lax.axis_index("gx")
     last = lax.axis_size("gx") - 1
     zero = jnp.zeros((8, COLS), F32)
     totals = tuple(begun[4 * s : 4 * s + 8, :] if s % 2 == 0 else zero for s in range(8))
     vector[...] = jnp.where(place > 0, before[:FLAT, :].astype(F32), 0.0)
-    totals = project_part(coarse, vector, 0, totals)
+    totals = project_part(early, vector, 0, totals, 0, 0, EARLY)
+    totals = project_part(late, vector, 0, totals, EARLY, 0, LAYERS - EARLY)
     vector[...] = jnp.where(place < last, after[:FLAT, :].astype(F32), 0.0)
-    totals = project_part(coarse, vector, 2, totals)
+    totals = project_part(early, vector, 2, totals, 0, 0, EARLY)
+    totals = project_part(late, vector, 2, totals, EARLY, 0, LAYERS - EARLY)
     full = jnp.concatenate([totals[2 * r] + totals[2 * r + 1] for r in range(4)], axis=0)
     sums = jnp.sum(full, axis=1, keepdims=True)
     index = lax.broadcasted_iota(jnp.int32, (K, COLS), 0)
@@ -153,34 +211,65 @@
     return merge(parts[0], parts[1], one, 1)
 
 
-def spread_part(coarse, weights, part, out):
+def reduction_masks():
     row = lax.broadcasted_iota(jnp.int32, (8, COLS), 0)
-    where = (row < 4, row % 4 < 2, row % 2 < 1)
+    return row < 4, row % 4 < 2, row % 2 < 1
+
+
+def combine(coarse, base, width, weights):
+    terms = [
+        coarse[8 * r : 8 * r + 8, pl.ds(base, width)].astype(F32) * weights[r][:, :width]
+        for r in range(4)
+    ]
+    return (terms[0] + terms[1]) + (terms[2] + terms[3])
+
+
+def spread_part(coarse, weights, part, out, first, count):
+    where = reduction_masks()
 
     def body(pair, carry):
         halves = []
         for half in range(2):
             base = pl.multiple_of((2 * pair + half) * WINDOW + part * PART, 128)
-            terms = [
-                coarse[8 * r : 8 * r + 8, pl.ds(base, PART)].astype(F32) * weights[r]
-                for r in range(4)
-            ]
-            halves.append((terms[0] + terms[1]) + (terms[2] + terms[3]))
+            halves.append(combine(coarse, base, PART, weights))
         for j in range(5):
             tiles = [
                 halves[half][:, (5 * m + j) * COLS : (5 * m + j + 1) * COLS]
                 for half in range(2)
                 for m in range(4)
             ]
-            start = pl.multiple_of(j * RUNS + 8 * pair, 8)
+            start = pl.multiple_of(j * RUNS + 4 * first + 8 * pair, 8)
             out[pl.ds(start, 8), :] = reduce_eight(tiles, where)
         return carry
 
-    lax.fori_loop(0, LAYERS // 2, body, 0, unroll=2)
+    lax.fori_loop(0, count // 2, body, 0, unroll=5)
+
+
+def spread_ends(coarse, weights, out, first, count):
+    where = reduction_masks()
+
+    def body(pair, carry):
+        tiles = []
+        for half in range(2):
+            base = (2 * pair + half) * WINDOW + PART
+            for begin in (0, 18 * COLS):
+                both = combine(coarse, pl.multiple_of(base + begin, 128), 2 * COLS, weights)
+                tiles += [both[:, :COLS], both[:, COLS:]]
+        start = pl.multiple_of(4 * first + 8 * pair, 8)
+        out[pl.ds(start, 8), :] = reduce_eight(tiles, where)
+        return carry
+
+    lax.fori_loop(0, count // 2, body, 0, unroll=5)
+
+
+def widen(weights):
+    return [
+        jnp.concatenate([weights[8 * r : 8 * r + 8, :]] * (PART // COLS), axis=1) for r in range(4)
+    ]
 
 
 def spread_kernel(
-    coarse, inverse, gathered, count, local, own, up, dn, up2, dn2, edge, rhs, low, high
+    early, late, inverse, gathered, count, local, weights, up, dn, up2, dn2, edge, rhs, low, high, ends
 ):
     at = lanes(K)
     rows = jnp.zeros((K, COLS), F32)
@@ -193,12 +282,12 @@
     solved = jnp.sum(total, axis=1, keepdims=True)
     index = lax.broadcasted_iota(jnp.int32, (K, COLS), 0)
     solved = jnp.where(index < count[0, 0], solved, 0.0).astype(BF16).astype(F32)
-    weights = [
-        jnp.concatenate([solved[8 * r : 8 * r + 8, :]] * (PART // COLS), axis=1) for r in range(4)
-    ]
-    spread_part(coarse, weights, 0, low)
-    spread_part(coarse, weights, 2, high)
-    spread_part(coarse, weights, 1, own)
+    weights[...] = solved
+    wide = widen(solved)
+    for coarse, first, size in ((early, 0, EARLY), (late, EARLY, LAYERS - EARLY)):
+        spread_part(coarse, wide, 0, low, first, size)
+        spread_part(coarse, wide, 2, high, first, size)
+        spread_ends(coarse, wide, ends, first, size)
     at = lanes(LAYERS)
 
     def strip(ref, j, m):
@@ -213,13 +302,16 @@
         ref[FLAT : FLAT + 80, :] = top
         ref[FLAT + 80 :, :] = (ring - top.astype(F32)).astype(BF16)
 
+    def end(index):
+        return ends[pl.ds(index, LAYERS, stride=4), :]
+
     last = strip(local, 3, 3)
     put(
         up,
         high,
         both(
-            strip(own, 3, 3) + jnp.where(at >= 112, last, 0.0),
-            strip(own, 4, 3) + jnp.where(at < 112, last, 0.0),
+            end(2) + jnp.where(at >= 112, last, 0.0),
+            end(3) + jnp.where(at < 112, last, 0.0),
         ),
     )
     first = strip(local, 0, 0)
@@ -227,14 +319,20 @@
         dn,
         low,
         both(
-            strip(own, 0, 0) + jnp.where(at >= 16, first, 0.0),
-            strip(own, 1, 0) + jnp.where(at < 16, first, 0.0),
+            end(0) + jnp.where(at >= 16, first, 0.0),
+            end(1) + jnp.where(at < 16, first, 0.0),
         ),
     )
     up2[...] = both(strip(high, 3, 3), strip(high, 4, 3)).astype(BF16)
     dn2[...] = both(strip(low, 0, 0), strip(low, 1, 0)).astype(BF16)
     edge[:80, :] = both(strip(low, 3, 3), strip(low, 4, 3))
     edge[80:, :] = both(strip(high, 0, 0), strip(high, 1, 0))
+
+
+def own_spread_kernel(early, late, weights, own):
+    wide = widen(weights[...])
+    spread_part(early, wide, 1, own, 0, EARLY)
+    spread_part(late, wide, 1, own, EARLY, LAYERS - EARLY)
 
 
 def fold_rows_kernel(own, edge, local, before, after, before2, after2, field, rim, up, dn):
@@ -487,62 +585,61 @@
 def on_device(basis, soil, frozen, soil_table, coarse_basis, coarse_inverse, active_count):
     basis = basis.reshape(4, CELLS, COLS)
     soil, frozen = soil.reshape(CELLS, COLS), frozen.reshape(CELLS, COLS)
-    coarse = pltpu.with_memory_space_constraint(coarse_basis.reshape(K, -1), pltpu.VMEM)
+    source = pltpu.with_memory_space_constraint(coarse_basis.reshape(K, -1), pltpu.HBM)
     devices = lax.axis_size("gx") * lax.axis_size("gy")
-
-    def pack(basis_ref, *refs):
-        pack_kernel(basis_ref, *refs)
-
-    one = pl.BlockSpec((1, CELLS, COLS), lambda i: (3, 0, 0))
-    whole = pl.BlockSpec((CELLS, COLS), lambda i: (0, 0))
-    up, dn, flat = pl.pallas_call(
-        pack,
-        grid=(1,),
-        in_specs=[one, whole, whole],
-        out_specs=[
-            pl.BlockSpec((RUNS, COLS), lambda i: (0, 0)),
-            pl.BlockSpec((RUNS, COLS), lambda i: (0, 0)),
-            pl.BlockSpec((FLAT + 80, COLS), lambda i: (0, 0)),
-        ],
-        out_shape=[
+    field_space = pltpu.VMEM((CELLS, COLS), F32)
+    kinds = pltpu.VMEM((CELLS, COLS), jnp.int32)
+    up, dn, flat = call(
+        pack_kernel,
+        [
             shape(RUNS, COLS, dtype=BF16),
             shape(RUNS, COLS, dtype=BF16),
             shape(FLAT + 80, COLS, dtype=BF16),
         ],
-        scratch_shapes=[pltpu.VMEM((CELLS, COLS), F32)],
-        compiler_params=pltpu.CompilerParams(vmem_limit_bytes=16 * 2**20),
+        [HB] * 3,
+        [pltpu.with_memory_space_constraint(x, pltpu.HBM) for x in (basis, soil, frozen)],
+        [field_space, kinds, kinds, field_space, pltpu.SemaphoreType.DMA((3,))],
         name="pack",
-    )(basis, soil, frozen)
+    )
     left, right = shift(up, "gy", 1), shift(dn, "gy", -1)
-    conduct, diagonal, above, local, gram = call(
-        columns_kernel,
-        [shape(CELLS, COLS)] * 4 + [shape(80, COLS)],
-        [VM, VM, VM, SM],
-        (basis, soil, frozen, soil_table),
-        [pltpu.VMEM((CELLS, COLS), F32)] * 2,
-        flops=10_000_000,
-        moved=4_000_000,
-        name="columns",
-    )
+    early = call(
+        early_kernel,
+        pltpu.VMEM((K, EARLY * WINDOW), BF16),
+        [HB],
+        (source,),
+        [pltpu.SemaphoreType.DMA],
+        out_specs=VM,
+        moved=10_000_000,
+        name="early",
+    )
+    early, flat = lax.optimization_barrier((early, flat))
     flat = call(
         flat_kernel, shape(FLAT + 80, COLS, dtype=BF16), [VM] * 3, (flat, left, right), name="flat"
     )
     before, after = shift(flat, "gx", 1), shift(flat, "gx", -1)
-    begun = call(
-        own_rhs_kernel,
-        shape(K, COLS),
-        [VM] * 2,
-        (coarse, flat),
-        [pltpu.VMEM((FLAT, COLS), F32)],
-        flops=6_000_000,
-        moved=6_000_000,
-        name="own_rhs",
+    late, begun, conduct, diagonal, above, local, gram = call(
+        load_kernel,
+        [pltpu.VMEM((K, (LAYERS - EARLY) * WINDOW), BF16), shape(K, COLS)]
+        + [shape(CELLS, COLS)] * 4
+        + [shape(80, COLS)],
+        [HB] + [VM] * 5 + [SM],
+        (source, early, flat, basis, soil, frozen, soil_table),
+        [
+            pltpu.VMEM((FLAT, COLS), F32),
+            field_space,
+            field_space,
+            pltpu.SemaphoreType.DMA(((LAYERS - EARLY) // CHUNK,)),
+        ],
+        out_specs=[VM] * 7,
+        flops=16_000_000,
+        moved=20_000_000,
+        name="load",
     )
     lines = call(
         rhs_kernel,
         shape(devices, COLS),
-        [VM] * 4 + [SM],
-        (coarse, begun, before, after, active_count),
+        [VM] * 5 + [SM],
+        (early, late, begun, before, after, active_count),
         [pltpu.VMEM((FLAT, COLS), F32)],
         flops=12_000_000,
         moved=12_000_000,
@@ -551,24 +648,39 @@
     gathered = exchange(lines)
     message = shape(FLAT + 160, COLS, dtype=BF16)
     small = shape(80, COLS, dtype=BF16)
-    own, up, dn, up2, dn2, edge = call(
+    weights, up, dn, up2, dn2, edge = call(
         spread_kernel,
-        [shape(FLAT, COLS), message, message, small, small, shape(160, COLS)],
-        [VM, VM, VM, SM, VM],
-        (coarse, coarse_inverse, gathered, active_count, local),
-        [pltpu.VMEM((K, COLS), F32)] + [pltpu.VMEM((FLAT, COLS), F32)] * 2,
+        [shape(K, COLS), message, message, small, small, shape(160, COLS)],
+        [VM, VM, VM, VM, SM, VM],
+        (early, late, coarse_inverse, gathered, active_count, local),
+        [
+            pltpu.VMEM((K, COLS), F32),
+            pltpu.VMEM((FLAT, COLS), F32),
+            pltpu.VMEM((FLAT, COLS), F32),
+            pltpu.VMEM((RUNS, COLS), F32),
+        ],
         flops=40_000_000,
         moved=20_000_000,
         name="spread",
     )
     near = shift(up, "gx", 1), shift(dn, "gx", -1)
     far = shift(up2, "gx", 2), shift(dn2, "gx", -2)
+    own = call(
+        own_spread_kernel,
+        shape(FLAT, COLS),
+        [VM] * 3,
+        (early, late, weights),
+        flops=20_000_000,
+        moved=7_000_000,
+        name="own_spread",
+    )
+    conduct, diagonal, weights = lax.optimization_barrier((conduct, diagonal, weights))
     faces, total = call(
         faces_kernel,
         [shape(4, CELLS, COLS), shape(CELLS, COLS)],
         [VM, VM, SM, VM, VM, VM, VM],
         (conduct, diagonal, soil_table, left, right, before, after),
-        [pltpu.VMEM((CELLS, COLS), F32)],
+        [field_space],
         flops=4_000_000,
         moved=2_000_000,
         name="faces",
@@ -586,7 +698,7 @@
         [shape(CELLS, COLS), shape(CELLS, COLS), shape(devices, COLS)],
         [VM] * 11,
         (field, rim, up, dn, left, right, basis, faces, total, above, gram),
-        [pltpu.VMEM((CELLS, COLS), F32)],
+        [field_space],
         name="image",
     )
     gathered = exchange(sums)

time: 104 us -> 87.1 us (0.84)
  local copies, waits for them, and re-layouts: 22.4 us -> 0.02 us
  blocking collectives: 18.9 us -> 35.7 us
  waiting for transfers between devices: 14.8 us -> 5.45 us
  starting transfers between devices: 29.4 us -> 20.9 us
  Pallas kernels: 16.6 us -> 23.4 us
    unnamed x34 -> x10, local copies, waits for them, and re-layouts: 22.4 us -> 0.02 us
    all_to_all x1 -> x2, blocking collectives: 18.9 us -> 35.7 us  [exchange(): out = lax.all_to_all(lines.reshape(size, 1, COLS), ('gx', 'gy'), 0, 0)]
    all_to_all x1 -> x0, starting transfers between devices: 8.38 us -> none  [exchange(): out = lax.all_to_all(lines.reshape(size, 1, COLS), ('gx', 'gy'), 0, 0)]
    pallas_call x9 -> x11, Pallas kernels: 16.3 us -> 23.4 us  [call(): pl.pallas_call(kernel, out_shape=outs, in_specs=specs, out_specs=out_spec...]
    all_to_all x1 -> x0, waiting for transfers between devices: 5.15 us -> none  [exchange(): out = lax.all_to_all(lines.reshape(size, 1, COLS), ('gx', 'gy'), 0, 0)]
    ppermute x10, waiting for transfers between devices: 9.64 us -> 5.45 us  [shift(): lax.ppermute(values, axis, [(i, (i + step) % count) for i in range(count)])]
  transfers between devices with their start and end apart: 11 -> 10, of which waited for: 7 -> 4; matrix products, arithmetic and copies ran while one was open for 0% -> 0% of each run, Pallas kernels for 5% -> 14%
where the time goes in v1:
time: 87.1 us; the launch traced here: 86.9 us
  blocking collectives  35.7 us (41%)
  Pallas kernels  23.4 us (27%)
  starting transfers between devices  20.9 us (24%)
  waiting for transfers between devices  5.45 us (6%)
  between operations  1.43 us (2%)
    all_to_all x2, blocking collectives, exchange(): out = lax.all_to_all(lines.reshape(size, 1, COLS), ('gx', 'gy'), 0, 0)  35.7 us
    pallas_call x11, Pallas kernels, call(): pl.pallas_call(kernel, out_shape=outs, in_specs=specs, out_specs=out_spec...  23.4 us
    ppermute x10, starting transfers between devices, shift(): lax.ppermute(values, axis, [(i, (i + step) % count) for i in range(count)])  20.9 us
    ppermute x10, waiting for transfers between devices, shift(): lax.ppermute(values, axis, [(i, (i + step) % count) for i in range(count)])  5.45 us
  transfers between devices with their start and end apart: 10, of which 4 were waited for; matrix products, arithmetic and copies ran while one was open for 0% of the time, Pallas kernels for 14%

profile of v1, /device:TPU:1, one launch (start us, length us, event | category | flops | bytes accessed | tf_op | source)
XLA Modules:
  0.0 86.9 jit_solution(1260333720301464421)
XLA Ops:
  0.6 1.5 %pack.1 = (bf16[160,128]{1,0:T(8,128)(2,1)S(1)}, bf16[160,128]{1,0:T(8,128)(2,1)S(1)}, bf16[880,128]{1,0:T(8,128)(2,1)S(1)}) custom-call(f32[4,640,128]{2,1,0:T(8,128)} %bitcast.14, s32[640,128]{1,0:T(8,128)} %bitcast.18, s32[640,128]{1,0:T(8,128)} %bitcast.20), custom_call_target="tpu_custom_call" | custom-call | tf_op jit(solution)/shard_map/pack/pallas_call | solution.py:33
  2.1 2.7 %collective-permute-start = (bf16[160,128]{1,0:T(8,128)(2,1)S(1)}, bf16[160,128]{1,0:T(8,128)(2,1)S(1)}, u32[]{:S(2)}, u32[]{:S(2)}) collective-permute-start(bf16[160,128]{1,0:T(8,128)(2,1)S(1)} %get-tuple-element.37), channel_id=1, source_target_pairs={{0,1},{1,2},{2,3},{3,4},{4,5},{5,6},{6,7},{7,0},{8,9},{9,10},{10,1... | collective-permute-start | bytes 122888 | tf_op jit(solution)/shard_map/ppermute | solution.py:576
  4.8 0.0 collective-permute-start.1
  4.8 0.0 copy-start
  4.8 0.0 copy-start.1
  4.8 0.0 copy-start.2
  4.8 0.0 copy-start.4
  4.8 2.5 %early.1 = bf16[32,76800]{1,0:T(8,128)(2,1)S(1)} custom-call(bf16[32,307200]{1,0:T(8,128)(2,1)} %bitcast.26), custom_call_target="tpu_custom_call" | custom-call | bytes 10000000 | tf_op jit(solution)/shard_map/early/pallas_call | solution.py:33
  7.4 0.0 collective-permute-done.left
  7.4 0.8 collective-permute-done.1.right
  8.2 0.1 flat.1.own
  8.3 6.0 %collective-permute-start.3 = (bf16[880,128]{1,0:T(8,128)(2,1)S(1)}, bf16[880,128]{1,0:T(8,128)(2,1)S(1)}, u32[]{:S(2)}, u32[]{:S(2)}) collective-permute-start(bf16[880,128]{1,0:T(8,128)(2,1)S(1)} %flat.1.own), channel_id=1, source_target_pairs={{0,120},{8,0},{16,8},{24,16},{32,24},{40,32},{48,40},{56,48},{64,5... | collective-permute-start | bytes 675848 | tf_op jit(solution)/shard_map/ppermute | solution.py:576
  14.3 0.0 collective-permute-start.2
  15.0 0.0 copy-done
  15.0 0.0 copy-done.1
  15.0 0.0 copy-done.2
  15.0 0.0 copy-done.4
  15.0 7.0 %load.1 = (bf16[32,230400]{1,0:T(8,128)(2,1)S(1)}, f32[32,128]{1,0:T(8,128)S(1)}, f32[640,128]{1,0:T(8,128)S(1)}, f32[640,128]{1,0:T(8,128)S(1)}, f32[640,128]{1...) custom-call(bf16[32,307200]{1,0:T(8,128)(2,1)} %bitcast.27, bf16[32,76800]{1,0:T(8,128)(2,1)S(1)} %early.1, ...), custom_call_target="tpu_custom_call" | custom-call | flops 16000000 | bytes 20000000 | tf_op jit(solution)/shard_map/load/pallas_call | solution.py:33
  22.0 0.0 collective-permute-done.3.after
  22.0 1.4 %collective-permute-done.2.before = bf16[880,128]{1,0:T(8,128)(2,1)S(1)} collective-permute-done((bf16[880,128]{1,0:T(8,128)(2,1)S(1)}, bf16[880,128]{1,0:T(8,128)(2,1)S(1)}, u32[]{:S(2)}, u32[]{:S(2)}) %collective-permute-start.2) | collective-permute-done | bytes 225312 | tf_op jit(solution)/shard_map/ppermute | solution.py:576
  23.4 0.0 copy-start.3
  23.4 2.9 %rhs.1 = f32[128,128]{1,0:T(8,128)S(1)} custom-call(bf16[32,76800]{1,0:T(8,128)(2,1)S(1)} %early.1, bf16[32,230400]{1,0:T(8,128)(2,1)S(1)} %get-tuple-element.39.late, f32[32,128]{1,0:T(8,128)S(1)} %get-tuple-element.40.begun, bf16[880,128]{1,0:T(8,128)(2,1)S(1)} %collective-permute-done.2.before, bf16[880,128]{1,0:T(8,128)(2,1)S(1)} %collective-permute-done.3.after, ...), custom_call_target="tpu_custom_call" | custom-call | flops 12000000 | bytes 12000000 | tf_op jit(solution)/shard_map/rhs/pallas_call | solution.py:33
  26.3 16.8 %all_to_all.10 = f32[128,1,128]{2,1,0:T(1,128)S(1)} all-to-all(f32[128,1,128]{2,1,0:T(1,128)S(1)} %bitcast.23), channel_id=1, replica_groups=mesh['gx'=16,'gy'=8] {'gx','gy'}, dimensions={0} | all-to-all | bytes 131072 | tf_op jit(solution)/shard_map/all_to_all | solution.py:581
  43.1 0.0 copy-done.3
  43.1 3.8 %spread.1 = (f32[32,128]{1,0:T(8,128)S(1)}, bf16[960,128]{1,0:T(8,128)(2,1)S(1)}, bf16[960,128]{1,0:T(8,128)(2,1)S(1)}, bf16[80,128]{1,0:T(8,128)(2,1)S(1)}, bf1...) custom-call(bf16[32,76800]{1,0:T(8,128)(2,1)S(1)} %early.1, bf16[32,230400]{1,0:T(8,128)(2,1)S(1)} %get-tuple-element.39.late, ...), custom_call_target="tpu_custom_call" | custom-call | flops 40000000 | bytes 20000000 | tf_op jit(solution)/shard_map/spread/pallas_call | solution.py:33
  46.9 0.5 collective-permute-start.4
  47.4 4.4 %collective-permute-start.5 = (bf16[960,128]{1,0:T(8,128)(2,1)S(1)}, bf16[960,128]{1,0:T(8,128)(2,1)S(1)}, u32[]{:S(2)}, u32[]{:S(2)}) collective-permute-start(bf16[960,128]{1,0:T(8,128)(2,1)S(1)} %get-tuple-element.45), channel_id=1, source_target_pairs={{0,120},{8,0},{16,8},{24,16},{32,24},{40,32},{48,40},{56,48},{64,5... | collective-permute-start | bytes 737288 | tf_op jit(solution)/shard_map/ppermute | solution.py:576
  51.8 0.0 collective-permute-start.6
  51.8 5.1 %collective-permute-start.7 = (bf16[80,128]{1,0:T(8,128)(2,1)S(1)}, bf16[80,128]{1,0:T(8,128)(2,1)S(1)}, u32[]{:S(2)}, u32[]{:S(2)}) collective-permute-start(bf16[80,128]{1,0:T(8,128)(2,1)S(1)} %get-tuple-element.47), channel_id=1, source_target_pairs={{0,112},{8,120},{16,0},{24,8},{32,16},{40,24},{48,32},{56,40},{64,... | collective-permute-start | bytes 61448 | tf_op jit(solution)/shard_map/ppermute | solution.py:576
  56.9 1.6 %own_spread.1.own = f32[800,128]{1,0:T(8,128)S(1)} custom-call(bf16[32,76800]{1,0:T(8,128)(2,1)S(1)} %early.1, bf16[32,230400]{1,0:T(8,128)(2,1)S(1)} %get-tuple-element.39.late, f32[32,128]{1,0:T(8,128)S(1)} %get-tuple-element.42.weights), custom_call_target="tpu_custom_call" | custom-call | flops 20000000 | bytes 7000000 | tf_op jit(solution)/shard_map/own_spread/pallas_call | solution.py:33
  58.5 0.0 collective-permute-done.6.before2
  58.5 0.0 collective-permute-done.7.after2
  58.5 0.0 collective-permute-done.4.before
  58.5 0.0 collective-permute-done.5.after
  58.6 0.2 fold_rows.1
  58.7 2.3 %collective-permute-start.8 = (f32[200,128]{1,0:T(8,128)S(1)}, f32[200,128]{1,0:T(8,128)S(1)}, u32[]{:S(2)}, u32[]{:S(2)}) collective-permute-start(f32[200,128]{1,0:T(8,128)S(1)} %get-tuple-element.50.up), channel_id=1, source_target_pairs={{0,1},{1,2},{2,3},{3,4},{4,5},{5,6},{6,7},{7,0},{8,9},{9,10},{10,1... | collective-permute-start | bytes 307208 | tf_op jit(solution)/shard_map/ppermute | solution.py:576
  61.0 0.0 collective-permute-start.9
  61.0 1.2 %faces.1 = (f32[4,640,128]{2,1,0:T(8,128)S(1)}, f32[640,128]{1,0:T(8,128)S(1)}) custom-call(f32[640,128]{1,0:T(8,128)S(1)} %get-tuple-element.54.conduct, f32[640,128]{1,0:T(8,128)S(1)} %get-tuple-element.55.diagonal, f32[4,8]{1,0:T(4,128)S(1)} %copy-done.4, bf16[160,128]{1,0:T(8,128)(2,1)S(1)} %collective-permute-done.left, ...), custom_call_target="tpu_custom_call" | custom-call | flops 4000000 | bytes 2000000 | tf_op jit(solution)/shard_map/faces/pallas_call | solution.py:33
  62.2 0.5 collective-permute-done.8.left
  62.7 2.7 %collective-permute-done.9.right = f32[200,128]{1,0:T(8,128)S(1)} collective-permute-done((f32[200,128]{1,0:T(8,128)S(1)}, f32[200,128]{1,0:T(8,128)S(1)}, u32[]{:S(2)}, u32[]{:S(2)}) %collective-permute-start.9) | collective-permute-done | bytes 102432 | tf_op jit(solution)/shard_map/ppermute | solution.py:576
  65.4 1.4 %image.1 = (f32[640,128]{1,0:T(8,128)}, f32[640,128]{1,0:T(8,128)S(1)}, f32[128,128]{1,0:T(8,128)S(1)}) custom-call(f32[640,128]{1,0:T(8,128)S(1)} %get-tuple-element.48.field, f32[80,128]{1,0:T(8,128)S(1)} %get-tuple-element.49.rim, f32[200,128]{1,0:T(8,128)S(1)} %get-tuple-element.50.up, f32[200,128]{1,0:T(8,128)S(1)} %get-tuple-element.51.dn, ...), custom_call_target="tpu_custom_call" | custom-call | tf_op jit(solution)/shard_map/image/pallas_call | solution.py:33
  66.8 18.9 %all_to_all.11 = f32[128,1,128]{2,1,0:T(1,128)S(1)} all-to-all(f32[128,1,128]{2,1,0:T(1,128)S(1)} %bitcast.25), channel_id=1, replica_groups=mesh['gx'=16,'gy'=8] {'gx','gy'}, dimensions={0} | all-to-all | bytes 131072 | tf_op jit(solution)/shard_map/all_to_all | solution.py:581
  85.7 1.2 %next.1 = (f32[640,128]{1,0:T(8,128)}, f32[5]{0:T(128)}) custom-call(f32[128,128]{1,0:T(8,128)S(1)} %bitcast.24, f32[640,128]{1,0:T(8,128)S(1)} %get-tuple-element.62.image, f32[4,640,128]{2,1,0:T(8,128)S(1)} %bitcast.17), custom_call_target="tpu_custom_call" | custom-call | tf_op jit(solution)/shard_map/next/pallas_call | solution.py:33
Async XLA Ops:
  2.1 5.3 %collective-permute-start = (bf16[160,128]{1,0:T(8,128)(2,1)S(1)}, bf16[160,128]{1,0:T(8,128)(2,1)S(1)}, u32[]{:S(2)}, u32[]{:S(2)}) collective-permute-start(bf16[160,128]{1,0:T(8,128)(2,1)S(1)} %get-tuple-element.37), channel_id=1, source_target_pairs={{0,1},{1,2},{2,3},{3,4},{4,5},{5,6},{6,7},{7,0},{8,9},{9,10},{10,1... | collective-permute-start | bytes 122888 | tf_op jit(solution)/shard_map/ppermute | solution.py:576
  4.8 3.4 %collective-permute-start.1 = (bf16[160,128]{1,0:T(8,128)(2,1)S(1)}, bf16[160,128]{1,0:T(8,128)(2,1)S(1)}, u32[]{:S(2)}, u32[]{:S(2)}) collective-permute-start(bf16[160,128]{1,0:T(8,128)(2,1)S(1)} %get-tuple-element.38), channel_id=1, source_target_pairs={{0,7},{1,0},{2,1},{3,2},{4,3},{5,4},{6,5},{7,6},{8,15},{9,8},{10,9... | collective-permute-start | bytes 122888 | tf_op jit(solution)/shard_map/ppermute | solution.py:576
  4.8 10.2 %copy-start = (f32[4,40,16,128]{3,2,1,0:T(8,128)S(1)}, f32[4,40,16,128]{3,2,1,0:T(8,128)}, u32[]{:S(2)}) copy-start(f32[4,40,16,128]{3,2,1,0:T(8,128)} %param.7) | copy-start | bytes 3932164
  4.8 10.2 %copy-start.1 = (s32[40,16,128]{2,1,0:T(8,128)S(1)}, s32[40,16,128]{2,1,0:T(8,128)}, u32[]{:S(2)}) copy-start(s32[40,16,128]{2,1,0:T(8,128)} %param.8) | copy-start | bytes 983044
  4.8 10.2 %copy-start.2 = (s32[40,16,128]{2,1,0:T(8,128)S(1)}, s32[40,16,128]{2,1,0:T(8,128)}, u32[]{:S(2)}) copy-start(s32[40,16,128]{2,1,0:T(8,128)} %param.9) | copy-start | bytes 983044
  4.8 10.2 %copy-start.4 = (f32[4,8]{1,0:T(4,128)S(1)}, f32[4,8]{1,0:T(4,128)}, u32[]{:S(2)}) copy-start(f32[4,8]{1,0:T(4,128)} %table.3) | copy-start | bytes 388
  8.3 13.7 %collective-permute-start.3 = (bf16[880,128]{1,0:T(8,128)(2,1)S(1)}, bf16[880,128]{1,0:T(8,128)(2,1)S(1)}, u32[]{:S(2)}, u32[]{:S(2)}) collective-permute-start(bf16[880,128]{1,0:T(8,128)(2,1)S(1)} %flat.1.own), channel_id=1, source_target_pairs={{0,120},{8,0},{16,8},{24,16},{32,24},{40,32},{48,40},{56,48},{64,5... | collective-permute-start | bytes 675848 | tf_op jit(solution)/shard_map/ppermute | solution.py:576
  14.3 9.1 %collective-permute-start.2 = (bf16[880,128]{1,0:T(8,128)(2,1)S(1)}, bf16[880,128]{1,0:T(8,128)(2,1)S(1)}, u32[]{:S(2)}, u32[]{:S(2)}) collective-permute-start(bf16[880,128]{1,0:T(8,128)(2,1)S(1)} %flat.1.own), channel_id=1, source_target_pairs={{0,8},{8,16},{16,24},{24,32},{32,40},{40,48},{48,56},{56,64},{64,7... | collective-permute-start | bytes 675848 | tf_op jit(solution)/shard_map/ppermute | solution.py:576
  23.4 19.7 %copy-start.3 = (f32[32,4096]{1,0:T(8,128)S(1)}, f32[32,4096]{1,0:T(8,128)}, u32[]{:S(2)}) copy-start(f32[32,4096]{1,0:T(8,128)} %inverse.1) | copy-start | bytes 1572868
  46.9 11.6 %collective-permute-start.4 = (bf16[960,128]{1,0:T(8,128)(2,1)S(1)}, bf16[960,128]{1,0:T(8,128)(2,1)S(1)}, u32[]{:S(2)}, u32[]{:S(2)}) collective-permute-start(bf16[960,128]{1,0:T(8,128)(2,1)S(1)} %get-tuple-element.44), channel_id=1, source_target_pairs={{0,8},{8,16},{16,24},{24,32},{32,40},{40,48},{48,56},{56,64},{64,7... | collective-permute-start | bytes 737288 | tf_op jit(solution)/shard_map/ppermute | solution.py:576
  47.4 11.1 %collective-permute-start.5 = (bf16[960,128]{1,0:T(8,128)(2,1)S(1)}, bf16[960,128]{1,0:T(8,128)(2,1)S(1)}, u32[]{:S(2)}, u32[]{:S(2)}) collective-permute-start(bf16[960,128]{1,0:T(8,128)(2,1)S(1)} %get-tuple-element.45), channel_id=1, source_target_pairs={{0,120},{8,0},{16,8},{24,16},{32,24},{40,32},{48,40},{56,48},{64,5... | collective-permute-start | bytes 737288 | tf_op jit(solution)/shard_map/ppermute | solution.py:576
  51.8 6.7 %collective-permute-start.6 = (bf16[80,128]{1,0:T(8,128)(2,1)S(1)}, bf16[80,128]{1,0:T(8,128)(2,1)S(1)}, u32[]{:S(2)}, u32[]{:S(2)}) collective-permute-start(bf16[80,128]{1,0:T(8,128)(2,1)S(1)} %get-tuple-element.46), channel_id=1, source_target_pairs={{0,16},{8,24},{16,32},{24,40},{32,48},{40,56},{48,64},{56,72},{64,... | collective-permute-start | bytes 61448 | tf_op jit(solution)/shard_map/ppermute | solution.py:576
  51.8 6.7 %collective-permute-start.7 = (bf16[80,128]{1,0:T(8,128)(2,1)S(1)}, bf16[80,128]{1,0:T(8,128)(2,1)S(1)}, u32[]{:S(2)}, u32[]{:S(2)}) collective-permute-start(bf16[80,128]{1,0:T(8,128)(2,1)S(1)} %get-tuple-element.47), channel_id=1, source_target_pairs={{0,112},{8,120},{16,0},{24,8},{32,16},{40,24},{48,32},{56,40},{64,... | collective-permute-start | bytes 61448 | tf_op jit(solution)/shard_map/ppermute | solution.py:576
  58.7 3.9 %collective-permute-start.8 = (f32[200,128]{1,0:T(8,128)S(1)}, f32[200,128]{1,0:T(8,128)S(1)}, u32[]{:S(2)}, u32[]{:S(2)}) collective-permute-start(f32[200,128]{1,0:T(8,128)S(1)} %get-tuple-element.50.up), channel_id=1, source_target_pairs={{0,1},{1,2},{2,3},{3,4},{4,5},{5,6},{6,7},{7,0},{8,9},{9,10},{10,1... | collective-permute-start | bytes 307208 | tf_op jit(solution)/shard_map/ppermute | solution.py:576
  61.0 4.4 %collective-permute-start.9 = (f32[200,128]{1,0:T(8,128)S(1)}, f32[200,128]{1,0:T(8,128)S(1)}, u32[]{:S(2)}, u32[]{:S(2)}) collective-permute-start(f32[200,128]{1,0:T(8,128)S(1)} %get-tuple-element.51.dn), channel_id=1, source_target_pairs={{0,7},{1,0},{2,1},{3,2},{4,3},{5,4},{6,5},{7,6},{8,15},{9,8},{10,9... | collective-permute-start | bytes 307208 | tf_op jit(solution)/shard_map/ppermute | solution.py:576

commit v2 on v1

--- a/solution.py
+++ b/solution.py
@@ -15,8 +15,11 @@
 RUNS = CELLS // 4
 FLAT = 5 * RUNS
 WINDOW = 7680
-EARLY = 10
-CHUNK = 10
+EARLY = 12
+CHUNK = 14
+PAD = FLAT + 48
+SIDE = RUNS + 48
+ENDS = FLAT + 80
 PART = 2560
 WEIGHT_V, WEIGHT_H, EPS = 4.0, 1.0, 1e-06
 
@@ -50,11 +53,28 @@
     return 2.0 * first * second / (first + second)
 
 
+def steps(count):
+    return max(n for n in range(1, 8) if count % n == 0)
+
+
 def turn(values, amount):
     return pltpu.roll(values, amount % COLS, 1)
 
 
-def pack_kernel(basis_in, soil_in, frozen_in, up, dn, flat, basis, soil, frozen, code, arrived):
+def pack_kernel(
+    basis_in,
+    soil_in,
+    frozen_in,
+    first,
+    second,
+    flat,
+    kinds,
+    basis,
+    code,
+    soil,
+    frozen,
+    arrived,
+):
     copies = [
         pltpu.make_async_copy(basis_in.at[3], basis, arrived.at[0]),
         pltpu.make_async_copy(soil_in, soil, arrived.at[1]),
@@ -79,28 +99,41 @@
         to_dn = jnp.where(high, turned, jnp.where(at == cut - 1, turn(kind, cut - 1), to_dn))
         flats[q] = jnp.where(at >= cut, turned, flats[q])
         flats[q + 1] = jnp.where(at < cut, turned, flats[q + 1])
-    up[...] = to_up.astype(BF16)
-    dn[...] = to_dn.astype(BF16)
+    even = lax.axis_index("gy") % 2 == 0
+    first[...] = jnp.where(even, to_up, to_dn).astype(BF16)
+    second[...] = jnp.where(even, to_dn, to_up).astype(BF16)
     for j in range(5):
         flat[j * RUNS : (j + 1) * RUNS, :] = flats[j].astype(BF16)
-    rows = [code[pl.ds(0, LAYERS, stride=ROWS), :], code[pl.ds(ROWS - 1, LAYERS, stride=ROWS), :]]
-    flat[FLAT:, :] = jnp.concatenate(rows, axis=0).astype(BF16)
-
-
-def flat_kernel(own, left, right, out):
+    spare = jnp.zeros((PAD - FLAT - LAYERS, COLS), F32)
+    for index, row in enumerate((0, ROWS - 1)):
+        line = jnp.concatenate([code[pl.ds(row, LAYERS, stride=ROWS), :], spare], axis=0)
+        kinds[index] = line
+
+
+def sides(even, first, second):
+    return jnp.where(even, second, first), jnp.where(even, first, second)
+
+
+def flat_kernel(own, kinds, from_first, from_second, first, second):
     place = lax.axis_index("gy")
     last = lax.axis_size("gy") - 1
     at = lanes(RUNS)
-    from_left = jnp.where(place > 0, left[...].astype(F32), 0.0)
-    from_right = jnp.where(place < last, right[...].astype(F32), 0.0)
+    from_left, from_right = sides(
+        place % 2 == 0, from_first[...].astype(F32), from_second[...].astype(F32)
+    )
+    from_left = jnp.where(place > 0, from_left, 0.0)
+    from_right = jnp.where(place < last, from_right, 0.0)
     for j in range(5):
         part = own[j * RUNS : (j + 1) * RUNS, :].astype(F32)
         if j < 4:
             part = jnp.where((at >= 32 * j) & (at < 32 * j + 16), from_left, part)
         if j > 0:
             part = jnp.where((at >= 32 * j - 16) & (at < 32 * j), from_right, part)
-        out[j * RUNS : (j + 1) * RUNS, :] = part.astype(BF16)
-    out[FLAT:, :] = own[FLAT:, :]
+        first[j * RUNS : (j + 1) * RUNS, :] = part.astype(BF16)
+        second[j * RUNS : (j + 1) * RUNS, :] = part.astype(BF16)
+    even = lax.axis_index("gx") % 2 == 0
+    first[FLAT:, :] = jnp.where(even, kinds[1], kinds[0]).astype(BF16)
+    second[FLAT:, :] = jnp.where(even, kinds[0], kinds[1]).astype(BF16)
 
 
 def project_part(coarse, vector, part, totals, first, begin, count):
@@ -123,35 +156,55 @@
                 totals[slot] = totals[slot] + product[:, t * COLS : (t + 1) * COLS]
         return tuple(totals)
 
-    return lax.fori_loop(0, count, body, totals, unroll=5)
-
-
-def early_kernel(source, out, arrived):
-    copy = pltpu.make_async_copy(source.at[:, : EARLY * WINDOW], out, arrived)
-    copy.start()
-    copy.wait()
-
-
-def load_kernel(
+    return lax.fori_loop(0, count, body, totals, unroll=steps(count))
+
+
+def early_kernel(
     source,
-    early,
-    own,
+    table_in,
     basis,
-    soil,
-    frozen,
-    table,
-    late,
-    begun,
+    code,
+    out,
     conduct,
     diagonal,
     above,
     local,
-    gram,
-    vector,
     ratio,
     value,
+    table,
     arrived,
 ):
+    small = pltpu.make_async_copy(table_in, table, arrived.at[0])
+    small.start()
+    copy = pltpu.make_async_copy(source.at[:, : EARLY * WINDOW], out, arrived.at[1])
+    copy.start()
+    small.wait()
+    solve_columns(basis, code, table, conduct, diagonal, above, local, ratio, value)
+    copy.wait()
+
+
+def multiply_out(basis, gram):
+    def body(level, grams):
+        grams = list(grams)
+        cut = pl.ds(pl.multiple_of(level * ROWS, ROWS), ROWS)
+        vectors = [basis[j, cut, :] for j in range(4)]
+        slot = 0
+        for i in range(4):
+            for j in range(i, 4):
+                square = vectors[i] * vectors[j]
+                grams[slot] = grams[slot] + (square[:8] + square[8:])
+                slot += 1
+        return tuple(grams)
+
+    zero = jnp.zeros((8, COLS), F32)
+    grams = lax.fori_loop(0, LAYERS, body, (zero,) * 10, unroll=4)
+    for slot in range(10):
+        gram[8 * slot : 8 * slot + 8, :] = grams[slot]
+
+
+def load_kernel(source, basis_in, early, own, late, basis, begun, gram, vector, arrived):
+    ready = pltpu.make_async_copy(basis_in, basis, arrived.at[0])
+    ready.start()
     copies = []
     for index in range((LAYERS - EARLY) // CHUNK):
         begin, size = index * CHUNK * WINDOW, CHUNK * WINDOW
@@ -159,17 +212,16 @@
             pltpu.make_async_copy(
                 source.at[:, EARLY * WINDOW + begin : EARLY * WINDOW + begin + size],
                 late.at[:, begin : begin + size],
-                arrived.at[index],
+                arrived.at[index + 1],
             )
         )
     for copy in copies:
         copy.start()
-    columns_kernel(
-        basis, soil, frozen, table, conduct, diagonal, above, local, gram, ratio, value
-    )
     vector[...] = own[:FLAT, :].astype(F32)
     totals = (jnp.zeros((8, COLS), F32),) * 8
     totals = project_part(early, vector, 1, totals, 0, 0, EARLY)
+    ready.wait()
+    multiply_out(basis, gram)
     for index, copy in enumerate(copies):
         copy.wait()
         totals = project_part(late, vector, 1, totals, EARLY, index * CHUNK, CHUNK)
@@ -177,21 +229,33 @@
         begun[8 * r : 8 * r + 8, :] = totals[2 * r] + totals[2 * r + 1]
 
 
-def rhs_kernel(early, late, begun, before, after, count, out, vector):
+def project_neighbour(early, late, whole, vector, upper, valid, totals):
+    vector[...] = jnp.where(valid, whole[:FLAT, :].astype(F32), 0.0)
+    part = jnp.where(upper, 2, 0)
+    totals = project_part(early, vector, part, totals, 0, 0, EARLY)
+    return project_part(late, vector, part, totals, EARLY, 0, LAYERS - EARLY)
+
+
+def unfold(begun):
+    zero = jnp.zeros((8, COLS), F32)
+    return tuple(begun[4 * s : 4 * s + 8, :] if s % 2 == 0 else zero for s in range(8))
+
+
+def first_rhs_kernel(early, late, begun, whole, out, vector):
+    upper = lax.axis_index("gx") % 2 == 0
+    totals = project_neighbour(early, late, whole, vector, upper, True, unfold(begun))
+    for r in range(4):
+        out[8 * r : 8 * r + 8, :] = totals[2 * r] + totals[2 * r + 1]
+
+
+def second_rhs_kernel(early, late, begun, whole, count, out, vector):
     place = lax.axis_index("gx")
-    last = lax.axis_size("gx") - 1
-    zero = jnp.zeros((8, COLS), F32)
-    totals = tuple(begun[4 * s : 4 * s + 8, :] if s % 2 == 0 else zero for s in range(8))
-    vector[...] = jnp.where(place > 0, before[:FLAT, :].astype(F32), 0.0)
-    totals = project_part(early, vector, 0, totals, 0, 0, EARLY)
-    totals = project_part(late, vector, 0, totals, EARLY, 0, LAYERS - EARLY)
-    vector[...] = jnp.where(place < last, after[:FLAT, :].astype(F32), 0.0)
-    totals = project_part(early, vector, 2, totals, 0, 0, EARLY)
-    totals = project_part(late, vector, 2, totals, EARLY, 0, LAYERS - EARLY)
+    valid = (place > 0) & (place < lax.axis_size("gx") - 1)
+    totals = project_neighbour(early, late, whole, vector, place % 2 == 1, valid, unfold(begun))
     full = jnp.concatenate([totals[2 * r] + totals[2 * r + 1] for r in range(4)], axis=0)
     sums = jnp.sum(full, axis=1, keepdims=True)
     index = lax.broadcasted_iota(jnp.int32, (K, COLS), 0)
-    keep = (lanes(K) % K == index) & (index < count[0, 0])
+    keep = (lanes(K) % K == index) & (index < count[...])
     row = jnp.sum(jnp.where(keep, sums, 0.0), axis=0, keepdims=True)
     out[...] = jnp.broadcast_to(row, out.shape)
 
@@ -242,24 +306,23 @@
             out[pl.ds(start, 8), :] = reduce_eight(tiles, where)
         return carry
 
-    lax.fori_loop(0, count // 2, body, 0, unroll=5)
-
-
-def spread_ends(coarse, weights, out, first, count):
+    lax.fori_loop(0, count // 2, body, 0, unroll=steps(count // 2))
+
+
+def spread_ends(coarse, weights, begin, out, first, count):
     where = reduction_masks()
 
-    def body(pair, carry):
+    def body(four, carry):
         tiles = []
-        for half in range(2):
-            base = (2 * pair + half) * WINDOW + PART
-            for begin in (0, 18 * COLS):
-                both = combine(coarse, pl.multiple_of(base + begin, 128), 2 * COLS, weights)
-                tiles += [both[:, :COLS], both[:, COLS:]]
-        start = pl.multiple_of(4 * first + 8 * pair, 8)
+        for layer in range(4):
+            base = (4 * four + layer) * WINDOW + PART + begin
+            both = combine(coarse, pl.multiple_of(base, 128), 2 * COLS, weights)
+            tiles += [both[:, :COLS], both[:, COLS:]]
+        start = pl.multiple_of(2 * first + 8 * four, 8)
         out[pl.ds(start, 8), :] = reduce_eight(tiles, where)
         return carry
 
-    lax.fori_loop(0, count // 2, body, 0, unroll=5)
+    lax.fori_loop(0, count // 4, body, 0, unroll=steps(count // 4))
 
 
 def widen(weights):
@@ -268,9 +331,7 @@
     ]
 
 
-def spread_kernel(
-    early, late, inverse, gathered, count, local, weights, up, dn, up2, dn2, edge, rhs, low, high, ends
-):
+def solve(inverse, gathered, count, rhs):
     at = lanes(K)
     rows = jnp.zeros((K, COLS), F32)
     for e in range(4):
@@ -281,14 +342,16 @@
         total = total + inverse[:, i * COLS : (i + 1) * COLS] * rhs[i : i + 1, :]
     solved = jnp.sum(total, axis=1, keepdims=True)
     index = lax.broadcasted_iota(jnp.int32, (K, COLS), 0)
-    solved = jnp.where(index < count[0, 0], solved, 0.0).astype(BF16).astype(F32)
-    weights[...] = solved
+    return jnp.where(index < count[...], solved, 0.0).astype(BF16).astype(F32)
+
+
+def spread_to(upper, early, late, solved, local, message, near, whole, ends):
     wide = widen(solved)
-    for coarse, first, size in ((early, 0, EARLY), (late, EARLY, LAYERS - EARLY)):
-        spread_part(coarse, wide, 0, low, first, size)
-        spread_part(coarse, wide, 2, high, first, size)
-        spread_ends(coarse, wide, ends, first, size)
-    at = lanes(LAYERS)
+    part, begin = jnp.where(upper, 2, 0), jnp.where(upper, 18 * COLS, 0)
+    for coarse, start, size in ((early, 0, EARLY), (late, EARLY, LAYERS - EARLY)):
+        spread_part(coarse, wide, part, whole, start, size)
+        spread_ends(coarse, wide, begin, ends, start, size)
+    message[:FLAT, :] = whole[...].astype(BF16)
 
     def strip(ref, j, m):
         return ref[pl.ds(j * RUNS + m, LAYERS, stride=4), :]
@@ -296,37 +359,37 @@
     def both(first, second):
         return jnp.concatenate([first, second], axis=0)
 
-    def put(ref, whole, ring):
-        ref[:FLAT, :] = whole[...].astype(BF16)
-        top = ring.astype(BF16)
-        ref[FLAT : FLAT + 80, :] = top
-        ref[FLAT + 80 :, :] = (ring - top.astype(F32)).astype(BF16)
-
-    def end(index):
-        return ends[pl.ds(index, LAYERS, stride=4), :]
-
-    last = strip(local, 3, 3)
-    put(
-        up,
-        high,
-        both(
-            end(2) + jnp.where(at >= 112, last, 0.0),
-            end(3) + jnp.where(at < 112, last, 0.0),
-        ),
-    )
-    first = strip(local, 0, 0)
-    put(
-        dn,
-        low,
-        both(
-            end(0) + jnp.where(at >= 16, first, 0.0),
-            end(1) + jnp.where(at < 16, first, 0.0),
-        ),
-    )
-    up2[...] = both(strip(high, 3, 3), strip(high, 4, 3)).astype(BF16)
-    dn2[...] = both(strip(low, 0, 0), strip(low, 1, 0)).astype(BF16)
-    edge[:80, :] = both(strip(low, 3, 3), strip(low, 4, 3))
-    edge[80:, :] = both(strip(high, 0, 0), strip(high, 1, 0))
+    at = lanes(LAYERS)
+    cut = jnp.where(upper, 112, 16)
+    row = jnp.where(upper, strip(local, 3, 3), strip(local, 0, 0))
+    ours = [ends[pl.ds(index, LAYERS, stride=2), :] for index in range(2)]
+    message[FLAT:, :] = both(
+        ours[0] + jnp.where(at >= cut, row, 0.0), ours[1] + jnp.where(at < cut, row, 0.0)
+    ).astype(BF16)
+    top = both(strip(whole, 0, 0), strip(whole, 1, 0))
+    bottom = both(strip(whole, 3, 3), strip(whole, 4, 3))
+    near[...] = jnp.where(upper, top, bottom)
+    return jnp.where(upper, bottom, top)
+
+
+def second_spread_kernel(
+    early, late, inverse, gathered, count, local, weights, message, near, far, rhs, whole, ends
+):
+    solved = solve(inverse, gathered, count, rhs)
+    weights[...] = solved
+    upper = lax.axis_index("gx") % 2 == 1
+    far[...] = spread_to(upper, early, late, solved, local, message, near, whole, ends)
+
+
+def first_spread_kernel(
+    early, late, weights, local, far, message, near, far_first, far_second, whole, ends
+):
+    place = lax.axis_index("gx")
+    upper = place % 2 == 0
+    own = spread_to(upper, early, late, weights[...], local, message, near, whole, ends)
+    swapped = (place % 4 == 1) | (place % 4 == 2)
+    far_first[...] = jnp.where(swapped, far[...], own).astype(BF16)
+    far_second[...] = jnp.where(swapped, own, far[...]).astype(BF16)
 
 
 def own_spread_kernel(early, late, weights, own):
@@ -335,18 +398,32 @@
     spread_part(late, wide, 1, own, EARLY, LAYERS - EARLY)
 
 
-def fold_rows_kernel(own, edge, local, before, after, before2, after2, field, rim, up, dn):
+def fold_rows_kernel(
+    own,
+    near_first,
+    near_second,
+    local,
+    from_first,
+    from_second,
+    far_first,
+    far_second,
+    field,
+    rim,
+    up,
+    dn,
+    first,
+    second,
+):
     place = lax.axis_index("gx")
     last = lax.axis_size("gx") - 1
+    even, lower = place % 2 == 0, place % 4 < 2
     at = lanes(RUNS)
     whole = []
     for j in range(5):
         cut = slice(j * RUNS, (j + 1) * RUNS)
-        part = (
-            own[cut, :]
-            + jnp.where(place > 0, before[cut, :].astype(F32), 0.0)
-            + jnp.where(place < last, after[cut, :].astype(F32), 0.0)
-        )
+        before, after = sides(even, from_first[cut, :].astype(F32), from_second[cut, :].astype(F32))
+        part = own[cut, :] + jnp.where(place > 0, before, 0.0)
+        part = part + jnp.where(place < last, after, 0.0)
         if j < 4:
             part = part + jnp.where(at >= 32 * j + 16, local[cut, :], 0.0)
         if j > 0:
@@ -365,22 +442,23 @@
     up[:RUNS, :] = to_up
     dn[:RUNS, :] = to_dn
 
-    def ring(ours, near, far, valid):
-        return (
-            ours
-            + near[FLAT : FLAT + 80, :].astype(F32)
-            + near[FLAT + 80 :, :].astype(F32)
-            + jnp.where(valid, far[...].astype(F32), 0.0)
-        )
-
-    top = ring(edge[:80, :], before, before2, place > 1)
-    bottom = ring(edge[80:, :], after, after2, place < last - 1)
+    before, after = sides(even, from_first[FLAT:, :].astype(F32), from_second[FLAT:, :].astype(F32))
+    before2, after2 = sides(lower, far_first[...].astype(F32), far_second[...].astype(F32))
+    near_before, near_after = sides(even, near_first[...], near_second[...])
+    top = near_before + before + jnp.where(place > 1, before2, 0.0)
+    bottom = near_after + after + jnp.where(place < last - 1, after2, 0.0)
     at = lanes(LAYERS)
     half = LAYERS
     rim[:half, :] = jnp.where(at >= 112, top[:half], top[half:])
     rim[half:, :] = jnp.where(at >= 16, bottom[:half], bottom[half:])
     up[RUNS:, :] = jnp.where(at >= 96, top[half:], bottom[half:])
     dn[RUNS:, :] = jnp.where(at >= 96, top[:half], bottom[:half])
+    even = lax.axis_index("gy") % 2 == 0
+    spare = jnp.zeros((SIDE - RUNS - LAYERS, COLS), F32)
+    to_up = jnp.concatenate([up[...], spare], axis=0)
+    to_dn = jnp.concatenate([dn[...], spare], axis=0)
+    first[...] = jnp.where(even, to_up, to_dn).astype(BF16)
+    second[...] = jnp.where(even, to_dn, to_up).astype(BF16)
 
 
 def look_up(kind, table, rows):
@@ -391,12 +469,16 @@
     return value
 
 
-def columns_kernel(basis, soil, frozen, table, conduct, diagonal, above, local, gram, ratio, value):
-    kind = soil[...] + 8 * frozen[...]
-    conduct[...] = look_up(kind, table, (0, 1))
-    diagonal[...] = look_up(kind, table, (2, 3))
+def solve_columns(basis, code, table, conduct, diagonal, above, local, ratio, value):
+    def body(index, carry):
+        cut = pl.ds(pl.multiple_of(index * 64, 64), 64)
+        kind = code[cut, :]
+        conduct[cut, :] = look_up(kind, table, (0, 1))
+        diagonal[cut, :] = look_up(kind, table, (2, 3))
+        return carry
+
+    lax.fori_loop(0, CELLS // 64, body, 0)
     zero = jnp.zeros((ROWS, COLS), F32)
-    grams = [jnp.zeros((8, COLS), F32) for _ in range(10)]
     below = zero
     last_ratio = zero
     last_value = zero
@@ -412,32 +494,36 @@
         denom = sides + 4.0 * WEIGHT_H * own + below * last_ratio
         inverse = 1.0 / denom
         last_ratio = -over * inverse
-        last_value = (basis[3, cut, :] + below * last_value) * inverse
+        last_value = (basis[cut, :] + below * last_value) * inverse
         ratio[cut, :] = last_ratio
         value[cut, :] = last_value
         below = over
-        vectors = [basis[j, cut, :] for j in range(4)]
-        slot = 0
-        for i in range(4):
-            for j in range(i, 4):
-                square = vectors[i] * vectors[j]
-                grams[slot] = grams[slot] + (square[:8] + square[8:])
-                slot += 1
     for level in range(LAYERS - 2, -1, -1):
         cut = slice(level * ROWS, (level + 1) * ROWS)
         last_value = value[cut, :] - ratio[cut, :] * last_value
         value[cut, :] = last_value
     for q in range(4):
         local[q * RUNS : (q + 1) * RUNS, :] = turn(value[pl.ds(q, RUNS, stride=4), :], 32 * q + 16)
-    for slot in range(10):
-        gram[8 * slot : 8 * slot + 8, :] = grams[slot]
-
-
-def faces_kernel(conduct, diagonal, table, left, right, before, after, faces, total, side):
+
+
+def faces_kernel(
+    conduct,
+    diagonal,
+    table,
+    first_y,
+    second_y,
+    first_x,
+    second_x,
+    faces,
+    total,
+    side,
+):
     gx, gy = lax.axis_index("gx"), lax.axis_index("gy")
     last_x, last_y = lax.axis_size("gx") - 1, lax.axis_size("gy") - 1
     at = lanes(RUNS)
-    from_left, from_right = left[...].astype(F32), right[...].astype(F32)
+    from_left, from_right = sides(
+        gy % 2 == 0, first_y[...].astype(F32), second_y[...].astype(F32)
+    )
     kinds = jnp.zeros((RUNS, COLS), F32)
     for q in range(4):
         kinds = jnp.where(at == 32 * q + 16, from_left, kinds)
@@ -445,15 +531,18 @@
     known = look_up(kinds.astype(jnp.int32), table, (0, 1))
     for q in range(4):
         side[pl.ds(q, RUNS, stride=4), :] = turn(known, -(32 * q + 16))
-    row_before = look_up(before[FLAT:, :].astype(F32).astype(jnp.int32), table, (0, 1))
-    row_after = look_up(after[FLAT:, :].astype(F32).astype(jnp.int32), table, (0, 1))
+    before, after = sides(
+        gx % 2 == 0, first_x[FLAT:, :].astype(F32), second_x[FLAT:, :].astype(F32)
+    )
+    row_before = look_up(before.astype(jnp.int32), table, (0, 1))
+    row_after = look_up(after.astype(jnp.int32), table, (0, 1))
     at = lanes(ROWS)
     row = lax.broadcasted_iota(jnp.int32, (ROWS, COLS), 0)
     for level in range(LAYERS):
         cut = slice(level * ROWS, (level + 1) * ROWS)
         own = conduct[cut, :]
         aside = side[cut, :]
-        over = row_before[LAYERS + level : LAYERS + level + 1, :]
+        over = row_before[level : level + 1, :]
         under = row_after[level : level + 1, :]
         weights = [
             jnp.where((at > 0) | (gy > 0), harmonic(own, jnp.where(at == 0, aside, turn(own, 1))), 0.0),
@@ -481,13 +570,32 @@
 
 
 def image_kernel(
-    field, rim, up, dn, left, right, basis, faces, total, above, gram, precond, image, sums, side
+    field,
+    rim,
+    up,
+    dn,
+    from_first,
+    from_second,
+    basis,
+    faces,
+    total,
+    above,
+    gram,
+    precond,
+    image,
+    sums,
+    side,
 ):
     gy = lax.axis_index("gy")
     last_y = lax.axis_size("gy") - 1
     at = lanes(RUNS)
-    from_left = jnp.where(gy > 0, left[...], 0.0)
-    from_right = jnp.where(gy < last_y, right[...], 0.0)
+    from_left, from_right = sides(
+        gy % 2 == 0,
+        from_first[...].astype(F32)[: RUNS + LAYERS],
+        from_second[...].astype(F32)[: RUNS + LAYERS],
+    )
+    from_left = jnp.where(gy > 0, from_left, 0.0)
+    from_right = jnp.where(gy < last_y, from_right, 0.0)
     to_left = dn[...] + from_left
     to_right = up[...] + from_right
     for q in range(4):
@@ -571,9 +679,40 @@
         out[cut, :] = value
 
 
-def shift(values, axis, step):
-    count = lax.axis_size(axis)
-    return lax.ppermute(values, axis, [(i, (i + step) % count) for i in range(count)])
+def swap(values, partner):
+    across, along = lax.axis_size("gx"), lax.axis_size("gy")
+    pairs = []
+    for a in range(across):
+        for b in range(along):
+            c, d = partner(a, b)
+            if not 0 <= d < along:
+                c, d = a ^ 1, b
+            if not 0 <= c < across:
+                c, d = a, b ^ 1
+            pairs.append((a * along + b, c * along + d))
+    return lax.ppermute(values, ("gx", "gy"), pairs)
+
+
+def swap_y(first, second):
+    return (
+        swap(first, lambda a, b: (a, b ^ 1)),
+        swap(second, lambda a, b: (a, ((b + 1) ^ 1) - 1)),
+    )
+
+
+def swap_x_first(values):
+    return swap(values, lambda a, b: (a ^ 1, b))
+
+
+def swap_x_second(values):
+    return swap(values, lambda a, b: (((a + 1) ^ 1) - 1, b))
+
+
+def swap_far(first, second):
+    return (
+        swap(first, lambda a, b: (a ^ 2, b)),
+        swap(second, lambda a, b: (((a + 2) ^ 2) - 2, b)),
+    )
 
 
 def exchange(lines):
@@ -589,82 +728,113 @@
     devices = lax.axis_size("gx") * lax.axis_size("gy")
     field_space = pltpu.VMEM((CELLS, COLS), F32)
     kinds = pltpu.VMEM((CELLS, COLS), jnp.int32)
-    up, dn, flat = call(
+    basis, soil, frozen = (
+        pltpu.with_memory_space_constraint(x, pltpu.HBM) for x in (basis, soil, frozen)
+    )
+    first, second, flat, kinds_x, current, code = call(
         pack_kernel,
         [
             shape(RUNS, COLS, dtype=BF16),
             shape(RUNS, COLS, dtype=BF16),
-            shape(FLAT + 80, COLS, dtype=BF16),
+            shape(FLAT, COLS, dtype=BF16),
+            shape(2, PAD - FLAT, COLS),
+            pltpu.VMEM((CELLS, COLS), F32),
+            pltpu.VMEM((CELLS, COLS), F32),
         ],
         [HB] * 3,
-        [pltpu.with_memory_space_constraint(x, pltpu.HBM) for x in (basis, soil, frozen)],
-        [field_space, kinds, kinds, field_space, pltpu.SemaphoreType.DMA((3,))],
+        (basis, soil, frozen),
+        [kinds, kinds, pltpu.SemaphoreType.DMA((3,))],
+        out_specs=[VM] * 6,
         name="pack",
     )
-    left, right = shift(up, "gy", 1), shift(dn, "gy", -1)
-    early = call(
+    from_y = swap_y(first, second)
+    early, conduct, diagonal, above, local = call(
         early_kernel,
-        pltpu.VMEM((K, EARLY * WINDOW), BF16),
-        [HB],
-        (source,),
-        [pltpu.SemaphoreType.DMA],
-        out_specs=VM,
+        [pltpu.VMEM((K, EARLY * WINDOW), BF16)] + [shape(CELLS, COLS)] * 4,
+        [HB, HB, VM, VM],
+        (source, pltpu.with_memory_space_constraint(soil_table, pltpu.HBM), current, code),
+        [
+            field_space,
+            field_space,
+            pltpu.SMEM((4, 8), F32),
+            pltpu.SemaphoreType.DMA((2,)),
+        ],
+        out_specs=[VM] * 5,
         moved=10_000_000,
         name="early",
     )
     early, flat = lax.optimization_barrier((early, flat))
-    flat = call(
-        flat_kernel, shape(FLAT + 80, COLS, dtype=BF16), [VM] * 3, (flat, left, right), name="flat"
-    )
-    before, after = shift(flat, "gx", 1), shift(flat, "gx", -1)
-    late, begun, conduct, diagonal, above, local, gram = call(
+    flat, second = call(
+        flat_kernel, [shape(PAD, COLS, dtype=BF16)] * 2, [VM] * 4, (flat, kinds_x, *from_y), name="flat"
+    )
+    from_second = swap_x_second(second)
+    from_x = swap_x_first(flat), from_second
+    late, basis, begun, gram = call(
         load_kernel,
-        [pltpu.VMEM((K, (LAYERS - EARLY) * WINDOW), BF16), shape(K, COLS)]
-        + [shape(CELLS, COLS)] * 4
-        + [shape(80, COLS)],
-        [HB] + [VM] * 5 + [SM],
-        (source, early, flat, basis, soil, frozen, soil_table),
+        [
+            pltpu.VMEM((K, (LAYERS - EARLY) * WINDOW), BF16),
+            pltpu.VMEM((4, CELLS, COLS), F32),
+            shape(K, COLS),
+            shape(80, COLS),
+        ],
+        [HB, HB, VM, VM],
+        (source, basis, early, flat),
         [
             pltpu.VMEM((FLAT, COLS), F32),
-            field_space,
-            field_space,
-            pltpu.SemaphoreType.DMA(((LAYERS - EARLY) // CHUNK,)),
+            pltpu.SemaphoreType.DMA(((LAYERS - EARLY) // CHUNK + 1,)),
         ],
-        out_specs=[VM] * 7,
+        out_specs=[VM] * 4,
         flops=16_000_000,
         moved=20_000_000,
         name="load",
     )
+    vector = pltpu.VMEM((FLAT, COLS), F32)
+    begun = call(
+        first_rhs_kernel,
+        shape(K, COLS),
+        [VM] * 4,
+        (early, late, begun, from_x[0]),
+        [vector],
+        flops=6_000_000,
+        moved=6_000_000,
+        name="first_rhs",
+    )
     lines = call(
-        rhs_kernel,
+        second_rhs_kernel,
         shape(devices, COLS),
-        [VM] * 5 + [SM],
-        (early, late, begun, before, after, active_count),
-        [pltpu.VMEM((FLAT, COLS), F32)],
-        flops=12_000_000,
-        moved=12_000_000,
-        name="rhs",
+        [VM] * 5,
+        (early, late, begun, from_x[1], active_count),
+        [vector],
+        flops=6_000_000,
+        moved=6_000_000,
+        name="second_rhs",
     )
     gathered = exchange(lines)
-    message = shape(FLAT + 160, COLS, dtype=BF16)
-    small = shape(80, COLS, dtype=BF16)
-    weights, up, dn, up2, dn2, edge = call(
-        spread_kernel,
-        [shape(K, COLS), message, message, small, small, shape(160, COLS)],
-        [VM, VM, VM, VM, SM, VM],
+    message = shape(ENDS, COLS, dtype=BF16)
+    ends = pltpu.VMEM((2 * LAYERS, COLS), F32)
+    weights, second, near_second, far = call(
+        second_spread_kernel,
+        [shape(K, COLS), message, shape(80, COLS), shape(80, COLS)],
+        [VM] * 6,
         (early, late, coarse_inverse, gathered, active_count, local),
-        [
-            pltpu.VMEM((K, COLS), F32),
-            pltpu.VMEM((FLAT, COLS), F32),
-            pltpu.VMEM((FLAT, COLS), F32),
-            pltpu.VMEM((RUNS, COLS), F32),
-        ],
-        flops=40_000_000,
-        moved=20_000_000,
-        name="spread",
-    )
-    near = shift(up, "gx", 1), shift(dn, "gx", -1)
-    far = shift(up2, "gx", 2), shift(dn2, "gx", -2)
+        [pltpu.VMEM((K, COLS), F32), vector, ends],
+        flops=20_000_000,
+        moved=8_000_000,
+        name="second_spread",
+    )
+    from_second = swap_x_second(second)
+    first, near_first, far_first, far_second = call(
+        first_spread_kernel,
+        [message, shape(80, COLS)] + [shape(80, COLS, dtype=BF16)] * 2,
+        [VM] * 5,
+        (early, late, weights, local, far),
+        [vector, ends],
+        flops=20_000_000,
+        moved=8_000_000,
+        name="first_spread",
+    )
+    near = swap_x_first(first), from_second
+    far = swap_far(far_first, far_second)
     own = call(
         own_spread_kernel,
         shape(FLAT, COLS),
@@ -679,25 +849,27 @@
         faces_kernel,
         [shape(4, CELLS, COLS), shape(CELLS, COLS)],
         [VM, VM, SM, VM, VM, VM, VM],
-        (conduct, diagonal, soil_table, left, right, before, after),
+        (conduct, diagonal, soil_table, *from_y, *from_x),
         [field_space],
         flops=4_000_000,
         moved=2_000_000,
         name="faces",
     )
-    field, rim, up, dn = call(
+    field, rim, up, dn, first, second = call(
         fold_rows_kernel,
-        [shape(CELLS, COLS), shape(80, COLS), shape(RUNS + LAYERS, COLS), shape(RUNS + LAYERS, COLS)],
-        [VM] * 7,
-        (own, edge, local, *near, *far),
+        [shape(CELLS, COLS), shape(80, COLS)]
+        + [shape(RUNS + LAYERS, COLS)] * 2
+        + [shape(SIDE, COLS, dtype=BF16)] * 2,
+        [VM] * 8,
+        (own, near_first, near_second, local, *near, *far),
         name="fold_rows",
     )
-    left, right = shift(up, "gy", 1), shift(dn, "gy", -1)
+    from_y = swap_y(first, second)
     precond, image, sums = call(
         image_kernel,
         [shape(CELLS, COLS), shape(CELLS, COLS), shape(devices, COLS)],
         [VM] * 11,
-        (field, rim, up, dn, left, right, basis, faces, total, above, gram),
+        (field, rim, up, dn, *from_y, basis, faces, total, above, gram),
         [field_space],
         name="image",
     )

time: 87.1 us -> 74.5 us (0.86)
  starting transfers between devices: 20.9 us -> 13.5 us
  blocking collectives: 35.7 us -> 33.4 us
  waiting for transfers between devices: 5.45 us -> 3.48 us
  Pallas kernels: 23.4 us -> 22.5 us
    ppermute x10, starting transfers between devices: 20.9 us -> 13.5 us  [swap(): return lax.ppermute(values, ('gx', 'gy'), pairs)]
    all_to_all x2, blocking collectives: 35.7 us -> 33.4 us  [exchange(): out = lax.all_to_all(lines.reshape(size, 1, COLS), ('gx', 'gy'), 0, 0)]
    ppermute x10, waiting for transfers between devices: 5.45 us -> 3.48 us  [swap(): return lax.ppermute(values, ('gx', 'gy'), pairs)]
    pallas_call x11 -> x13, Pallas kernels: 23.4 us -> 22.5 us  [call(): pl.pallas_call(kernel, out_shape=outs, in_specs=specs, out_specs=out_spec...]
  transfers between devices with their start and end apart: 10 -> 10, of which waited for: 4 -> 2; matrix products, arithmetic and copies ran while one was open for 0% -> 0% of each run, Pallas kernels for 14% -> 20%
where the time goes in v2:
time: 74.5 us; the launch traced here: 74.3 us
  blocking collectives  33.4 us (45%)
  Pallas kernels  22.5 us (30%)
  starting transfers between devices  13.5 us (18%)
  waiting for transfers between devices  3.48 us (5%)
  between operations  1.41 us (2%)
    all_to_all x2, blocking collectives, exchange(): out = lax.all_to_all(lines.reshape(size, 1, COLS), ('gx', 'gy'), 0, 0)  33.4 us
    pallas_call x13, Pallas kernels, call(): pl.pallas_call(kernel, out_shape=outs, in_specs=specs, out_specs=out_spec...  22.5 us
    ppermute x10, starting transfers between devices, swap(): return lax.ppermute(values, ('gx', 'gy'), pairs)  13.5 us
    ppermute x10, waiting for transfers between devices, swap(): return lax.ppermute(values, ('gx', 'gy'), pairs)  3.48 us
  transfers between devices with their start and end apart: 10, of which 2 were waited for; matrix products, arithmetic and copies ran while one was open for 0% of the time, Pallas kernels for 20%

profile of v2, /device:TPU:1, one launch (start us, length us, event | category | flops | bytes accessed | tf_op | source)
XLA Modules:
  0.0 74.3 jit_solution(9004251245135139570)
XLA Ops:
  0.6 1.5 %pack.1 = (bf16[160,128]{1,0:T(8,128)(2,1)S(1)}, bf16[160,128]{1,0:T(8,128)(2,1)S(1)}, bf16[800,128]{1,0:T(8,128)(2,1)S(1)}, f32[2,48,128]{2,1,0:T(8,128)S(1)}, ...) custom-call(f32[4,640,128]{2,1,0:T(8,128)} %bitcast.20, s32[640,128]{1,0:T(8,128)} %bitcast.22, s32[640,128]{1,0:T(8,128)} %bitcast.23), custom_call_target="tpu_custom_call" | custom-call | tf_op jit(solution)/shard_map/pack/pallas_call | solution.py:36
  2.1 1.5 %collective-permute-start = (bf16[160,128]{1,0:T(8,128)(2,1)S(1)}, bf16[160,128]{1,0:T(8,128)(2,1)S(1)}, u32[]{:S(2)}, u32[]{:S(2)}) collective-permute-start(bf16[160,128]{1,0:T(8,128)(2,1)S(1)} %get-tuple-element.52), channel_id=1, source_target_pairs={{0,1},{1,0},{2,3},{3,2},{4,5},{5,4},{6,7},{7,6},{8,9},{9,8},{10,11... | collective-permute-start | bytes 122888 | tf_op jit(solution)/shard_map/ppermute | solution.py:693
  3.6 1.4 %collective-permute-start.1 = (bf16[160,128]{1,0:T(8,128)(2,1)S(1)}, bf16[160,128]{1,0:T(8,128)(2,1)S(1)}, u32[]{:S(2)}, u32[]{:S(2)}) collective-permute-start(bf16[160,128]{1,0:T(8,128)(2,1)S(1)} %get-tuple-element.53), channel_id=1, source_target_pairs={{0,8},{1,2},{2,1},{3,4},{4,3},{5,6},{6,5},{7,15},{8,0},{9,10},{10,... | collective-permute-start | bytes 122888 | tf_op jit(solution)/shard_map/ppermute | solution.py:693
  5.0 2.7 %early.1 = (bf16[32,92160]{1,0:T(8,128)(2,1)S(1)}, f32[640,128]{1,0:T(8,128)S(1)}, f32[640,128]{1,0:T(8,128)S(1)}, f32[640,128]{1,0:T(8,128)S(1)}, f32[640,128]{1,0:T(8,128)S(1)}) custom-call(bf16[32,307200]{1,0:T(8,128)(2,1)} %bitcast.18, f32[4,8]{1,0:T(4,128)} %table.1, f32[640,128]{1,0:T(8,128)S(1)} %get-tuple-element.45.basis, ...), custom_call_target="tpu_custom_call" | custom-call | bytes 10000000 | tf_op jit(solution)/shard_map/early/pallas_call | solution.py:36
  7.7 0.0 collective-permute-done.from_first.first_y
  7.7 0.0 collective-permute-done.1.from_second.second_y
  7.7 0.1 flat.1
  7.8 1.7 %collective-permute-start.2 = (bf16[848,128]{1,0:T(8,128)(2,1)S(1)}, bf16[848,128]{1,0:T(8,128)(2,1)S(1)}, u32[]{:S(2)}, u32[]{:S(2)}) collective-permute-start(bf16[848,128]{1,0:T(8,128)(2,1)S(1)} %get-tuple-element.54.own), channel_id=1, source_target_pairs={{0,8},{1,9},{2,10},{3,11},{4,12},{5,13},{6,14},{7,15},{8,0},{9,1},... | collective-permute-start | bytes 651272 | tf_op jit(solution)/shard_map/ppermute | solution.py:693
  9.5 0.4 collective-permute-start.3
  10.5 5.8 %load.1 = (bf16[32,215040]{1,0:T(8,128)(2,1)S(1)}, f32[4,640,128]{2,1,0:T(8,128)S(1)}, f32[32,128]{1,0:T(8,128)S(1)}, f32[80,128]{1,0:T(8,128)S(1)}) custom-call(bf16[32,307200]{1,0:T(8,128)(2,1)} %bitcast.19, f32[4,640,128]{2,1,0:T(8,128)} %bitcast.21, bf16[32,92160]{1,0:T(8,128)(2,1)S(1)} %get-tuple-element.49.early, ...), custom_call_target="tpu_custom_call" | custom-call | flops 16000000 | bytes 20000000 | tf_op jit(solution)/shard_map/load/pallas_call | solution.py:36
  16.3 0.0 collective-permute-done.2.whole.first_x
  16.4 1.4 %first_rhs.1.begun = f32[32,128]{1,0:T(8,128)S(1)} custom-call(bf16[32,92160]{1,0:T(8,128)(2,1)S(1)} %get-tuple-element.49.early, bf16[32,215040]{1,0:T(8,128)(2,1)S(1)} %get-tuple-element.55.late, f32[32,128]{1,0:T(8,128)S(1)} %get-tuple-element.56.begun, bf16[848,128]{1,0:T(8,128)(2,1)S(1)} %collective-permute-done.2.whole.first_x), custom_call_target="tpu_custom_call" | custom-call | flops 6000000 | bytes 6000000 | tf_op jit(solution)/shard_map/first_rhs/pallas_call | solution.py:36
  17.7 0.0 copy-start
  17.8 0.0 collective-permute-done.3.whole.second_x
  17.8 1.5 %second_rhs.1 = f32[128,128]{1,0:T(8,128)S(1)} custom-call(bf16[32,92160]{1,0:T(8,128)(2,1)S(1)} %get-tuple-element.49.early, bf16[32,215040]{1,0:T(8,128)(2,1)S(1)} %get-tuple-element.55.late, f32[32,128]{1,0:T(8,128)S(1)} %first_rhs.1.begun, bf16[848,128]{1,0:T(8,128)(2,1)S(1)} %collective-permute-done.3.whole.second_x, s32[1,1]{1,0:T(1,128)S(6)} %copy.12.count), custom_call_target="tpu_custom_call" | custom-call | flops 6000000 | bytes 6000000 | tf_op jit(solution)/shard_map/second_rhs/pallas_call | solution.py:36
  19.3 19.2 %all_to_all.10 = f32[128,1,128]{2,1,0:T(1,128)S(1)} all-to-all(f32[128,1,128]{2,1,0:T(1,128)S(1)} %bitcast.15), channel_id=1, replica_groups=mesh['gx'=16,'gy'=8] {'gx','gy'}, dimensions={0} | all-to-all | bytes 131072 | tf_op jit(solution)/shard_map/all_to_all | solution.py:720
  38.5 0.0 copy-done
  38.5 2.0 %second_spread.1 = (f32[32,128]{1,0:T(8,128)S(1)}, bf16[880,128]{1,0:T(8,128)(2,1)S(1)}, f32[80,128]{1,0:T(8,128)S(1)}, f32[80,128]{1,0:T(8,128)S(1)}) custom-call(bf16[32,92160]{1,0:T(8,128)(2,1)S(1)} %get-tuple-element.49.early, bf16[32,215040]{1,0:T(8,128)(2,1)S(1)} %get-tuple-element.55.late, f32[32,4096]{1,0:T(8,128)S(1)} %copy-done, ...), custom_call_target="tpu_custom_call" | custom-call | flops 20000000 | bytes 8000000 | tf_op jit(solution)/shard_map/second_spread/pallas_call | solution.py:36
  40.5 1.0 %collective-permute-start.5 = (bf16[880,128]{1,0:T(8,128)(2,1)S(1)}, bf16[880,128]{1,0:T(8,128)(2,1)S(1)}, u32[]{:S(2)}, u32[]{:S(2)}) collective-permute-start(bf16[880,128]{1,0:T(8,128)(2,1)S(1)} %get-tuple-element.64), channel_id=1, source_target_pairs={{0,1},{1,0},{2,3},{3,2},{4,5},{5,4},{6,7},{7,6},{8,16},{9,17},{10,... | collective-permute-start | bytes 675848 | tf_op jit(solution)/shard_map/ppermute | solution.py:693
  41.5 1.8 %first_spread.1 = (bf16[880,128]{1,0:T(8,128)(2,1)S(1)}, f32[80,128]{1,0:T(8,128)S(1)}, bf16[80,128]{1,0:T(8,128)(2,1)S(1)}, bf16[80,128]{1,0:T(8,128)(2,1)S(1)}) custom-call(bf16[32,92160]{1,0:T(8,128)(2,1)S(1)} %get-tuple-element.49.early, bf16[32,215040]{1,0:T(8,128)(2,1)S(1)} %get-tuple-element.55.late, f32[32,128]{1,0:T(8,128)S(1)} %get-tuple-element.59.weights, ...), custom_call_target="tpu_custom_call" | custom-call | flops 20000000 | bytes 8000000 | tf_op jit(solution)/shard_map/first_spread/pallas_call | solution.py:36
  43.3 0.3 collective-permute-start.4
  43.6 2.8 %collective-permute-start.6 = (bf16[80,128]{1,0:T(8,128)(2,1)S(1)}, bf16[80,128]{1,0:T(8,128)(2,1)S(1)}, u32[]{:S(2)}, u32[]{:S(2)}) collective-permute-start(bf16[80,128]{1,0:T(8,128)(2,1)S(1)} %get-tuple-element.65), channel_id=1, source_target_pairs={{0,16},{1,17},{2,18},{3,19},{4,20},{5,21},{6,22},{7,23},{8,24},{9,... | collective-permute-start | bytes 61448 | tf_op jit(solution)/shard_map/ppermute | solution.py:693
  46.4 0.0 copy-start.1
  46.4 1.7 %collective-permute-start.7 = (bf16[80,128]{1,0:T(8,128)(2,1)S(1)}, bf16[80,128]{1,0:T(8,128)(2,1)S(1)}, u32[]{:S(2)}, u32[]{:S(2)}) collective-permute-start(bf16[80,128]{1,0:T(8,128)(2,1)S(1)} %get-tuple-element.66), channel_id=1, source_target_pairs={{0,1},{1,0},{2,3},{3,2},{4,5},{5,4},{6,7},{7,6},{8,9},{9,8},{10,11... | collective-permute-start | bytes 61448 | tf_op jit(solution)/shard_map/ppermute | solution.py:693
  48.1 1.6 %own_spread.1.own = f32[800,128]{1,0:T(8,128)S(1)} custom-call(bf16[32,92160]{1,0:T(8,128)(2,1)S(1)} %get-tuple-element.49.early, bf16[32,215040]{1,0:T(8,128)(2,1)S(1)} %get-tuple-element.55.late, f32[32,128]{1,0:T(8,128)S(1)} %get-tuple-element.59.weights), custom_call_target="tpu_custom_call" | custom-call | flops 20000000 | bytes 7000000 | tf_op jit(solution)/shard_map/own_spread/pallas_call | solution.py:36
  49.7 1.2 %collective-permute-done.6.far_first = bf16[80,128]{1,0:T(8,128)(2,1)S(1)} collective-permute-done((bf16[80,128]{1,0:T(8,128)(2,1)S(1)}, bf16[80,128]{1,0:T(8,128)(2,1)S(1)}, u32[]{:S(2)}, u32[]{:S(2)}) %collective-permute-start.6) | collective-permute-done | bytes 20512 | tf_op jit(solution)/shard_map/ppermute | solution.py:693
  50.9 0.0 collective-permute-done.7.far_second
  50.9 0.0 collective-permute-done.5.from_second
  50.9 0.0 collective-permute-done.4.from_first
  50.9 0.3 fold_rows.1
  51.2 2.5 %collective-permute-start.8 = (bf16[208,128]{1,0:T(8,128)(2,1)S(1)}, bf16[208,128]{1,0:T(8,128)(2,1)S(1)}, u32[]{:S(2)}, u32[]{:S(2)}) collective-permute-start(bf16[208,128]{1,0:T(8,128)(2,1)S(1)} %get-tuple-element.71), channel_id=1, source_target_pairs={{0,1},{1,0},{2,3},{3,2},{4,5},{5,4},{6,7},{7,6},{8,9},{9,8},{10,11... | collective-permute-start | bytes 159752 | tf_op jit(solution)/shard_map/ppermute | solution.py:693
  53.7 0.3 collective-permute-start.9
  54.0 0.0 copy-done.1
  54.0 1.2 %faces.1 = (f32[4,640,128]{2,1,0:T(8,128)S(1)}, f32[640,128]{1,0:T(8,128)S(1)}) custom-call(f32[640,128]{1,0:T(8,128)S(1)} %get-tuple-element.76.conduct, f32[640,128]{1,0:T(8,128)S(1)} %get-tuple-element.77.diagonal, f32[4,8]{1,0:T(4,128)S(1)} %copy-done.1, bf16[160,128]{1,0:T(8,128)(2,1)S(1)} %collective-permute-done.from_first.first_y, ...), custom_call_target="tpu_custom_call" | custom-call | flops 4000000 | bytes 2000000 | tf_op jit(solution)/shard_map/faces/pallas_call | solution.py:36
  55.2 0.0 collective-permute-done.8.from_first
  55.2 2.3 %collective-permute-done.9.from_second = bf16[208,128]{1,0:T(8,128)(2,1)S(1)} collective-permute-done((bf16[208,128]{1,0:T(8,128)(2,1)S(1)}, bf16[208,128]{1,0:T(8,128)(2,1)S(1)}, u32[]{:S(2)}, u32[]{:S(2)}) %collective-permute-start.9) | collective-permute-done | bytes 53280 | tf_op jit(solution)/shard_map/ppermute | solution.py:693
  57.5 1.4 %image.1 = (f32[640,128]{1,0:T(8,128)}, f32[640,128]{1,0:T(8,128)S(1)}, f32[128,128]{1,0:T(8,128)S(1)}) custom-call(f32[640,128]{1,0:T(8,128)S(1)} %get-tuple-element.67.field, f32[80,128]{1,0:T(8,128)S(1)} %get-tuple-element.68.rim, f32[200,128]{1,0:T(8,128)S(1)} %get-tuple-element.69.up, f32[200,128]{1,0:T(8,128)S(1)} %get-tuple-element.70.dn, ...), custom_call_target="tpu_custom_call" | custom-call | tf_op jit(solution)/shard_map/image/pallas_call | solution.py:36
  58.9 14.1 %all_to_all.11 = f32[128,1,128]{2,1,0:T(1,128)S(1)} all-to-all(f32[128,1,128]{2,1,0:T(1,128)S(1)} %bitcast.17), channel_id=1, replica_groups=mesh['gx'=16,'gy'=8] {'gx','gy'}, dimensions={0} | all-to-all | bytes 131072 | tf_op jit(solution)/shard_map/all_to_all | solution.py:720
  73.1 1.2 %next.1 = (f32[640,128]{1,0:T(8,128)}, f32[5]{0:T(128)}) custom-call(f32[128,128]{1,0:T(8,128)S(1)} %bitcast.16, f32[640,128]{1,0:T(8,128)S(1)} %get-tuple-element.84.image, f32[4,640,128]{2,1,0:T(8,128)S(1)} %get-tuple-element.73.basis), custom_call_target="tpu_custom_call" | custom-call | tf_op jit(solution)/shard_map/next/pallas_call | solution.py:36
Async XLA Ops:
  2.1 5.6 %collective-permute-start = (bf16[160,128]{1,0:T(8,128)(2,1)S(1)}, bf16[160,128]{1,0:T(8,128)(2,1)S(1)}, u32[]{:S(2)}, u32[]{:S(2)}) collective-permute-start(bf16[160,128]{1,0:T(8,128)(2,1)S(1)} %get-tuple-element.52), channel_id=1, source_target_pairs={{0,1},{1,0},{2,3},{3,2},{4,5},{5,4},{6,7},{7,6},{8,9},{9,8},{10,11... | collective-permute-start | bytes 122888 | tf_op jit(solution)/shard_map/ppermute | solution.py:693
  3.6 4.1 %collective-permute-start.1 = (bf16[160,128]{1,0:T(8,128)(2,1)S(1)}, bf16[160,128]{1,0:T(8,128)(2,1)S(1)}, u32[]{:S(2)}, u32[]{:S(2)}) collective-permute-start(bf16[160,128]{1,0:T(8,128)(2,1)S(1)} %get-tuple-element.53), channel_id=1, source_target_pairs={{0,8},{1,2},{2,1},{3,4},{4,3},{5,6},{6,5},{7,15},{8,0},{9,10},{10,... | collective-permute-start | bytes 122888 | tf_op jit(solution)/shard_map/ppermute | solution.py:693
  7.8 8.6 %collective-permute-start.2 = (bf16[848,128]{1,0:T(8,128)(2,1)S(1)}, bf16[848,128]{1,0:T(8,128)(2,1)S(1)}, u32[]{:S(2)}, u32[]{:S(2)}) collective-permute-start(bf16[848,128]{1,0:T(8,128)(2,1)S(1)} %get-tuple-element.54.own), channel_id=1, source_target_pairs={{0,8},{1,9},{2,10},{3,11},{4,12},{5,13},{6,14},{7,15},{8,0},{9,1},... | collective-permute-start | bytes 651272 | tf_op jit(solution)/shard_map/ppermute | solution.py:693
  9.5 8.3 %collective-permute-start.3 = (bf16[848,128]{1,0:T(8,128)(2,1)S(1)}, bf16[848,128]{1,0:T(8,128)(2,1)S(1)}, u32[]{:S(2)}, u32[]{:S(2)}) collective-permute-start(bf16[848,128]{1,0:T(8,128)(2,1)S(1)} %get-tuple-element.57), channel_id=1, source_target_pairs={{0,1},{1,0},{2,3},{3,2},{4,5},{5,4},{6,7},{7,6},{8,16},{9,17},{10,... | collective-permute-start | bytes 651272 | tf_op jit(solution)/shard_map/ppermute | solution.py:693
  17.7 20.8 %copy-start = (f32[32,4096]{1,0:T(8,128)S(1)}, f32[32,4096]{1,0:T(8,128)}, u32[]{:S(2)}) copy-start(f32[32,4096]{1,0:T(8,128)} %inverse.1) | copy-start | bytes 1572868
  40.5 10.4 %collective-permute-start.5 = (bf16[880,128]{1,0:T(8,128)(2,1)S(1)}, bf16[880,128]{1,0:T(8,128)(2,1)S(1)}, u32[]{:S(2)}, u32[]{:S(2)}) collective-permute-start(bf16[880,128]{1,0:T(8,128)(2,1)S(1)} %get-tuple-element.64), channel_id=1, source_target_pairs={{0,1},{1,0},{2,3},{3,2},{4,5},{5,4},{6,7},{7,6},{8,16},{9,17},{10,... | collective-permute-start | bytes 675848 | tf_op jit(solution)/shard_map/ppermute | solution.py:693
  43.3 7.6 %collective-permute-start.4 = (bf16[880,128]{1,0:T(8,128)(2,1)S(1)}, bf16[880,128]{1,0:T(8,128)(2,1)S(1)}, u32[]{:S(2)}, u32[]{:S(2)}) collective-permute-start(bf16[880,128]{1,0:T(8,128)(2,1)S(1)} %get-tuple-element.63), channel_id=1, source_target_pairs={{0,8},{1,9},{2,10},{3,11},{4,12},{5,13},{6,14},{7,15},{8,0},{9,1},... | collective-permute-start | bytes 675848 | tf_op jit(solution)/shard_map/ppermute | solution.py:693
  43.6 7.3 %collective-permute-start.6 = (bf16[80,128]{1,0:T(8,128)(2,1)S(1)}, bf16[80,128]{1,0:T(8,128)(2,1)S(1)}, u32[]{:S(2)}, u32[]{:S(2)}) collective-permute-start(bf16[80,128]{1,0:T(8,128)(2,1)S(1)} %get-tuple-element.65), channel_id=1, source_target_pairs={{0,16},{1,17},{2,18},{3,19},{4,20},{5,21},{6,22},{7,23},{8,24},{9,... | collective-permute-start | bytes 61448 | tf_op jit(solution)/shard_map/ppermute | solution.py:693
  46.4 7.6 %copy-start.1 = (f32[4,8]{1,0:T(4,128)S(1)}, f32[4,8]{1,0:T(4,128)}, u32[]{:S(2)}) copy-start(f32[4,8]{1,0:T(4,128)} %table.1) | copy-start | bytes 388
  46.4 4.5 %collective-permute-start.7 = (bf16[80,128]{1,0:T(8,128)(2,1)S(1)}, bf16[80,128]{1,0:T(8,128)(2,1)S(1)}, u32[]{:S(2)}, u32[]{:S(2)}) collective-permute-start(bf16[80,128]{1,0:T(8,128)(2,1)S(1)} %get-tuple-element.66), channel_id=1, source_target_pairs={{0,1},{1,0},{2,3},{3,2},{4,5},{5,4},{6,7},{7,6},{8,9},{9,8},{10,11... | collective-permute-start | bytes 61448 | tf_op jit(solution)/shard_map/ppermute | solution.py:693
  51.2 4.0 %collective-permute-start.8 = (bf16[208,128]{1,0:T(8,128)(2,1)S(1)}, bf16[208,128]{1,0:T(8,128)(2,1)S(1)}, u32[]{:S(2)}, u32[]{:S(2)}) collective-permute-start(bf16[208,128]{1,0:T(8,128)(2,1)S(1)} %get-tuple-element.71), channel_id=1, source_target_pairs={{0,1},{1,0},{2,3},{3,2},{4,5},{5,4},{6,7},{7,6},{8,9},{9,8},{10,11... | collective-permute-start | bytes 159752 | tf_op jit(solution)/shard_map/ppermute | solution.py:693
  53.7 3.8 %collective-permute-start.9 = (bf16[208,128]{1,0:T(8,128)(2,1)S(1)}, bf16[208,128]{1,0:T(8,128)(2,1)S(1)}, u32[]{:S(2)}, u32[]{:S(2)}) collective-permute-start(bf16[208,128]{1,0:T(8,128)(2,1)S(1)} %get-tuple-element.72), channel_id=1, source_target_pairs={{0,8},{1,2},{2,1},{3,4},{4,3},{5,6},{6,5},{7,15},{8,0},{9,10},{10,... | collective-permute-start | bytes 159752 | tf_op jit(solution)/shard_map/ppermute | solution.py:693

commit v3 on v2

--- a/solution.py
+++ b/solution.py
@@ -15,8 +15,8 @@
 RUNS = CELLS // 4
 FLAT = 5 * RUNS
 WINDOW = 7680
-EARLY = 12
-CHUNK = 14
+EARLY = 8
+CHUNK = 16
 PAD = FLAT + 48
 SIDE = RUNS + 48
 ENDS = FLAT + 80
@@ -372,24 +372,24 @@
     return jnp.where(upper, bottom, top)
 
 
-def second_spread_kernel(
+def first_spread_kernel(
     early, late, inverse, gathered, count, local, weights, message, near, far, rhs, whole, ends
 ):
     solved = solve(inverse, gathered, count, rhs)
     weights[...] = solved
-    upper = lax.axis_index("gx") % 2 == 1
+    upper = lax.axis_index("gx") % 2 == 0
     far[...] = spread_to(upper, early, late, solved, local, message, near, whole, ends)
 
 
-def first_spread_kernel(
+def second_spread_kernel(
     early, late, weights, local, far, message, near, far_first, far_second, whole, ends
 ):
     place = lax.axis_index("gx")
-    upper = place % 2 == 0
+    upper = place % 2 == 1
     own = spread_to(upper, early, late, weights[...], local, message, near, whole, ends)
     swapped = (place % 4 == 1) | (place % 4 == 2)
-    far_first[...] = jnp.where(swapped, far[...], own).astype(BF16)
-    far_second[...] = jnp.where(swapped, own, far[...]).astype(BF16)
+    far_first[...] = jnp.where(swapped, own, far[...]).astype(BF16)
+    far_second[...] = jnp.where(swapped, far[...], own).astype(BF16)
 
 
 def own_spread_kernel(early, late, weights, own):
@@ -405,8 +405,8 @@
     local,
     from_first,
     from_second,
+    far_second,
     far_first,
-    far_second,
     field,
     rim,
     up,
@@ -622,10 +622,8 @@
         own = precond[cut, :]
         aside = side[cut, :]
         result = total[cut, :] * own
-        result = result - faces[0, cut, :] * jnp.where(at == 0, turn(aside, 1), turn(own, 1))
-        result = result - faces[1, cut, :] * jnp.where(
-            at == COLS - 1, turn(aside, -1), turn(own, -1)
-        )
+        result = result - faces[0, cut, :] * turn(jnp.where(at == COLS - 1, aside, own), 1)
+        result = result - faces[1, cut, :] * turn(jnp.where(at == 0, aside, own), -1)
         result = result - faces[2, cut, :] * jnp.where(
             row == 0, over[level : level + 1, :], pltpu.roll(own, 1, 0)
         )
@@ -694,10 +692,8 @@
 
 
 def swap_y(first, second):
-    return (
-        swap(first, lambda a, b: (a, b ^ 1)),
-        swap(second, lambda a, b: (a, ((b + 1) ^ 1) - 1)),
-    )
+    from_second = swap(second, lambda a, b: (a, ((b + 1) ^ 1) - 1))
+    return swap(first, lambda a, b: (a, b ^ 1)), from_second
 
 
 def swap_x_first(values):
@@ -709,10 +705,8 @@
 
 
 def swap_far(first, second):
-    return (
-        swap(first, lambda a, b: (a ^ 2, b)),
-        swap(second, lambda a, b: (((a + 2) ^ 2) - 2, b)),
-    )
+    from_second = swap(second, lambda a, b: (((a + 2) ^ 2) - 2, b))
+    return swap(first, lambda a, b: (a ^ 2, b)), from_second
 
 
 def exchange(lines):
@@ -812,28 +806,28 @@
     gathered = exchange(lines)
     message = shape(ENDS, COLS, dtype=BF16)
     ends = pltpu.VMEM((2 * LAYERS, COLS), F32)
-    weights, second, near_second, far = call(
-        second_spread_kernel,
+    weights, first, near_first, far = call(
+        first_spread_kernel,
         [shape(K, COLS), message, shape(80, COLS), shape(80, COLS)],
         [VM] * 6,
         (early, late, coarse_inverse, gathered, active_count, local),
         [pltpu.VMEM((K, COLS), F32), vector, ends],
         flops=20_000_000,
         moved=8_000_000,
-        name="second_spread",
-    )
-    from_second = swap_x_second(second)
-    first, near_first, far_first, far_second = call(
-        first_spread_kernel,
+        name="first_spread",
+    )
+    from_first = swap_x_first(first)
+    second, near_second, far_first, far_second = call(
+        second_spread_kernel,
         [message, shape(80, COLS)] + [shape(80, COLS, dtype=BF16)] * 2,
         [VM] * 5,
         (early, late, weights, local, far),
         [vector, ends],
         flops=20_000_000,
         moved=8_000_000,
-        name="first_spread",
-    )
-    near = swap_x_first(first), from_second
+        name="second_spread",
+    )
+    near = from_first, swap_x_second(second)
     far = swap_far(far_first, far_second)
     own = call(
         own_spread_kernel,
@@ -861,7 +855,7 @@
         + [shape(RUNS + LAYERS, COLS)] * 2
         + [shape(SIDE, COLS, dtype=BF16)] * 2,
         [VM] * 8,
-        (own, near_first, near_second, local, *near, *far),
+        (own, near_first, near_second, local, *near, far[1], far[0]),
         name="fold_rows",
     )
     from_y = swap_y(first, second)

time: 74.5 us -> 73.6 us (0.988)
  waiting for transfers between devices: 3.48 us -> 2.51 us
    ppermute x10, waiting for transfers between devices: 3.48 us -> 2.51 us  [swap(): return lax.ppermute(values, ('gx', 'gy'), pairs)]
where the time goes in v3:
time: 73.6 us; the launch traced here: 73.4 us
  blocking collectives  33.5 us (46%)
  Pallas kernels  22.6 us (31%)
  starting transfers between devices  13.3 us (18%)
  waiting for transfers between devices  2.51 us (3%)
  between operations  1.43 us (2%)
    all_to_all x2, blocking collectives, exchange(): out = lax.all_to_all(lines.reshape(size, 1, COLS), ('gx', 'gy'), 0, 0)  33.5 us
    pallas_call x13, Pallas kernels, call(): pl.pallas_call(kernel, out_shape=outs, in_specs=specs, out_specs=out_spec...  22.6 us
    ppermute x10, starting transfers between devices, swap(): return lax.ppermute(values, ('gx', 'gy'), pairs)  13.3 us
    ppermute x10, waiting for transfers between devices, swap(): return lax.ppermute(values, ('gx', 'gy'), pairs)  2.51 us
  transfers between devices with their start and end apart: 10, of which 2 were waited for; matrix products, arithmetic and copies ran while one was open for 0% of the time, Pallas kernels for 20%

profile of v3, /device:TPU:1, one launch (start us, length us, event | category | flops | bytes accessed | tf_op | source)
XLA Modules:
  0.0 73.4 jit_solution(9611601552656270229)
XLA Ops:
  0.6 1.5 %pack.1 = (bf16[160,128]{1,0:T(8,128)(2,1)S(1)}, bf16[160,128]{1,0:T(8,128)(2,1)S(1)}, bf16[800,128]{1,0:T(8,128)(2,1)S(1)}, f32[2,48,128]{2,1,0:T(8,128)S(1)}, ...) custom-call(f32[4,640,128]{2,1,0:T(8,128)} %bitcast.20, s32[640,128]{1,0:T(8,128)} %bitcast.22, s32[640,128]{1,0:T(8,128)} %bitcast.23), custom_call_target="tpu_custom_call" | custom-call | tf_op jit(solution)/shard_map/pack/pallas_call | solution.py:36
  2.1 1.5 %collective-permute-start = (bf16[160,128]{1,0:T(8,128)(2,1)S(1)}, bf16[160,128]{1,0:T(8,128)(2,1)S(1)}, u32[]{:S(2)}, u32[]{:S(2)}) collective-permute-start(bf16[160,128]{1,0:T(8,128)(2,1)S(1)} %get-tuple-element.52), channel_id=1, source_target_pairs={{0,1},{1,0},{2,3},{3,2},{4,5},{5,4},{6,7},{7,6},{8,9},{9,8},{10,11... | collective-permute-start | bytes 122888 | tf_op jit(solution)/shard_map/ppermute | solution.py:691
  3.6 1.4 %collective-permute-start.1 = (bf16[160,128]{1,0:T(8,128)(2,1)S(1)}, bf16[160,128]{1,0:T(8,128)(2,1)S(1)}, u32[]{:S(2)}, u32[]{:S(2)}) collective-permute-start(bf16[160,128]{1,0:T(8,128)(2,1)S(1)} %get-tuple-element.53), channel_id=1, source_target_pairs={{0,8},{1,2},{2,1},{3,4},{4,3},{5,6},{6,5},{7,15},{8,0},{9,10},{10,... | collective-permute-start | bytes 122888 | tf_op jit(solution)/shard_map/ppermute | solution.py:691
  5.0 2.1 %early.1 = (bf16[32,61440]{1,0:T(8,128)(2,1)S(1)}, f32[640,128]{1,0:T(8,128)S(1)}, f32[640,128]{1,0:T(8,128)S(1)}, f32[640,128]{1,0:T(8,128)S(1)}, f32[640,128]{1,0:T(8,128)S(1)}) custom-call(bf16[32,307200]{1,0:T(8,128)(2,1)} %bitcast.18, f32[4,8]{1,0:T(4,128)} %table.1, f32[640,128]{1,0:T(8,128)S(1)} %get-tuple-element.45.basis, ...), custom_call_target="tpu_custom_call" | custom-call | bytes 10000000 | tf_op jit(solution)/shard_map/early/pallas_call | solution.py:36
  7.1 0.0 collective-permute-done.from_first.first_y
  7.1 0.2 collective-permute-done.1.from_second.second_y
  7.3 0.1 flat.1
  7.4 1.8 %collective-permute-start.2 = (bf16[848,128]{1,0:T(8,128)(2,1)S(1)}, bf16[848,128]{1,0:T(8,128)(2,1)S(1)}, u32[]{:S(2)}, u32[]{:S(2)}) collective-permute-start(bf16[848,128]{1,0:T(8,128)(2,1)S(1)} %get-tuple-element.54.own), channel_id=1, source_target_pairs={{0,8},{1,9},{2,10},{3,11},{4,12},{5,13},{6,14},{7,15},{8,0},{9,1},... | collective-permute-start | bytes 651272 | tf_op jit(solution)/shard_map/ppermute | solution.py:691
  9.2 0.7 collective-permute-start.3
  10.5 6.5 %load.1 = (bf16[32,245760]{1,0:T(8,128)(2,1)S(1)}, f32[4,640,128]{2,1,0:T(8,128)S(1)}, f32[32,128]{1,0:T(8,128)S(1)}, f32[80,128]{1,0:T(8,128)S(1)}) custom-call(bf16[32,307200]{1,0:T(8,128)(2,1)} %bitcast.19, f32[4,640,128]{2,1,0:T(8,128)} %bitcast.21, bf16[32,61440]{1,0:T(8,128)(2,1)S(1)} %get-tuple-element.49.early, ...), custom_call_target="tpu_custom_call" | custom-call | flops 16000000 | bytes 20000000 | tf_op jit(solution)/shard_map/load/pallas_call | solution.py:36
  17.0 0.0 collective-permute-done.2.whole.first_x
  17.0 1.4 %first_rhs.1.begun = f32[32,128]{1,0:T(8,128)S(1)} custom-call(bf16[32,61440]{1,0:T(8,128)(2,1)S(1)} %get-tuple-element.49.early, bf16[32,245760]{1,0:T(8,128)(2,1)S(1)} %get-tuple-element.55.late, f32[32,128]{1,0:T(8,128)S(1)} %get-tuple-element.56.begun, bf16[848,128]{1,0:T(8,128)(2,1)S(1)} %collective-permute-done.2.whole.first_x), custom_call_target="tpu_custom_call" | custom-call | flops 6000000 | bytes 6000000 | tf_op jit(solution)/shard_map/first_rhs/pallas_call | solution.py:36
  18.4 0.0 copy-start
  18.4 0.0 collective-permute-done.3.whole.second_x
  18.4 1.5 %second_rhs.1 = f32[128,128]{1,0:T(8,128)S(1)} custom-call(bf16[32,61440]{1,0:T(8,128)(2,1)S(1)} %get-tuple-element.49.early, bf16[32,245760]{1,0:T(8,128)(2,1)S(1)} %get-tuple-element.55.late, f32[32,128]{1,0:T(8,128)S(1)} %first_rhs.1.begun, bf16[848,128]{1,0:T(8,128)(2,1)S(1)} %collective-permute-done.3.whole.second_x, s32[1,1]{1,0:T(1,128)S(6)} %copy.12.count), custom_call_target="tpu_custom_call" | custom-call | flops 6000000 | bytes 6000000 | tf_op jit(solution)/shard_map/second_rhs/pallas_call | solution.py:36
  20.0 18.6 %all_to_all.10 = f32[128,1,128]{2,1,0:T(1,128)S(1)} all-to-all(f32[128,1,128]{2,1,0:T(1,128)S(1)} %bitcast.15), channel_id=1, replica_groups=mesh['gx'=16,'gy'=8] {'gx','gy'}, dimensions={0} | all-to-all | bytes 131072 | tf_op jit(solution)/shard_map/all_to_all | solution.py:714
  38.5 0.0 copy-done
  38.5 2.0 %first_spread.1 = (f32[32,128]{1,0:T(8,128)S(1)}, bf16[880,128]{1,0:T(8,128)(2,1)S(1)}, f32[80,128]{1,0:T(8,128)S(1)}, f32[80,128]{1,0:T(8,128)S(1)}) custom-call(bf16[32,61440]{1,0:T(8,128)(2,1)S(1)} %get-tuple-element.49.early, bf16[32,245760]{1,0:T(8,128)(2,1)S(1)} %get-tuple-element.55.late, f32[32,4096]{1,0:T(8,128)S(1)} %copy-done, ...), custom_call_target="tpu_custom_call" | custom-call | flops 20000000 | bytes 8000000 | tf_op jit(solution)/shard_map/first_spread/pallas_call | solution.py:36
  40.5 0.5 collective-permute-start.4
  41.0 1.9 %second_spread.1 = (bf16[880,128]{1,0:T(8,128)(2,1)S(1)}, f32[80,128]{1,0:T(8,128)S(1)}, bf16[80,128]{1,0:T(8,128)(2,1)S(1)}, bf16[80,128]{1,0:T(8,128)(2,1)S(1)}) custom-call(bf16[32,61440]{1,0:T(8,128)(2,1)S(1)} %get-tuple-element.49.early, bf16[32,245760]{1,0:T(8,128)(2,1)S(1)} %get-tuple-element.55.late, f32[32,128]{1,0:T(8,128)S(1)} %get-tuple-element.59.weights, ...), custom_call_target="tpu_custom_call" | custom-call | flops 20000000 | bytes 8000000 | tf_op jit(solution)/shard_map/second_spread/pallas_call | solution.py:36
  42.9 1.4 %collective-permute-start.5 = (bf16[880,128]{1,0:T(8,128)(2,1)S(1)}, bf16[880,128]{1,0:T(8,128)(2,1)S(1)}, u32[]{:S(2)}, u32[]{:S(2)}) collective-permute-start(bf16[880,128]{1,0:T(8,128)(2,1)S(1)} %get-tuple-element.64), channel_id=1, source_target_pairs={{0,1},{1,0},{2,3},{3,2},{4,5},{5,4},{6,7},{7,6},{8,16},{9,17},{10,... | collective-permute-start | bytes 675848 | tf_op jit(solution)/shard_map/ppermute | solution.py:691
  44.3 0.1 collective-permute-start.6
  44.4 0.0 copy-start.1
  44.4 3.8 %collective-permute-start.7 = (bf16[80,128]{1,0:T(8,128)(2,1)S(1)}, bf16[80,128]{1,0:T(8,128)(2,1)S(1)}, u32[]{:S(2)}, u32[]{:S(2)}) collective-permute-start(bf16[80,128]{1,0:T(8,128)(2,1)S(1)} %get-tuple-element.66), channel_id=1, source_target_pairs={{0,16},{1,17},{2,18},{3,19},{4,20},{5,21},{6,22},{7,23},{8,24},{9,... | collective-permute-start | bytes 61448 | tf_op jit(solution)/shard_map/ppermute | solution.py:691
  48.2 1.7 %own_spread.1.own = f32[800,128]{1,0:T(8,128)S(1)} custom-call(bf16[32,61440]{1,0:T(8,128)(2,1)S(1)} %get-tuple-element.49.early, bf16[32,245760]{1,0:T(8,128)(2,1)S(1)} %get-tuple-element.55.late, f32[32,128]{1,0:T(8,128)S(1)} %get-tuple-element.59.weights), custom_call_target="tpu_custom_call" | custom-call | flops 20000000 | bytes 7000000 | tf_op jit(solution)/shard_map/own_spread/pallas_call | solution.py:36
  49.8 0.0 collective-permute-done.6.far_second
  49.8 0.0 collective-permute-done.7.far_first
  49.9 0.0 collective-permute-done.4.from_first
  49.9 0.0 collective-permute-done.5.from_second
  49.9 0.3 fold_rows.1
  50.2 1.9 %collective-permute-start.8 = (bf16[208,128]{1,0:T(8,128)(2,1)S(1)}, bf16[208,128]{1,0:T(8,128)(2,1)S(1)}, u32[]{:S(2)}, u32[]{:S(2)}) collective-permute-start(bf16[208,128]{1,0:T(8,128)(2,1)S(1)} %get-tuple-element.71), channel_id=1, source_target_pairs={{0,1},{1,0},{2,3},{3,2},{4,5},{5,4},{6,7},{7,6},{8,9},{9,8},{10,11... | collective-permute-start | bytes 159752 | tf_op jit(solution)/shard_map/ppermute | solution.py:691
  52.1 0.3 collective-permute-start.9
  52.4 0.0 copy-done.1
  52.4 1.2 %faces.1 = (f32[4,640,128]{2,1,0:T(8,128)S(1)}, f32[640,128]{1,0:T(8,128)S(1)}) custom-call(f32[640,128]{1,0:T(8,128)S(1)} %get-tuple-element.76.conduct, f32[640,128]{1,0:T(8,128)S(1)} %get-tuple-element.77.diagonal, f32[4,8]{1,0:T(4,128)S(1)} %copy-done.1, bf16[160,128]{1,0:T(8,128)(2,1)S(1)} %collective-permute-done.from_first.first_y, ...), custom_call_target="tpu_custom_call" | custom-call | flops 4000000 | bytes 2000000 | tf_op jit(solution)/shard_map/faces/pallas_call | solution.py:36
  53.6 0.0 collective-permute-done.8.from_first
  53.6 2.3 %collective-permute-done.9.from_second = bf16[208,128]{1,0:T(8,128)(2,1)S(1)} collective-permute-done((bf16[208,128]{1,0:T(8,128)(2,1)S(1)}, bf16[208,128]{1,0:T(8,128)(2,1)S(1)}, u32[]{:S(2)}, u32[]{:S(2)}) %collective-permute-start.9) | collective-permute-done | bytes 53280 | tf_op jit(solution)/shard_map/ppermute | solution.py:691
  55.9 1.4 %image.1 = (f32[640,128]{1,0:T(8,128)}, f32[640,128]{1,0:T(8,128)S(1)}, f32[128,128]{1,0:T(8,128)S(1)}) custom-call(f32[640,128]{1,0:T(8,128)S(1)} %get-tuple-element.67.field, f32[80,128]{1,0:T(8,128)S(1)} %get-tuple-element.68.rim, f32[200,128]{1,0:T(8,128)S(1)} %get-tuple-element.69.up, f32[200,128]{1,0:T(8,128)S(1)} %get-tuple-element.70.dn, ...), custom_call_target="tpu_custom_call" | custom-call | tf_op jit(solution)/shard_map/image/pallas_call | solution.py:36
  57.2 15.0 %all_to_all.11 = f32[128,1,128]{2,1,0:T(1,128)S(1)} all-to-all(f32[128,1,128]{2,1,0:T(1,128)S(1)} %bitcast.17), channel_id=1, replica_groups=mesh['gx'=16,'gy'=8] {'gx','gy'}, dimensions={0} | all-to-all | bytes 131072 | tf_op jit(solution)/shard_map/all_to_all | solution.py:714
  72.2 1.2 %next.1 = (f32[640,128]{1,0:T(8,128)}, f32[5]{0:T(128)}) custom-call(f32[128,128]{1,0:T(8,128)S(1)} %bitcast.16, f32[640,128]{1,0:T(8,128)S(1)} %get-tuple-element.84.image, f32[4,640,128]{2,1,0:T(8,128)S(1)} %get-tuple-element.73.basis), custom_call_target="tpu_custom_call" | custom-call | tf_op jit(solution)/shard_map/next/pallas_call | solution.py:36
Async XLA Ops:
  2.1 5.0 %collective-permute-start = (bf16[160,128]{1,0:T(8,128)(2,1)S(1)}, bf16[160,128]{1,0:T(8,128)(2,1)S(1)}, u32[]{:S(2)}, u32[]{:S(2)}) collective-permute-start(bf16[160,128]{1,0:T(8,128)(2,1)S(1)} %get-tuple-element.52), channel_id=1, source_target_pairs={{0,1},{1,0},{2,3},{3,2},{4,5},{5,4},{6,7},{7,6},{8,9},{9,8},{10,11... | collective-permute-start | bytes 122888 | tf_op jit(solution)/shard_map/ppermute | solution.py:691
  3.6 3.7 %collective-permute-start.1 = (bf16[160,128]{1,0:T(8,128)(2,1)S(1)}, bf16[160,128]{1,0:T(8,128)(2,1)S(1)}, u32[]{:S(2)}, u32[]{:S(2)}) collective-permute-start(bf16[160,128]{1,0:T(8,128)(2,1)S(1)} %get-tuple-element.53), channel_id=1, source_target_pairs={{0,8},{1,2},{2,1},{3,4},{4,3},{5,6},{6,5},{7,15},{8,0},{9,10},{10,... | collective-permute-start | bytes 122888 | tf_op jit(solution)/shard_map/ppermute | solution.py:691
  7.4 9.6 %collective-permute-start.2 = (bf16[848,128]{1,0:T(8,128)(2,1)S(1)}, bf16[848,128]{1,0:T(8,128)(2,1)S(1)}, u32[]{:S(2)}, u32[]{:S(2)}) collective-permute-start(bf16[848,128]{1,0:T(8,128)(2,1)S(1)} %get-tuple-element.54.own), channel_id=1, source_target_pairs={{0,8},{1,9},{2,10},{3,11},{4,12},{5,13},{6,14},{7,15},{8,0},{9,1},... | collective-permute-start | bytes 651272 | tf_op jit(solution)/shard_map/ppermute | solution.py:691
  9.2 9.2 %collective-permute-start.3 = (bf16[848,128]{1,0:T(8,128)(2,1)S(1)}, bf16[848,128]{1,0:T(8,128)(2,1)S(1)}, u32[]{:S(2)}, u32[]{:S(2)}) collective-permute-start(bf16[848,128]{1,0:T(8,128)(2,1)S(1)} %get-tuple-element.57), channel_id=1, source_target_pairs={{0,1},{1,0},{2,3},{3,2},{4,5},{5,4},{6,7},{7,6},{8,16},{9,17},{10,... | collective-permute-start | bytes 651272 | tf_op jit(solution)/shard_map/ppermute | solution.py:691
  18.4 20.1 %copy-start = (f32[32,4096]{1,0:T(8,128)S(1)}, f32[32,4096]{1,0:T(8,128)}, u32[]{:S(2)}) copy-start(f32[32,4096]{1,0:T(8,128)} %inverse.1) | copy-start | bytes 1572868
  40.5 9.3 %collective-permute-start.4 = (bf16[880,128]{1,0:T(8,128)(2,1)S(1)}, bf16[880,128]{1,0:T(8,128)(2,1)S(1)}, u32[]{:S(2)}, u32[]{:S(2)}) collective-permute-start(bf16[880,128]{1,0:T(8,128)(2,1)S(1)} %get-tuple-element.63), channel_id=1, source_target_pairs={{0,8},{1,9},{2,10},{3,11},{4,12},{5,13},{6,14},{7,15},{8,0},{9,1},... | collective-permute-start | bytes 675848 | tf_op jit(solution)/shard_map/ppermute | solution.py:691
  42.9 7.0 %collective-permute-start.5 = (bf16[880,128]{1,0:T(8,128)(2,1)S(1)}, bf16[880,128]{1,0:T(8,128)(2,1)S(1)}, u32[]{:S(2)}, u32[]{:S(2)}) collective-permute-start(bf16[880,128]{1,0:T(8,128)(2,1)S(1)} %get-tuple-element.64), channel_id=1, source_target_pairs={{0,1},{1,0},{2,3},{3,2},{4,5},{5,4},{6,7},{7,6},{8,16},{9,17},{10,... | collective-permute-start | bytes 675848 | tf_op jit(solution)/shard_map/ppermute | solution.py:691
  44.3 5.5 %collective-permute-start.6 = (bf16[80,128]{1,0:T(8,128)(2,1)S(1)}, bf16[80,128]{1,0:T(8,128)(2,1)S(1)}, u32[]{:S(2)}, u32[]{:S(2)}) collective-permute-start(bf16[80,128]{1,0:T(8,128)(2,1)S(1)} %get-tuple-element.65), channel_id=1, source_target_pairs={{0,1},{1,0},{2,3},{3,2},{4,5},{5,4},{6,7},{7,6},{8,9},{9,8},{10,11... | collective-permute-start | bytes 61448 | tf_op jit(solution)/shard_map/ppermute | solution.py:691
  44.4 8.0 %copy-start.1 = (f32[4,8]{1,0:T(4,128)S(1)}, f32[4,8]{1,0:T(4,128)}, u32[]{:S(2)}) copy-start(f32[4,8]{1,0:T(4,128)} %table.1) | copy-start | bytes 388
  44.4 5.5 %collective-permute-start.7 = (bf16[80,128]{1,0:T(8,128)(2,1)S(1)}, bf16[80,128]{1,0:T(8,128)(2,1)S(1)}, u32[]{:S(2)}, u32[]{:S(2)}) collective-permute-start(bf16[80,128]{1,0:T(8,128)(2,1)S(1)} %get-tuple-element.66), channel_id=1, source_target_pairs={{0,16},{1,17},{2,18},{3,19},{4,20},{5,21},{6,22},{7,23},{8,24},{9,... | collective-permute-start | bytes 61448 | tf_op jit(solution)/shard_map/ppermute | solution.py:691
  50.2 3.4 %collective-permute-start.8 = (bf16[208,128]{1,0:T(8,128)(2,1)S(1)}, bf16[208,128]{1,0:T(8,128)(2,1)S(1)}, u32[]{:S(2)}, u32[]{:S(2)}) collective-permute-start(bf16[208,128]{1,0:T(8,128)(2,1)S(1)} %get-tuple-element.71), channel_id=1, source_target_pairs={{0,1},{1,0},{2,3},{3,2},{4,5},{5,4},{6,7},{7,6},{8,9},{9,8},{10,11... | collective-permute-start | bytes 159752 | tf_op jit(solution)/shard_map/ppermute | solution.py:691
  52.1 3.8 %collective-permute-start.9 = (bf16[208,128]{1,0:T(8,128)(2,1)S(1)}, bf16[208,128]{1,0:T(8,128)(2,1)S(1)}, u32[]{:S(2)}, u32[]{:S(2)}) collective-permute-start(bf16[208,128]{1,0:T(8,128)(2,1)S(1)} %get-tuple-element.72), channel_id=1, source_target_pairs={{0,8},{1,2},{2,1},{3,4},{4,3},{5,6},{6,5},{7,15},{8,0},{9,10},{10,... | collective-permute-start | bytes 159752 | tf_op jit(solution)/shard_map/ppermute | solution.py:691

commit v4 on v3

--- a/solution.py
+++ b/solution.py
@@ -54,7 +54,7 @@
 
 
 def steps(count):
-    return max(n for n in range(1, 8) if count % n == 0)
+    return max(n for n in range(1, 9) if count % n == 0)
 
 
 def turn(values, amount):
@@ -202,9 +202,7 @@
         gram[8 * slot : 8 * slot + 8, :] = grams[slot]
 
 
-def load_kernel(source, basis_in, early, own, late, basis, begun, gram, vector, arrived):
-    ready = pltpu.make_async_copy(basis_in, basis, arrived.at[0])
-    ready.start()
+def load_kernel(source, early, own, late, begun, vector, arrived):
     copies = []
     for index in range((LAYERS - EARLY) // CHUNK):
         begin, size = index * CHUNK * WINDOW, CHUNK * WINDOW
@@ -212,7 +210,7 @@
             pltpu.make_async_copy(
                 source.at[:, EARLY * WINDOW + begin : EARLY * WINDOW + begin + size],
                 late.at[:, begin : begin + size],
-                arrived.at[index + 1],
+                arrived.at[index],
             )
         )
     for copy in copies:
@@ -220,8 +218,6 @@
     vector[...] = own[:FLAT, :].astype(F32)
     totals = (jnp.zeros((8, COLS), F32),) * 8
     totals = project_part(early, vector, 1, totals, 0, 0, EARLY)
-    ready.wait()
-    multiply_out(basis, gram)
     for index, copy in enumerate(copies):
         copy.wait()
         totals = project_part(late, vector, 1, totals, EARLY, index * CHUNK, CHUNK)
@@ -392,10 +388,14 @@
     far_second[...] = jnp.where(swapped, far[...], own).astype(BF16)
 
 
-def own_spread_kernel(early, late, weights, own):
+def own_spread_kernel(early, late, weights, basis_in, own, basis, gram, ready):
+    copy = pltpu.make_async_copy(basis_in, basis, ready)
+    copy.start()
     wide = widen(weights[...])
     spread_part(early, wide, 1, own, 0, EARLY)
     spread_part(late, wide, 1, own, EARLY, LAYERS - EARLY)
+    copy.wait()
+    multiply_out(basis, gram)
 
 
 def fold_rows_kernel(
@@ -471,13 +471,13 @@
 
 def solve_columns(basis, code, table, conduct, diagonal, above, local, ratio, value):
     def body(index, carry):
-        cut = pl.ds(pl.multiple_of(index * 64, 64), 64)
+        cut = pl.ds(pl.multiple_of(index * 160, 160), 160)
         kind = code[cut, :]
         conduct[cut, :] = look_up(kind, table, (0, 1))
         diagonal[cut, :] = look_up(kind, table, (2, 3))
         return carry
 
-    lax.fori_loop(0, CELLS // 64, body, 0)
+    lax.fori_loop(0, CELLS // 160, body, 0)
     zero = jnp.zeros((ROWS, COLS), F32)
     below = zero
     last_ratio = zero
@@ -763,21 +763,19 @@
     )
     from_second = swap_x_second(second)
     from_x = swap_x_first(flat), from_second
-    late, basis, begun, gram = call(
+    late, begun = call(
         load_kernel,
         [
             pltpu.VMEM((K, (LAYERS - EARLY) * WINDOW), BF16),
-            pltpu.VMEM((4, CELLS, COLS), F32),
             shape(K, COLS),
-            shape(80, COLS),
         ],
-        [HB, HB, VM, VM],
-        (source, basis, early, flat),
+        [HB, VM, VM],
+        (source, early, flat),
         [
             pltpu.VMEM((FLAT, COLS), F32),
-            pltpu.SemaphoreType.DMA(((LAYERS - EARLY) // CHUNK + 1,)),
+            pltpu.SemaphoreType.DMA(((LAYERS - EARLY) // CHUNK,)),
         ],
-        out_specs=[VM] * 4,
+        out_specs=[VM] * 2,
         flops=16_000_000,
         moved=20_000_000,
         name="load",
@@ -829,11 +827,13 @@
     )
     near = from_first, swap_x_second(second)
     far = swap_far(far_first, far_second)
-    own = call(
+    own, basis, gram = call(
         own_spread_kernel,
-        shape(FLAT, COLS),
-        [VM] * 3,
-        (early, late, weights),
+        [shape(FLAT, COLS), pltpu.VMEM((4, CELLS, COLS), F32), shape(80, COLS)],
+        [VM] * 3 + [HB],
+        (early, late, weights, basis),
+        [pltpu.SemaphoreType.DMA],
+        out_specs=[VM] * 3,
         flops=20_000_000,
         moved=7_000_000,
         name="own_spread",

time: 73.6 us -> 73 us (level)
  no operation moved by 1% of the time
where the time goes in v4:
time: 73 us; the launch traced here: 72.8 us
  blocking collectives  33.4 us (46%)
  Pallas kernels  22.2 us (30%)
  starting transfers between devices  13.2 us (18%)
  waiting for transfers between devices  2.51 us (3%)
  between operations  1.43 us (2%)
    all_to_all x2, blocking collectives, exchange(): out = lax.all_to_all(lines.reshape(size, 1, COLS), ('gx', 'gy'), 0, 0)  33.4 us
    pallas_call x13, Pallas kernels, call(): pl.pallas_call(kernel, out_shape=outs, in_specs=specs, out_specs=out_spec...  22.2 us
    ppermute x10, starting transfers between devices, swap(): return lax.ppermute(values, ('gx', 'gy'), pairs)  13.2 us
    ppermute x10, waiting for transfers between devices, swap(): return lax.ppermute(values, ('gx', 'gy'), pairs)  2.51 us
  transfers between devices with their start and end apart: 10, of which 2 were waited for; matrix products, arithmetic and copies ran while one was open for 0% of the time, Pallas kernels for 20%

profile of v4, /device:TPU:1, one launch (start us, length us, event | category | flops | bytes accessed | tf_op | source)
XLA Modules:
  0.0 72.8 jit_solution(5673582256637390190)
XLA Ops:
  0.6 1.5 %pack.1 = (bf16[160,128]{1,0:T(8,128)(2,1)S(1)}, bf16[160,128]{1,0:T(8,128)(2,1)S(1)}, bf16[800,128]{1,0:T(8,128)(2,1)S(1)}, f32[2,48,128]{2,1,0:T(8,128)S(1)}, ...) custom-call(f32[4,640,128]{2,1,0:T(8,128)} %bitcast.20, s32[640,128]{1,0:T(8,128)} %bitcast.22, s32[640,128]{1,0:T(8,128)} %bitcast.23), custom_call_target="tpu_custom_call" | custom-call | tf_op jit(solution)/shard_map/pack/pallas_call | solution.py:36
  2.1 1.5 %collective-permute-start = (bf16[160,128]{1,0:T(8,128)(2,1)S(1)}, bf16[160,128]{1,0:T(8,128)(2,1)S(1)}, u32[]{:S(2)}, u32[]{:S(2)}) collective-permute-start(bf16[160,128]{1,0:T(8,128)(2,1)S(1)} %get-tuple-element.53), channel_id=1, source_target_pairs={{0,1},{1,0},{2,3},{3,2},{4,5},{5,4},{6,7},{7,6},{8,9},{9,8},{10,11... | collective-permute-start | bytes 122888 | tf_op jit(solution)/shard_map/ppermute | solution.py:691
  3.6 1.4 %collective-permute-start.1 = (bf16[160,128]{1,0:T(8,128)(2,1)S(1)}, bf16[160,128]{1,0:T(8,128)(2,1)S(1)}, u32[]{:S(2)}, u32[]{:S(2)}) collective-permute-start(bf16[160,128]{1,0:T(8,128)(2,1)S(1)} %get-tuple-element.54), channel_id=1, source_target_pairs={{0,8},{1,2},{2,1},{3,4},{4,3},{5,6},{6,5},{7,15},{8,0},{9,10},{10,... | collective-permute-start | bytes 122888 | tf_op jit(solution)/shard_map/ppermute | solution.py:691
  5.0 2.1 %early.1 = (bf16[32,61440]{1,0:T(8,128)(2,1)S(1)}, f32[640,128]{1,0:T(8,128)S(1)}, f32[640,128]{1,0:T(8,128)S(1)}, f32[640,128]{1,0:T(8,128)S(1)}, f32[640,128]{1,0:T(8,128)S(1)}) custom-call(bf16[32,307200]{1,0:T(8,128)(2,1)} %bitcast.18, f32[4,8]{1,0:T(4,128)} %table.1, f32[640,128]{1,0:T(8,128)S(1)} %get-tuple-element.46.basis, ...), custom_call_target="tpu_custom_call" | custom-call | bytes 10000000 | tf_op jit(solution)/shard_map/early/pallas_call | solution.py:36
  7.1 0.0 collective-permute-done.from_first.first_y
  7.1 0.2 collective-permute-done.1.from_second.second_y
  7.3 0.1 flat.1
  7.4 1.8 %collective-permute-start.2 = (bf16[848,128]{1,0:T(8,128)(2,1)S(1)}, bf16[848,128]{1,0:T(8,128)(2,1)S(1)}, u32[]{:S(2)}, u32[]{:S(2)}) collective-permute-start(bf16[848,128]{1,0:T(8,128)(2,1)S(1)} %get-tuple-element.55.own), channel_id=1, source_target_pairs={{0,8},{1,9},{2,10},{3,11},{4,12},{5,13},{6,14},{7,15},{8,0},{9,1},... | collective-permute-start | bytes 651272 | tf_op jit(solution)/shard_map/ppermute | solution.py:691
  9.2 0.7 collective-permute-start.3
  10.5 6.0 %load.1 = (bf16[32,245760]{1,0:T(8,128)(2,1)S(1)}, f32[32,128]{1,0:T(8,128)S(1)}) custom-call(bf16[32,307200]{1,0:T(8,128)(2,1)} %bitcast.19, bf16[32,61440]{1,0:T(8,128)(2,1)S(1)} %get-tuple-element.50.early, bf16[848,128]{1,0:T(8,128)(2,1)S(1)} %get-tuple-element.55.own), custom_call_target="tpu_custom_call" | custom-call | flops 16000000 | bytes 20000000 | tf_op jit(solution)/shard_map/load/pallas_call | solution.py:36
  16.6 0.0 collective-permute-done.2.whole.first_x
  16.6 1.3 %first_rhs.1.begun = f32[32,128]{1,0:T(8,128)S(1)} custom-call(bf16[32,61440]{1,0:T(8,128)(2,1)S(1)} %get-tuple-element.50.early, bf16[32,245760]{1,0:T(8,128)(2,1)S(1)} %get-tuple-element.56.late, f32[32,128]{1,0:T(8,128)S(1)} %get-tuple-element.57.begun, bf16[848,128]{1,0:T(8,128)(2,1)S(1)} %collective-permute-done.2.whole.first_x), custom_call_target="tpu_custom_call" | custom-call | flops 6000000 | bytes 6000000 | tf_op jit(solution)/shard_map/first_rhs/pallas_call | solution.py:36
  17.9 0.0 copy-start
  17.9 0.0 collective-permute-done.3.whole.second_x
  17.9 1.5 %second_rhs.1 = f32[128,128]{1,0:T(8,128)S(1)} custom-call(bf16[32,61440]{1,0:T(8,128)(2,1)S(1)} %get-tuple-element.50.early, bf16[32,245760]{1,0:T(8,128)(2,1)S(1)} %get-tuple-element.56.late, f32[32,128]{1,0:T(8,128)S(1)} %first_rhs.1.begun, bf16[848,128]{1,0:T(8,128)(2,1)S(1)} %collective-permute-done.3.whole.second_x, s32[1,1]{1,0:T(1,128)S(6)} %copy.12.count), custom_call_target="tpu_custom_call" | custom-call | flops 6000000 | bytes 6000000 | tf_op jit(solution)/shard_map/second_rhs/pallas_call | solution.py:36
  19.4 18.6 %all_to_all.10 = f32[128,1,128]{2,1,0:T(1,128)S(1)} all-to-all(f32[128,1,128]{2,1,0:T(1,128)S(1)} %bitcast.15), channel_id=1, replica_groups=mesh['gx'=16,'gy'=8] {'gx','gy'}, dimensions={0} | all-to-all | bytes 131072 | tf_op jit(solution)/shard_map/all_to_all | solution.py:714
  38.1 0.0 copy-done
  38.1 2.0 %first_spread.1 = (f32[32,128]{1,0:T(8,128)S(1)}, bf16[880,128]{1,0:T(8,128)(2,1)S(1)}, f32[80,128]{1,0:T(8,128)S(1)}, f32[80,128]{1,0:T(8,128)S(1)}) custom-call(bf16[32,61440]{1,0:T(8,128)(2,1)S(1)} %get-tuple-element.50.early, bf16[32,245760]{1,0:T(8,128)(2,1)S(1)} %get-tuple-element.56.late, f32[32,4096]{1,0:T(8,128)S(1)} %copy-done, ...), custom_call_target="tpu_custom_call" | custom-call | flops 20000000 | bytes 8000000 | tf_op jit(solution)/shard_map/first_spread/pallas_call | solution.py:36
  40.0 0.5 collective-permute-start.4
  40.5 1.8 %second_spread.1 = (bf16[880,128]{1,0:T(8,128)(2,1)S(1)}, f32[80,128]{1,0:T(8,128)S(1)}, bf16[80,128]{1,0:T(8,128)(2,1)S(1)}, bf16[80,128]{1,0:T(8,128)(2,1)S(1)}) custom-call(bf16[32,61440]{1,0:T(8,128)(2,1)S(1)} %get-tuple-element.50.early, bf16[32,245760]{1,0:T(8,128)(2,1)S(1)} %get-tuple-element.56.late, f32[32,128]{1,0:T(8,128)S(1)} %get-tuple-element.60.weights, ...), custom_call_target="tpu_custom_call" | custom-call | flops 20000000 | bytes 8000000 | tf_op jit(solution)/shard_map/second_spread/pallas_call | solution.py:36
  42.3 1.4 %collective-permute-start.5 = (bf16[880,128]{1,0:T(8,128)(2,1)S(1)}, bf16[880,128]{1,0:T(8,128)(2,1)S(1)}, u32[]{:S(2)}, u32[]{:S(2)}) collective-permute-start(bf16[880,128]{1,0:T(8,128)(2,1)S(1)} %get-tuple-element.66), channel_id=1, source_target_pairs={{0,1},{1,0},{2,3},{3,2},{4,5},{5,4},{6,7},{7,6},{8,16},{9,17},{10,... | collective-permute-start | bytes 675848 | tf_op jit(solution)/shard_map/ppermute | solution.py:691
  43.7 0.1 collective-permute-start.6
  43.8 0.0 copy-start.1
  43.8 3.8 %collective-permute-start.7 = (bf16[80,128]{1,0:T(8,128)(2,1)S(1)}, bf16[80,128]{1,0:T(8,128)(2,1)S(1)}, u32[]{:S(2)}, u32[]{:S(2)}) collective-permute-start(bf16[80,128]{1,0:T(8,128)(2,1)S(1)} %get-tuple-element.68), channel_id=1, source_target_pairs={{0,16},{1,17},{2,18},{3,19},{4,20},{5,21},{6,22},{7,23},{8,24},{9,... | collective-permute-start | bytes 61448 | tf_op jit(solution)/shard_map/ppermute | solution.py:691
  47.6 1.9 %own_spread.1 = (f32[800,128]{1,0:T(8,128)S(1)}, f32[4,640,128]{2,1,0:T(8,128)S(1)}, f32[80,128]{1,0:T(8,128)S(1)}) custom-call(bf16[32,61440]{1,0:T(8,128)(2,1)S(1)} %get-tuple-element.50.early, bf16[32,245760]{1,0:T(8,128)(2,1)S(1)} %get-tuple-element.56.late, f32[32,128]{1,0:T(8,128)S(1)} %get-tuple-element.60.weights, f32[4,640,128]{2,1,0:T(8,128)} %bitcast.21), custom_call_target="tpu_custom_call" | custom-call | flops 20000000 | bytes 7000000 | tf_op jit(solution)/shard_map/own_spread/pallas_call | solution.py:36
  49.5 0.0 collective-permute-done.6.far_second
  49.5 0.0 collective-permute-done.7.far_first
  49.5 0.0 collective-permute-done.4.from_first
  49.5 0.0 collective-permute-done.5.from_second
  49.6 0.3 fold_rows.1
  49.9 1.8 %collective-permute-start.8 = (bf16[208,128]{1,0:T(8,128)(2,1)S(1)}, bf16[208,128]{1,0:T(8,128)(2,1)S(1)}, u32[]{:S(2)}, u32[]{:S(2)}) collective-permute-start(bf16[208,128]{1,0:T(8,128)(2,1)S(1)} %get-tuple-element.73), channel_id=1, source_target_pairs={{0,1},{1,0},{2,3},{3,2},{4,5},{5,4},{6,7},{7,6},{8,9},{9,8},{10,11... | collective-permute-start | bytes 159752 | tf_op jit(solution)/shard_map/ppermute | solution.py:691
  51.7 0.3 collective-permute-start.9
  52.0 0.0 copy-done.1
  52.0 1.2 %faces.1 = (f32[4,640,128]{2,1,0:T(8,128)S(1)}, f32[640,128]{1,0:T(8,128)S(1)}) custom-call(f32[640,128]{1,0:T(8,128)S(1)} %get-tuple-element.78.conduct, f32[640,128]{1,0:T(8,128)S(1)} %get-tuple-element.79.diagonal, f32[4,8]{1,0:T(4,128)S(1)} %copy-done.1, bf16[160,128]{1,0:T(8,128)(2,1)S(1)} %collective-permute-done.from_first.first_y, ...), custom_call_target="tpu_custom_call" | custom-call | flops 4000000 | bytes 2000000 | tf_op jit(solution)/shard_map/faces/pallas_call | solution.py:36
  53.2 0.0 collective-permute-done.8.from_first
  53.2 2.3 %collective-permute-done.9.from_second = bf16[208,128]{1,0:T(8,128)(2,1)S(1)} collective-permute-done((bf16[208,128]{1,0:T(8,128)(2,1)S(1)}, bf16[208,128]{1,0:T(8,128)(2,1)S(1)}, u32[]{:S(2)}, u32[]{:S(2)}) %collective-permute-start.9) | collective-permute-done | bytes 53280 | tf_op jit(solution)/shard_map/ppermute | solution.py:691
  55.5 1.3 %image.1 = (f32[640,128]{1,0:T(8,128)}, f32[640,128]{1,0:T(8,128)S(1)}, f32[128,128]{1,0:T(8,128)S(1)}) custom-call(f32[640,128]{1,0:T(8,128)S(1)} %get-tuple-element.69.field, f32[80,128]{1,0:T(8,128)S(1)} %get-tuple-element.70.rim, f32[200,128]{1,0:T(8,128)S(1)} %get-tuple-element.71.up, f32[200,128]{1,0:T(8,128)S(1)} %get-tuple-element.72.dn, ...), custom_call_target="tpu_custom_call" | custom-call | tf_op jit(solution)/shard_map/image/pallas_call | solution.py:36
  56.8 14.8 %all_to_all.11 = f32[128,1,128]{2,1,0:T(1,128)S(1)} all-to-all(f32[128,1,128]{2,1,0:T(1,128)S(1)} %bitcast.17), channel_id=1, replica_groups=mesh['gx'=16,'gy'=8] {'gx','gy'}, dimensions={0} | all-to-all | bytes 131072 | tf_op jit(solution)/shard_map/all_to_all | solution.py:714
  71.6 1.2 %next.1 = (f32[640,128]{1,0:T(8,128)}, f32[5]{0:T(128)}) custom-call(f32[128,128]{1,0:T(8,128)S(1)} %bitcast.16, f32[640,128]{1,0:T(8,128)S(1)} %get-tuple-element.86.image, f32[4,640,128]{2,1,0:T(8,128)S(1)} %get-tuple-element.75.basis), custom_call_target="tpu_custom_call" | custom-call | tf_op jit(solution)/shard_map/next/pallas_call | solution.py:36
Async XLA Ops:
  2.1 5.0 %collective-permute-start = (bf16[160,128]{1,0:T(8,128)(2,1)S(1)}, bf16[160,128]{1,0:T(8,128)(2,1)S(1)}, u32[]{:S(2)}, u32[]{:S(2)}) collective-permute-start(bf16[160,128]{1,0:T(8,128)(2,1)S(1)} %get-tuple-element.53), channel_id=1, source_target_pairs={{0,1},{1,0},{2,3},{3,2},{4,5},{5,4},{6,7},{7,6},{8,9},{9,8},{10,11... | collective-permute-start | bytes 122888 | tf_op jit(solution)/shard_map/ppermute | solution.py:691
  3.6 3.7 %collective-permute-start.1 = (bf16[160,128]{1,0:T(8,128)(2,1)S(1)}, bf16[160,128]{1,0:T(8,128)(2,1)S(1)}, u32[]{:S(2)}, u32[]{:S(2)}) collective-permute-start(bf16[160,128]{1,0:T(8,128)(2,1)S(1)} %get-tuple-element.54), channel_id=1, source_target_pairs={{0,8},{1,2},{2,1},{3,4},{4,3},{5,6},{6,5},{7,15},{8,0},{9,10},{10,... | collective-permute-start | bytes 122888 | tf_op jit(solution)/shard_map/ppermute | solution.py:691
  7.4 9.2 %collective-permute-start.2 = (bf16[848,128]{1,0:T(8,128)(2,1)S(1)}, bf16[848,128]{1,0:T(8,128)(2,1)S(1)}, u32[]{:S(2)}, u32[]{:S(2)}) collective-permute-start(bf16[848,128]{1,0:T(8,128)(2,1)S(1)} %get-tuple-element.55.own), channel_id=1, source_target_pairs={{0,8},{1,9},{2,10},{3,11},{4,12},{5,13},{6,14},{7,15},{8,0},{9,1},... | collective-permute-start | bytes 651272 | tf_op jit(solution)/shard_map/ppermute | solution.py:691
  9.2 8.7 %collective-permute-start.3 = (bf16[848,128]{1,0:T(8,128)(2,1)S(1)}, bf16[848,128]{1,0:T(8,128)(2,1)S(1)}, u32[]{:S(2)}, u32[]{:S(2)}) collective-permute-start(bf16[848,128]{1,0:T(8,128)(2,1)S(1)} %get-tuple-element.58), channel_id=1, source_target_pairs={{0,1},{1,0},{2,3},{3,2},{4,5},{5,4},{6,7},{7,6},{8,16},{9,17},{10,... | collective-permute-start | bytes 651272 | tf_op jit(solution)/shard_map/ppermute | solution.py:691
  17.9 20.1 %copy-start = (f32[32,4096]{1,0:T(8,128)S(1)}, f32[32,4096]{1,0:T(8,128)}, u32[]{:S(2)}) copy-start(f32[32,4096]{1,0:T(8,128)} %inverse.1) | copy-start | bytes 1572868
  40.0 9.5 %collective-permute-start.4 = (bf16[880,128]{1,0:T(8,128)(2,1)S(1)}, bf16[880,128]{1,0:T(8,128)(2,1)S(1)}, u32[]{:S(2)}, u32[]{:S(2)}) collective-permute-start(bf16[880,128]{1,0:T(8,128)(2,1)S(1)} %get-tuple-element.65), channel_id=1, source_target_pairs={{0,8},{1,9},{2,10},{3,11},{4,12},{5,13},{6,14},{7,15},{8,0},{9,1},... | collective-permute-start | bytes 675848 | tf_op jit(solution)/shard_map/ppermute | solution.py:691
  42.3 7.2 %collective-permute-start.5 = (bf16[880,128]{1,0:T(8,128)(2,1)S(1)}, bf16[880,128]{1,0:T(8,128)(2,1)S(1)}, u32[]{:S(2)}, u32[]{:S(2)}) collective-permute-start(bf16[880,128]{1,0:T(8,128)(2,1)S(1)} %get-tuple-element.66), channel_id=1, source_target_pairs={{0,1},{1,0},{2,3},{3,2},{4,5},{5,4},{6,7},{7,6},{8,16},{9,17},{10,... | collective-permute-start | bytes 675848 | tf_op jit(solution)/shard_map/ppermute | solution.py:691
  43.7 5.8 %collective-permute-start.6 = (bf16[80,128]{1,0:T(8,128)(2,1)S(1)}, bf16[80,128]{1,0:T(8,128)(2,1)S(1)}, u32[]{:S(2)}, u32[]{:S(2)}) collective-permute-start(bf16[80,128]{1,0:T(8,128)(2,1)S(1)} %get-tuple-element.67), channel_id=1, source_target_pairs={{0,1},{1,0},{2,3},{3,2},{4,5},{5,4},{6,7},{7,6},{8,9},{9,8},{10,11... | collective-permute-start | bytes 61448 | tf_op jit(solution)/shard_map/ppermute | solution.py:691
  43.8 8.2 %copy-start.1 = (f32[4,8]{1,0:T(4,128)S(1)}, f32[4,8]{1,0:T(4,128)}, u32[]{:S(2)}) copy-start(f32[4,8]{1,0:T(4,128)} %table.1) | copy-start | bytes 388
  43.8 5.7 %collective-permute-start.7 = (bf16[80,128]{1,0:T(8,128)(2,1)S(1)}, bf16[80,128]{1,0:T(8,128)(2,1)S(1)}, u32[]{:S(2)}, u32[]{:S(2)}) collective-permute-start(bf16[80,128]{1,0:T(8,128)(2,1)S(1)} %get-tuple-element.68), channel_id=1, source_target_pairs={{0,16},{1,17},{2,18},{3,19},{4,20},{5,21},{6,22},{7,23},{8,24},{9,... | collective-permute-start | bytes 61448 | tf_op jit(solution)/shard_map/ppermute | solution.py:691
  49.9 3.3 %collective-permute-start.8 = (bf16[208,128]{1,0:T(8,128)(2,1)S(1)}, bf16[208,128]{1,0:T(8,128)(2,1)S(1)}, u32[]{:S(2)}, u32[]{:S(2)}) collective-permute-start(bf16[208,128]{1,0:T(8,128)(2,1)S(1)} %get-tuple-element.73), channel_id=1, source_target_pairs={{0,1},{1,0},{2,3},{3,2},{4,5},{5,4},{6,7},{7,6},{8,9},{9,8},{10,11... | collective-permute-start | bytes 159752 | tf_op jit(solution)/shard_map/ppermute | solution.py:691
  51.7 3.8 %collective-permute-start.9 = (bf16[208,128]{1,0:T(8,128)(2,1)S(1)}, bf16[208,128]{1,0:T(8,128)(2,1)S(1)}, u32[]{:S(2)}, u32[]{:S(2)}) collective-permute-start(bf16[208,128]{1,0:T(8,128)(2,1)S(1)} %get-tuple-element.74), channel_id=1, source_target_pairs={{0,8},{1,2},{2,1},{3,4},{4,3},{5,6},{6,5},{7,15},{8,0},{9,10},{10,... | collective-permute-start | bytes 159752 | tf_op jit(solution)/shard_map/ppermute | solution.py:691

commit v5 on v4

--- a/solution.py
+++ b/solution.py
@@ -82,28 +82,31 @@
     ]
     for copy in copies:
         copy.start()
-    for copy in copies:
-        copy.wait()
-    code[...] = (soil[...] + 8 * frozen[...]).astype(F32)
     at = lanes(RUNS)
     to_up = jnp.zeros((RUNS, COLS), F32)
     to_dn = to_up
     flats = [jnp.zeros((RUNS, COLS), F32) for _ in range(5)]
+    copies[0].wait()
     for q in range(4):
         cut = 32 * q + 16
         turned = turn(basis[pl.ds(q, RUNS, stride=4), :], cut)
-        kind = code[pl.ds(q, RUNS, stride=4), :]
-        low = (at >= cut - 16) & (at < cut)
-        high = (at >= cut) & (at < cut + 16)
-        to_up = jnp.where(low, turned, jnp.where(at == cut, turn(kind, cut + 1), to_up))
-        to_dn = jnp.where(high, turned, jnp.where(at == cut - 1, turn(kind, cut - 1), to_dn))
+        to_up = jnp.where((at >= cut - 16) & (at < cut), turned, to_up)
+        to_dn = jnp.where((at >= cut) & (at < cut + 16), turned, to_dn)
         flats[q] = jnp.where(at >= cut, turned, flats[q])
         flats[q + 1] = jnp.where(at < cut, turned, flats[q + 1])
+    for j in range(5):
+        flat[j * RUNS : (j + 1) * RUNS, :] = flats[j].astype(BF16)
+    for copy in copies[1:]:
+        copy.wait()
+    code[...] = (soil[...] + 8 * frozen[...]).astype(F32)
+    for q in range(4):
+        cut = 32 * q + 16
+        kind = code[pl.ds(q, RUNS, stride=4), :]
+        to_up = jnp.where(at == cut, turn(kind, cut + 1), to_up)
+        to_dn = jnp.where(at == cut - 1, turn(kind, cut - 1), to_dn)
     even = lax.axis_index("gy") % 2 == 0
     first[...] = jnp.where(even, to_up, to_dn).astype(BF16)
     second[...] = jnp.where(even, to_dn, to_up).astype(BF16)
-    for j in range(5):
-        flat[j * RUNS : (j + 1) * RUNS, :] = flats[j].astype(BF16)
     spare = jnp.zeros((PAD - FLAT - LAYERS, COLS), F32)
     for index, row in enumerate((0, ROWS - 1)):
         line = jnp.concatenate([code[pl.ds(row, LAYERS, stride=ROWS), :], spare], axis=0)
@@ -479,29 +482,51 @@
 
     lax.fori_loop(0, CELLS // 160, body, 0)
     zero = jnp.zeros((ROWS, COLS), F32)
-    below = zero
-    last_ratio = zero
-    last_value = zero
-    for level in range(LAYERS):
-        cut = slice(level * ROWS, (level + 1) * ROWS)
-        own = conduct[cut, :]
-        over = zero
-        if level < LAYERS - 1:
-            over = WEIGHT_V * harmonic(own, conduct[(level + 1) * ROWS : (level + 2) * ROWS, :])
-        above[cut, :] = over
-        sides = diagonal[cut, :] + below + over
-        diagonal[cut, :] = sides
-        denom = sides + 4.0 * WEIGHT_H * own + below * last_ratio
-        inverse = 1.0 / denom
-        last_ratio = -over * inverse
-        last_value = (basis[cut, :] + below * last_value) * inverse
-        ratio[cut, :] = last_ratio
-        value[cut, :] = last_value
-        below = over
-    for level in range(LAYERS - 2, -1, -1):
-        cut = slice(level * ROWS, (level + 1) * ROWS)
-        last_value = value[cut, :] - ratio[cut, :] * last_value
-        value[cut, :] = last_value
+    half = LAYERS // 2
+
+    def piece(level):
+        return slice(level * ROWS, (level + 1) * ROWS)
+
+    def face(level):
+        return WEIGHT_V * harmonic(conduct[piece(level), :], conduct[piece(level + 1), :])
+
+    def eliminate(level, below, over, outer, inner, last_ratio, last_value):
+        cut = piece(level)
+        middle = diagonal[cut, :] + below + over
+        diagonal[cut, :] = middle
+        inverse = 1.0 / (middle + 4.0 * WEIGHT_H * conduct[cut, :] + outer * last_ratio)
+        next_ratio = -inner * inverse
+        next_value = (basis[cut, :] + outer * last_value) * inverse
+        ratio[cut, :] = next_ratio
+        value[cut, :] = next_value
+        return next_ratio, next_value
+
+    low_ratio, low_value, below = zero, zero, zero
+    high_ratio, high_value, over = zero, zero, zero
+    above[piece(LAYERS - 1), :] = zero
+    for step in range(half):
+        low, high = step, LAYERS - 1 - step
+        low_over, high_below = face(low), face(high - 1)
+        above[piece(low), :] = low_over
+        if step < half - 1:
+            above[piece(high - 1), :] = high_below
+        low_ratio, low_value = eliminate(
+            low, below, low_over, below, low_over, low_ratio, low_value
+        )
+        high_ratio, high_value = eliminate(
+            high, high_below, over, over, high_below, high_ratio, high_value
+        )
+        below, over = low_over, high_below
+    low_value = (low_value - low_ratio * high_value) / (1.0 - low_ratio * high_ratio)
+    high_value = high_value - high_ratio * low_value
+    value[piece(half - 1), :] = low_value
+    value[piece(half), :] = high_value
+    for step in range(1, half):
+        low, high = piece(half - 1 - step), piece(half + step)
+        low_value = value[low, :] - ratio[low, :] * low_value
+        high_value = value[high, :] - ratio[high, :] * high_value
+        value[low, :] = low_value
+        value[high, :] = high_value
     for q in range(4):
         local[q * RUNS : (q + 1) * RUNS, :] = turn(value[pl.ds(q, RUNS, stride=4), :], 32 * q + 16)
 

time: 73 us -> 73 us (level)
  no operation moved by 1% of the time
where the time goes in v5:
time: 73 us; the launch traced here: 72.8 us
  blocking collectives  33.4 us (46%)
  Pallas kernels  22.2 us (30%)
  starting transfers between devices  13.2 us (18%)
  waiting for transfers between devices  2.51 us (3%)
  between operations  1.43 us (2%)
    all_to_all x2, blocking collectives, exchange(): out = lax.all_to_all(lines.reshape(size, 1, COLS), ('gx', 'gy'), 0, 0)  33.4 us
    pallas_call x13, Pallas kernels, call(): pl.pallas_call(kernel, out_shape=outs, in_specs=specs, out_specs=out_spec...  22.2 us
    ppermute x10, starting transfers between devices, swap(): return lax.ppermute(values, ('gx', 'gy'), pairs)  13.2 us
    ppermute x10, waiting for transfers between devices, swap(): return lax.ppermute(values, ('gx', 'gy'), pairs)  2.51 us
  transfers between devices with their start and end apart: 10, of which 2 were waited for; matrix products, arithmetic and copies ran while one was open for 0% of the time, Pallas kernels for 20%

profile of v5, /device:TPU:1, one launch (start us, length us, event | category | flops | bytes accessed | tf_op | source)
XLA Modules:
  0.0 72.8 jit_solution(4484787312631110119)
XLA Ops:
  0.6 1.4 %pack.1 = (bf16[160,128]{1,0:T(8,128)(2,1)S(1)}, bf16[160,128]{1,0:T(8,128)(2,1)S(1)}, bf16[800,128]{1,0:T(8,128)(2,1)S(1)}, f32[2,48,128]{2,1,0:T(8,128)S(1)}, ...) custom-call(f32[4,640,128]{2,1,0:T(8,128)} %bitcast.20, s32[640,128]{1,0:T(8,128)} %bitcast.22, s32[640,128]{1,0:T(8,128)} %bitcast.23), custom_call_target="tpu_custom_call" | custom-call | tf_op jit(solution)/shard_map/pack/pallas_call | solution.py:36
  2.1 1.5 %collective-permute-start = (bf16[160,128]{1,0:T(8,128)(2,1)S(1)}, bf16[160,128]{1,0:T(8,128)(2,1)S(1)}, u32[]{:S(2)}, u32[]{:S(2)}) collective-permute-start(bf16[160,128]{1,0:T(8,128)(2,1)S(1)} %get-tuple-element.53), channel_id=1, source_target_pairs={{0,1},{1,0},{2,3},{3,2},{4,5},{5,4},{6,7},{7,6},{8,9},{9,8},{10,11... | collective-permute-start | bytes 122888 | tf_op jit(solution)/shard_map/ppermute | solution.py:716
  3.6 1.4 %collective-permute-start.1 = (bf16[160,128]{1,0:T(8,128)(2,1)S(1)}, bf16[160,128]{1,0:T(8,128)(2,1)S(1)}, u32[]{:S(2)}, u32[]{:S(2)}) collective-permute-start(bf16[160,128]{1,0:T(8,128)(2,1)S(1)} %get-tuple-element.54), channel_id=1, source_target_pairs={{0,8},{1,2},{2,1},{3,4},{4,3},{5,6},{6,5},{7,15},{8,0},{9,10},{10,... | collective-permute-start | bytes 122888 | tf_op jit(solution)/shard_map/ppermute | solution.py:716
  4.9 2.1 %early.1 = (bf16[32,61440]{1,0:T(8,128)(2,1)S(1)}, f32[640,128]{1,0:T(8,128)S(1)}, f32[640,128]{1,0:T(8,128)S(1)}, f32[640,128]{1,0:T(8,128)S(1)}, f32[640,128]{1,0:T(8,128)S(1)}) custom-call(bf16[32,307200]{1,0:T(8,128)(2,1)} %bitcast.18, f32[4,8]{1,0:T(4,128)} %table.1, f32[640,128]{1,0:T(8,128)S(1)} %get-tuple-element.46.basis, ...), custom_call_target="tpu_custom_call" | custom-call | bytes 10000000 | tf_op jit(solution)/shard_map/early/pallas_call | solution.py:36
  7.1 0.0 collective-permute-done.from_first.first_y
  7.1 0.2 collective-permute-done.1.from_second.second_y
  7.3 0.1 flat.1
  7.3 1.8 %collective-permute-start.2 = (bf16[848,128]{1,0:T(8,128)(2,1)S(1)}, bf16[848,128]{1,0:T(8,128)(2,1)S(1)}, u32[]{:S(2)}, u32[]{:S(2)}) collective-permute-start(bf16[848,128]{1,0:T(8,128)(2,1)S(1)} %get-tuple-element.55.own), channel_id=1, source_target_pairs={{0,8},{1,9},{2,10},{3,11},{4,12},{5,13},{6,14},{7,15},{8,0},{9,1},... | collective-permute-start | bytes 651272 | tf_op jit(solution)/shard_map/ppermute | solution.py:716
  9.1 0.7 collective-permute-start.3
  10.5 6.0 %load.1 = (bf16[32,245760]{1,0:T(8,128)(2,1)S(1)}, f32[32,128]{1,0:T(8,128)S(1)}) custom-call(bf16[32,307200]{1,0:T(8,128)(2,1)} %bitcast.19, bf16[32,61440]{1,0:T(8,128)(2,1)S(1)} %get-tuple-element.50.early, bf16[848,128]{1,0:T(8,128)(2,1)S(1)} %get-tuple-element.55.own), custom_call_target="tpu_custom_call" | custom-call | flops 16000000 | bytes 20000000 | tf_op jit(solution)/shard_map/load/pallas_call | solution.py:36
  16.5 0.0 collective-permute-done.2.whole.first_x
  16.5 1.3 %first_rhs.1.begun = f32[32,128]{1,0:T(8,128)S(1)} custom-call(bf16[32,61440]{1,0:T(8,128)(2,1)S(1)} %get-tuple-element.50.early, bf16[32,245760]{1,0:T(8,128)(2,1)S(1)} %get-tuple-element.56.late, f32[32,128]{1,0:T(8,128)S(1)} %get-tuple-element.57.begun, bf16[848,128]{1,0:T(8,128)(2,1)S(1)} %collective-permute-done.2.whole.first_x), custom_call_target="tpu_custom_call" | custom-call | flops 6000000 | bytes 6000000 | tf_op jit(solution)/shard_map/first_rhs/pallas_call | solution.py:36
  17.9 0.0 copy-start
  17.9 0.0 collective-permute-done.3.whole.second_x
  17.9 1.5 %second_rhs.1 = f32[128,128]{1,0:T(8,128)S(1)} custom-call(bf16[32,61440]{1,0:T(8,128)(2,1)S(1)} %get-tuple-element.50.early, bf16[32,245760]{1,0:T(8,128)(2,1)S(1)} %get-tuple-element.56.late, f32[32,128]{1,0:T(8,128)S(1)} %first_rhs.1.begun, bf16[848,128]{1,0:T(8,128)(2,1)S(1)} %collective-permute-done.3.whole.second_x, s32[1,1]{1,0:T(1,128)S(6)} %copy.12.count), custom_call_target="tpu_custom_call" | custom-call | flops 6000000 | bytes 6000000 | tf_op jit(solution)/shard_map/second_rhs/pallas_call | solution.py:36
  19.4 18.6 %all_to_all.10 = f32[128,1,128]{2,1,0:T(1,128)S(1)} all-to-all(f32[128,1,128]{2,1,0:T(1,128)S(1)} %bitcast.15), channel_id=1, replica_groups=mesh['gx'=16,'gy'=8] {'gx','gy'}, dimensions={0} | all-to-all | bytes 131072 | tf_op jit(solution)/shard_map/all_to_all | solution.py:739
  38.0 0.0 copy-done
  38.0 2.0 %first_spread.1 = (f32[32,128]{1,0:T(8,128)S(1)}, bf16[880,128]{1,0:T(8,128)(2,1)S(1)}, f32[80,128]{1,0:T(8,128)S(1)}, f32[80,128]{1,0:T(8,128)S(1)}) custom-call(bf16[32,61440]{1,0:T(8,128)(2,1)S(1)} %get-tuple-element.50.early, bf16[32,245760]{1,0:T(8,128)(2,1)S(1)} %get-tuple-element.56.late, f32[32,4096]{1,0:T(8,128)S(1)} %copy-done, ...), custom_call_target="tpu_custom_call" | custom-call | flops 20000000 | bytes 8000000 | tf_op jit(solution)/shard_map/first_spread/pallas_call | solution.py:36
  40.0 0.5 collective-permute-start.4
  40.5 1.8 %second_spread.1 = (bf16[880,128]{1,0:T(8,128)(2,1)S(1)}, f32[80,128]{1,0:T(8,128)S(1)}, bf16[80,128]{1,0:T(8,128)(2,1)S(1)}, bf16[80,128]{1,0:T(8,128)(2,1)S(1)}) custom-call(bf16[32,61440]{1,0:T(8,128)(2,1)S(1)} %get-tuple-element.50.early, bf16[32,245760]{1,0:T(8,128)(2,1)S(1)} %get-tuple-element.56.late, f32[32,128]{1,0:T(8,128)S(1)} %get-tuple-element.60.weights, ...), custom_call_target="tpu_custom_call" | custom-call | flops 20000000 | bytes 8000000 | tf_op jit(solution)/shard_map/second_spread/pallas_call | solution.py:36
  42.3 1.4 %collective-permute-start.5 = (bf16[880,128]{1,0:T(8,128)(2,1)S(1)}, bf16[880,128]{1,0:T(8,128)(2,1)S(1)}, u32[]{:S(2)}, u32[]{:S(2)}) collective-permute-start(bf16[880,128]{1,0:T(8,128)(2,1)S(1)} %get-tuple-element.66), channel_id=1, source_target_pairs={{0,1},{1,0},{2,3},{3,2},{4,5},{5,4},{6,7},{7,6},{8,16},{9,17},{10,... | collective-permute-start | bytes 675848 | tf_op jit(solution)/shard_map/ppermute | solution.py:716
  43.7 0.1 collective-permute-start.6
  43.8 0.0 copy-start.1
  43.8 3.8 %collective-permute-start.7 = (bf16[80,128]{1,0:T(8,128)(2,1)S(1)}, bf16[80,128]{1,0:T(8,128)(2,1)S(1)}, u32[]{:S(2)}, u32[]{:S(2)}) collective-permute-start(bf16[80,128]{1,0:T(8,128)(2,1)S(1)} %get-tuple-element.68), channel_id=1, source_target_pairs={{0,16},{1,17},{2,18},{3,19},{4,20},{5,21},{6,22},{7,23},{8,24},{9,... | collective-permute-start | bytes 61448 | tf_op jit(solution)/shard_map/ppermute | solution.py:716
  47.6 1.9 %own_spread.1 = (f32[800,128]{1,0:T(8,128)S(1)}, f32[4,640,128]{2,1,0:T(8,128)S(1)}, f32[80,128]{1,0:T(8,128)S(1)}) custom-call(bf16[32,61440]{1,0:T(8,128)(2,1)S(1)} %get-tuple-element.50.early, bf16[32,245760]{1,0:T(8,128)(2,1)S(1)} %get-tuple-element.56.late, f32[32,128]{1,0:T(8,128)S(1)} %get-tuple-element.60.weights, f32[4,640,128]{2,1,0:T(8,128)} %bitcast.21), custom_call_target="tpu_custom_call" | custom-call | flops 20000000 | bytes 7000000 | tf_op jit(solution)/shard_map/own_spread/pallas_call | solution.py:36
  49.5 0.0 collective-permute-done.6.far_second
  49.5 0.0 collective-permute-done.7.far_first
  49.5 0.0 collective-permute-done.4.from_first
  49.5 0.0 collective-permute-done.5.from_second
  49.5 0.3 fold_rows.1
  49.8 1.8 %collective-permute-start.8 = (bf16[208,128]{1,0:T(8,128)(2,1)S(1)}, bf16[208,128]{1,0:T(8,128)(2,1)S(1)}, u32[]{:S(2)}, u32[]{:S(2)}) collective-permute-start(bf16[208,128]{1,0:T(8,128)(2,1)S(1)} %get-tuple-element.73), channel_id=1, source_target_pairs={{0,1},{1,0},{2,3},{3,2},{4,5},{5,4},{6,7},{7,6},{8,9},{9,8},{10,11... | collective-permute-start | bytes 159752 | tf_op jit(solution)/shard_map/ppermute | solution.py:716
  51.6 0.3 collective-permute-start.9
  51.9 0.0 copy-done.1
  51.9 1.2 %faces.1 = (f32[4,640,128]{2,1,0:T(8,128)S(1)}, f32[640,128]{1,0:T(8,128)S(1)}) custom-call(f32[640,128]{1,0:T(8,128)S(1)} %get-tuple-element.78.conduct, f32[640,128]{1,0:T(8,128)S(1)} %get-tuple-element.79.diagonal, f32[4,8]{1,0:T(4,128)S(1)} %copy-done.1, bf16[160,128]{1,0:T(8,128)(2,1)S(1)} %collective-permute-done.from_first.first_y, ...), custom_call_target="tpu_custom_call" | custom-call | flops 4000000 | bytes 2000000 | tf_op jit(solution)/shard_map/faces/pallas_call | solution.py:36
  53.1 0.0 collective-permute-done.8.from_first
  53.2 2.3 %collective-permute-done.9.from_second = bf16[208,128]{1,0:T(8,128)(2,1)S(1)} collective-permute-done((bf16[208,128]{1,0:T(8,128)(2,1)S(1)}, bf16[208,128]{1,0:T(8,128)(2,1)S(1)}, u32[]{:S(2)}, u32[]{:S(2)}) %collective-permute-start.9) | collective-permute-done | bytes 53280 | tf_op jit(solution)/shard_map/ppermute | solution.py:716
  55.5 1.3 %image.1 = (f32[640,128]{1,0:T(8,128)}, f32[640,128]{1,0:T(8,128)S(1)}, f32[128,128]{1,0:T(8,128)S(1)}) custom-call(f32[640,128]{1,0:T(8,128)S(1)} %get-tuple-element.69.field, f32[80,128]{1,0:T(8,128)S(1)} %get-tuple-element.70.rim, f32[200,128]{1,0:T(8,128)S(1)} %get-tuple-element.71.up, f32[200,128]{1,0:T(8,128)S(1)} %get-tuple-element.72.dn, ...), custom_call_target="tpu_custom_call" | custom-call | tf_op jit(solution)/shard_map/image/pallas_call | solution.py:36
  56.8 14.8 %all_to_all.11 = f32[128,1,128]{2,1,0:T(1,128)S(1)} all-to-all(f32[128,1,128]{2,1,0:T(1,128)S(1)} %bitcast.17), channel_id=1, replica_groups=mesh['gx'=16,'gy'=8] {'gx','gy'}, dimensions={0} | all-to-all | bytes 131072 | tf_op jit(solution)/shard_map/all_to_all | solution.py:739
  71.6 1.2 %next.1 = (f32[640,128]{1,0:T(8,128)}, f32[5]{0:T(128)}) custom-call(f32[128,128]{1,0:T(8,128)S(1)} %bitcast.16, f32[640,128]{1,0:T(8,128)S(1)} %get-tuple-element.86.image, f32[4,640,128]{2,1,0:T(8,128)S(1)} %get-tuple-element.75.basis), custom_call_target="tpu_custom_call" | custom-call | tf_op jit(solution)/shard_map/next/pallas_call | solution.py:36
Async XLA Ops:
  2.1 5.0 %collective-permute-start = (bf16[160,128]{1,0:T(8,128)(2,1)S(1)}, bf16[160,128]{1,0:T(8,128)(2,1)S(1)}, u32[]{:S(2)}, u32[]{:S(2)}) collective-permute-start(bf16[160,128]{1,0:T(8,128)(2,1)S(1)} %get-tuple-element.53), channel_id=1, source_target_pairs={{0,1},{1,0},{2,3},{3,2},{4,5},{5,4},{6,7},{7,6},{8,9},{9,8},{10,11... | collective-permute-start | bytes 122888 | tf_op jit(solution)/shard_map/ppermute | solution.py:716
  3.6 3.7 %collective-permute-start.1 = (bf16[160,128]{1,0:T(8,128)(2,1)S(1)}, bf16[160,128]{1,0:T(8,128)(2,1)S(1)}, u32[]{:S(2)}, u32[]{:S(2)}) collective-permute-start(bf16[160,128]{1,0:T(8,128)(2,1)S(1)} %get-tuple-element.54), channel_id=1, source_target_pairs={{0,8},{1,2},{2,1},{3,4},{4,3},{5,6},{6,5},{7,15},{8,0},{9,10},{10,... | collective-permute-start | bytes 122888 | tf_op jit(solution)/shard_map/ppermute | solution.py:716
  7.3 9.2 %collective-permute-start.2 = (bf16[848,128]{1,0:T(8,128)(2,1)S(1)}, bf16[848,128]{1,0:T(8,128)(2,1)S(1)}, u32[]{:S(2)}, u32[]{:S(2)}) collective-permute-start(bf16[848,128]{1,0:T(8,128)(2,1)S(1)} %get-tuple-element.55.own), channel_id=1, source_target_pairs={{0,8},{1,9},{2,10},{3,11},{4,12},{5,13},{6,14},{7,15},{8,0},{9,1},... | collective-permute-start | bytes 651272 | tf_op jit(solution)/shard_map/ppermute | solution.py:716
  9.1 8.7 %collective-permute-start.3 = (bf16[848,128]{1,0:T(8,128)(2,1)S(1)}, bf16[848,128]{1,0:T(8,128)(2,1)S(1)}, u32[]{:S(2)}, u32[]{:S(2)}) collective-permute-start(bf16[848,128]{1,0:T(8,128)(2,1)S(1)} %get-tuple-element.58), channel_id=1, source_target_pairs={{0,1},{1,0},{2,3},{3,2},{4,5},{5,4},{6,7},{7,6},{8,16},{9,17},{10,... | collective-permute-start | bytes 651272 | tf_op jit(solution)/shard_map/ppermute | solution.py:716
  17.9 20.1 %copy-start = (f32[32,4096]{1,0:T(8,128)S(1)}, f32[32,4096]{1,0:T(8,128)}, u32[]{:S(2)}) copy-start(f32[32,4096]{1,0:T(8,128)} %inverse.1) | copy-start | bytes 1572868
  40.0 9.5 %collective-permute-start.4 = (bf16[880,128]{1,0:T(8,128)(2,1)S(1)}, bf16[880,128]{1,0:T(8,128)(2,1)S(1)}, u32[]{:S(2)}, u32[]{:S(2)}) collective-permute-start(bf16[880,128]{1,0:T(8,128)(2,1)S(1)} %get-tuple-element.65), channel_id=1, source_target_pairs={{0,8},{1,9},{2,10},{3,11},{4,12},{5,13},{6,14},{7,15},{8,0},{9,1},... | collective-permute-start | bytes 675848 | tf_op jit(solution)/shard_map/ppermute | solution.py:716
  42.3 7.2 %collective-permute-start.5 = (bf16[880,128]{1,0:T(8,128)(2,1)S(1)}, bf16[880,128]{1,0:T(8,128)(2,1)S(1)}, u32[]{:S(2)}, u32[]{:S(2)}) collective-permute-start(bf16[880,128]{1,0:T(8,128)(2,1)S(1)} %get-tuple-element.66), channel_id=1, source_target_pairs={{0,1},{1,0},{2,3},{3,2},{4,5},{5,4},{6,7},{7,6},{8,16},{9,17},{10,... | collective-permute-start | bytes 675848 | tf_op jit(solution)/shard_map/ppermute | solution.py:716
  43.7 5.8 %collective-permute-start.6 = (bf16[80,128]{1,0:T(8,128)(2,1)S(1)}, bf16[80,128]{1,0:T(8,128)(2,1)S(1)}, u32[]{:S(2)}, u32[]{:S(2)}) collective-permute-start(bf16[80,128]{1,0:T(8,128)(2,1)S(1)} %get-tuple-element.67), channel_id=1, source_target_pairs={{0,1},{1,0},{2,3},{3,2},{4,5},{5,4},{6,7},{7,6},{8,9},{9,8},{10,11... | collective-permute-start | bytes 61448 | tf_op jit(solution)/shard_map/ppermute | solution.py:716
  43.8 8.2 %copy-start.1 = (f32[4,8]{1,0:T(4,128)S(1)}, f32[4,8]{1,0:T(4,128)}, u32[]{:S(2)}) copy-start(f32[4,8]{1,0:T(4,128)} %table.1) | copy-start | bytes 388
  43.8 5.7 %collective-permute-start.7 = (bf16[80,128]{1,0:T(8,128)(2,1)S(1)}, bf16[80,128]{1,0:T(8,128)(2,1)S(1)}, u32[]{:S(2)}, u32[]{:S(2)}) collective-permute-start(bf16[80,128]{1,0:T(8,128)(2,1)S(1)} %get-tuple-element.68), channel_id=1, source_target_pairs={{0,16},{1,17},{2,18},{3,19},{4,20},{5,21},{6,22},{7,23},{8,24},{9,... | collective-permute-start | bytes 61448 | tf_op jit(solution)/shard_map/ppermute | solution.py:716
  49.8 3.3 %collective-permute-start.8 = (bf16[208,128]{1,0:T(8,128)(2,1)S(1)}, bf16[208,128]{1,0:T(8,128)(2,1)S(1)}, u32[]{:S(2)}, u32[]{:S(2)}) collective-permute-start(bf16[208,128]{1,0:T(8,128)(2,1)S(1)} %get-tuple-element.73), channel_id=1, source_target_pairs={{0,1},{1,0},{2,3},{3,2},{4,5},{5,4},{6,7},{7,6},{8,9},{9,8},{10,11... | collective-permute-start | bytes 159752 | tf_op jit(solution)/shard_map/ppermute | solution.py:716
  51.6 3.8 %collective-permute-start.9 = (bf16[208,128]{1,0:T(8,128)(2,1)S(1)}, bf16[208,128]{1,0:T(8,128)(2,1)S(1)}, u32[]{:S(2)}, u32[]{:S(2)}) collective-permute-start(bf16[208,128]{1,0:T(8,128)(2,1)S(1)} %get-tuple-element.74), channel_id=1, source_target_pairs={{0,8},{1,2},{2,1},{3,4},{4,3},{5,6},{6,5},{7,15},{8,0},{9,10},{10,... | collective-permute-start | bytes 159752 | tf_op jit(solution)/shard_map/ppermute | solution.py:716
